TPU v7x, 512 devices: a whole 4x4x16 slice. The times are simulated.
512 devices in a mesh: rows: 8 (over x, y_lo), cols: 64 (over y_hi, z, core).
Axes of the slice: x: 4, y: 4 (y_hi: 2, y_lo: 2; y = y_hi * 2 + y_lo), z: 16, core: 2. Of those that a mesh axis runs over, the one named last changes fastest.
Arguments:
- grad_out: bfloat16 [1024, 6144], P('cols', 'rows'), may hold values from -6 to 6
- ctx_code: bfloat16 [1024, 6144], P('rows', 'cols'), may hold values from -3 to 3
- ctx_scale: float32 [1024, 192], P('rows', 'cols'), may hold values from 0.5 to 2
- stream_code: bfloat16 [1024, 6144], P('cols', 'rows'), may hold values from -3 to 3
- stream_scale: float32 [1024, 192], P('cols', 'rows'), may hold values from 0.5 to 2
- hidden_code: bfloat16 [1024, 24576], P('rows', 'cols'), may hold values from -3 to 3
- hidden_scale: float32 [1024, 768], P('rows', 'cols'), may hold values from 0.5 to 2
- out_weight: bfloat16 [6144, 6144], P('cols', 'rows'), may hold values from -0.078125 to 0.078125
- up_weight: bfloat16 [6144, 24576], P('rows', 'cols'), may hold values from -0.078125 to 0.078125
- down_weight: bfloat16 [24576, 6144], P('cols', 'rows'), may hold values from -0.0390625 to 0.0390625
Outputs:
- grad_ctx: bfloat16 [1024, 6144], P('rows', 'cols')
- grad_out_weight: float32 [6144, 6144], P('cols', 'rows')
- grad_up_weight: float32 [6144, 24576], P('rows', 'cols')
- grad_down_weight: float32 [24576, 6144], P('cols', 'rows')
All inputs are finite; a program needn't handle non-finite values.
Results may differ from a plain program's by a relative error of at most 0.034.
Values may be sent and summed in bfloat16 or wider, within the bound.
No kernel may reach another device: no remote copies, remote signals or barrier semaphores. Data moves between devices by JAX's collectives and lax.ppermute only.
A program may use at most 64 MiB of HBM per device.

v0:
```python
import jax
import jax.numpy as jnp
from jax import lax
from jax.sharding import PartitionSpec as P

QBLOCK = 32


def restore(code, scale):
    count, width = code.shape
    blocks = code.astype(jnp.float32).reshape(count, width // QBLOCK, QBLOCK) * scale[:, :, None]
    return blocks.reshape(count, width).astype(jnp.bfloat16)


def local(
    grad_out,
    ctx_code,
    ctx_scale,
    stream_code,
    stream_scale,
    hidden_code,
    hidden_scale,
    out_weight,
    up_weight,
    down_weight,
):
    grad_rows = lax.all_gather(grad_out, "cols", axis=0, tiled=True)
    hid_code, hid_scale = (
        lax.all_gather(hidden_code, "rows", axis=0, tiled=True),
        lax.all_gather(hidden_scale.astype(jnp.bfloat16), "rows", axis=0, tiled=True).astype(
            hidden_scale.dtype
        ),
    )
    preact_all = restore(hid_code, hid_scale).astype(jnp.float32)
    positive_all = jnp.maximum(preact_all, 0.0)
    piece = grad_rows
    grad_act_local = lax.psum_scatter(
        jnp.dot(piece, down_weight.T, preferred_element_type=jnp.float32).astype(jnp.bfloat16),
        "rows",
        scatter_dimension=0,
        tiled=True,
    ).astype(jnp.float32)
    positive_local = jnp.maximum(restore(hidden_code, hidden_scale).astype(jnp.float32), 0.0)
    grad_pre_local = (grad_act_local * 2.0 * positive_local).astype(jnp.bfloat16)
    grad_pre_all = lax.all_gather(grad_pre_local, "rows", axis=0, tiled=True)
    act_all = (positive_all * positive_all).astype(jnp.bfloat16)
    grad_down = jnp.dot(act_all.T, grad_rows, preferred_element_type=jnp.float32)
    str_code, str_scale = (
        lax.all_gather(stream_code, "cols", axis=0, tiled=True),
        lax.all_gather(stream_scale.astype(jnp.bfloat16), "cols", axis=0, tiled=True).astype(
            stream_scale.dtype
        ),
    )
    stream_rows = restore(str_code, str_scale)
    grad_up = jnp.dot(stream_rows.T, grad_pre_all, preferred_element_type=jnp.float32)
    piece = grad_pre_all
    summed_local = lax.psum_scatter(
        jnp.dot(piece, up_weight.T, preferred_element_type=jnp.float32),
        "cols",
        scatter_dimension=0,
        tiled=True,
    )
    grad_stream_local = (grad_out.astype(jnp.float32) + summed_local).astype(jnp.bfloat16)
    grad_stream_rows = lax.all_gather(grad_stream_local, "cols", axis=0, tiled=True)
    con_code, con_scale = (
        lax.all_gather(ctx_code, "rows", axis=0, tiled=True),
        lax.all_gather(ctx_scale.astype(jnp.bfloat16), "rows", axis=0, tiled=True).astype(
            ctx_scale.dtype
        ),
    )
    context_all = restore(con_code, con_scale)
    grad_outw = jnp.dot(context_all.T, grad_stream_rows, preferred_element_type=jnp.float32)
    piece = grad_stream_rows
    grad_ctx = lax.psum_scatter(
        jnp.dot(piece, out_weight.T, preferred_element_type=jnp.float32).astype(jnp.bfloat16),
        "rows",
        scatter_dimension=0,
        tiled=True,
    )
    return (grad_ctx, grad_outw, grad_up, grad_down)


def solution(mesh):
    in_specs = (
        P("cols", "rows"),
        P("rows", "cols"),
        P("rows", "cols"),
        P("cols", "rows"),
        P("cols", "rows"),
        P("rows", "cols"),
        P("rows", "cols"),
        P("cols", "rows"),
        P("rows", "cols"),
        P("cols", "rows"),
    )
    out_specs = (P("rows", "cols"), P("cols", "rows"), P("rows", "cols"), P("cols", "rows"))
    return jax.shard_map(local, mesh=mesh, in_specs=in_specs, out_specs=out_specs, check_vma=False)
```

profile of v0, /device:TPU:1, one launch (start us, length us, event | category | flops | bytes accessed | tf_op | source)
XLA Modules:
  0.0 781.9 jit_solution(10425792867628815745)
XLA Ops:
  7.2 0.7 all-gather.4.cloned.1.call-update
  8.0 151.1 %all-gather.4.cloned.1.call-done = bf16[1024,768]{1,0:T(8,128)(2,1)} async-done(((bf16[16,768]{1,0:T(8,128)(2,1)}), bf16[1024,768]{1,0:T(8,128)(2,1)}) %all-gather.4.cloned.1.call-update) | async-done | bytes 1572880 | tf_op jit(solution)/shard_map/all_gather | solution.py:27
  159.1 3.4 convolution_convert_fusion
  162.5 0.0 reduce-scatter.8.cloned.1.call-start
  162.6 0.1 copy.28
  162.7 34.9 %reduce-scatter.6.cloned.1.call-done = bf16[128,384]{1,0:T(8,128)(2,1)} async-done(((bf16[1024,384]{1,0:T(8,128)(2,1)}), bf16[128,384]{1,0:T(8,128)(2,1)}) %reduce-scatter.6.cloned.1.call-update) | async-done | bytes 98320 | tf_op jit(solution)/shard_map/reduce_scatter | solution.py:37
  197.7 0.9 multiply_convert_fusion.2
  198.6 23.6 %all_gather.28 = bf16[1024,384]{1,0:T(8,128)(2,1)S(1)} all-gather(bf16[128,384]{1,0:T(8,128)(2,1)S(1)} %multiply_convert_fusion.2), channel_id=1, replica_groups=mesh['rows'=8,'cols'=64] {'rows'}, dimensions={0}, use_global_device_ids=true | all-gather | bytes 884736 | tf_op jit(solution)/shard_map/all_gather | solution.py:45
  222.2 2.7 fusion.6
  225.0 0.5 all-gather.8.cloned.1.call-update
  225.5 216.2 %reduce-scatter.8.cloned.1.call-done = f32[16,768]{1,0:T(8,128)} async-done(((f32[1024,768]{1,0:T(8,128)}), f32[16,768]{1,0:T(8,128)}) %reduce-scatter.8.cloned.1.call-update) | async-done | bytes 49168 | tf_op jit(solution)/shard_map/reduce_scatter | solution.py:57
  441.8 1.4 add_convert_fusion
  443.2 0.0 reduce-scatter.10.cloned.1.call-start
  443.3 0.1 copy.31
  443.4 14.1 %all_gather.31 = bf16[1024,3]{0,1:T(4,128)(2,1)S(1)} all-gather(bf16[128,3]{0,1:T(4,128)(2,1)S(1)} %convert_element_type.79), channel_id=1, replica_groups=mesh['rows'=8,'cols'=64] {'rows'}, dimensions={0}, use_global_device_ids=true | all-gather | bytes 6912 | tf_op jit(solution)/shard_map/all_gather | solution.py:67
  457.6 90.7 %all_gather.33 = bf16[1024,24]{1,0:T(8,128)(2,1)S(1)} all-gather(bf16[16,24]{1,0:T(8,128)(2,1)S(1)} %convert_element_type.83), channel_id=1, replica_groups=mesh['rows'=8,'cols'=64] {'cols'}, dimensions={0}, use_global_device_ids=true | all-gather | bytes 49920 | tf_op jit(solution)/shard_map/all_gather | solution.py:50
  548.3 0.1 copy.30
  548.5 20.0 %all_gather.35 = bf16[1024,12]{0,1:T(8,128)(2,1)S(1)} all-gather(bf16[128,12]{0,1:T(8,128)(2,1)S(1)} %convert_element_type.87), channel_id=1, replica_groups=mesh['rows'=8,'cols'=64] {'rows'}, dimensions={0}, use_global_device_ids=true | all-gather | bytes 27648 | tf_op jit(solution)/shard_map/all_gather | solution.py:30
  568.5 21.4 %all_gather.30 = bf16[1024,96]{0,1:T(8,128)(2,1)S(1)} all-gather(bf16[128,96]{0,1:T(8,128)(2,1)S(1)} %copy-done.8), channel_id=1, replica_groups=mesh['rows'=8,'cols'=64] {'rows'}, dimensions={0}, use_global_device_ids=true | all-gather | bytes 221184 | tf_op jit(solution)/shard_map/all_gather | solution.py:66
  590.0 21.7 %all_gather.34 = bf16[1024,384]{0,1:T(8,128)(2,1)S(1)} all-gather(bf16[128,384]{0,1:T(8,128)(2,1)S(1)} %copy.31), channel_id=1, replica_groups=mesh['rows'=8,'cols'=64] {'rows'}, dimensions={0}, use_global_device_ids=true | all-gather | bytes 884736 | tf_op jit(solution)/shard_map/all_gather | solution.py:29
  611.7 1.1 fusion.1
  612.8 1.7 copy.29
  614.6 1.5 fusion
  616.1 0.7 copy-done.11
  616.8 1.8 fusion.2
  618.6 118.4 %all-gather.6.cloned.1.call-done = bf16[1024,768]{1,0:T(8,128)(2,1)} async-done(((bf16[16,768]{1,0:T(8,128)(2,1)}), bf16[1024,768]{1,0:T(8,128)(2,1)}) %all-gather.6.cloned.1.call-update) | async-done | bytes 1572880 | tf_op jit(solution)/shard_map/all_gather | solution.py:64
  736.9 2.0 convolution_convert_fusion.1
  739.0 0.8 copy.32
  739.8 2.0 fusion.8
  741.8 1.1 fusion.7
  742.9 30.6 %reduce-scatter.10.cloned.1.call-done = bf16[128,96]{1,0:T(8,128)(2,1)} async-done(((bf16[1024,96]{1,0:T(8,128)(2,1)}), bf16[128,96]{1,0:T(8,128)(2,1)}) %reduce-scatter.10.cloned.1.call-update) | async-done | bytes 24592
  773.6 1.5 copy.33
  (40 shorter events, 0.4 us)
Async XLA Ops:
  7.2 215.1 %copy-start = (bf16[768,384]{1,0:T(8,128)(2,1)S(1)}, bf16[768,384]{1,0:T(8,128)(2,1)}, u32[]{:S(2)}) copy-start(bf16[768,384]{1,0:T(8,128)(2,1)} %param.18) | copy-start | bytes 1769476
  7.2 151.9 %all-gather.4.cloned.1.call-start = ((), (), s32[]{:S(2)}) async-start(), calls=%async_computation.3 | async-start | bytes 1597440 | tf_op jit(solution)/shard_map/all_gather | solution.py:27
  7.9 154.7 %copy-start.7 = (f32[128,12]{0,1:T(8,128)S(1)}, f32[128,12]{0,1:T(8,128)}, u32[]{:S(2)}) copy-start(f32[128,12]{0,1:T(8,128)} %param.16) | copy-start | bytes 18436
  7.9 189.7 %copy-start.4 = (bf16[128,384]{1,0:T(8,128)(2,1)S(1)}, bf16[128,384]{1,0:T(8,128)(2,1)}, u32[]{:S(2)}) copy-start(bf16[128,384]{1,0:T(8,128)(2,1)} %param.15) | copy-start | bytes 294916
  7.9 189.7 %reduce-scatter.6.cloned.1.call-start = ((), (), s32[]{:S(2)}) async-start(), calls=%async_computation.4 | async-start | bytes 884736 | tf_op jit(solution)/shard_map/reduce_scatter | solution.py:37
  162.5 279.2 %reduce-scatter.8.cloned.1.call-start = ((), (), s32[]{:S(2)}) async-start(), calls=%async_computation.5 | async-start | bytes 3194880 | tf_op jit(solution)/shard_map/reduce_scatter | solution.py:57
  224.9 216.9 %copy-start.6 = (bf16[16,768]{1,0:T(8,128)(2,1)S(1)}, bf16[16,768]{1,0:T(8,128)(2,1)}, u32[]{:S(2)}) copy-start(bf16[16,768]{1,0:T(8,128)(2,1)} %param.10) | copy-start | bytes 73732
  224.9 218.5 %copy-start.10 = (f32[128,3]{0,1:T(4,128)S(1)}, f32[128,3]{0,1:T(4,128)}, u32[]{:S(2)}) copy-start(f32[128,3]{0,1:T(4,128)} %param.12) | copy-start | bytes 4612
  224.9 232.7 %copy-start.9 = (f32[16,24]{1,0:T(8,128)S(1)}, f32[16,24]{1,0:T(8,128)}, u32[]{:S(2)}) copy-start(f32[16,24]{1,0:T(8,128)} %param.14) | copy-start | bytes 4612
  224.9 343.6 %copy-start.8 = (bf16[128,96]{0,1:T(8,128)(2,1)S(1)}, bf16[128,96]{0,1:T(8,128)(2,1)}, u32[]{:S(2)}) copy-start(bf16[128,96]{0,1:T(8,128)(2,1)} %param.11) | copy-start | bytes 73732
  224.9 387.9 %all-gather.8.cloned.1.call-start = ((), (), s32[]{:S(2)}) async-start(), calls=%async_computation.7 | async-start | bytes 1597440 | tf_op jit(solution)/shard_map/all_gather | solution.py:49
  225.5 511.4 %all-gather.6.cloned.1.call-start = ((), (), s32[]{:S(2)}) async-start(), calls=%async_computation.6 | async-start | bytes 1597440 | tf_op jit(solution)/shard_map/all_gather | solution.py:64
  443.2 330.4 %reduce-scatter.10.cloned.1.call-start = ((), (), s32[]{:S(2)}) async-start(), calls=%async_computation.8 | async-start | bytes 294912
  614.5 1.6 copy-start.3
  614.5 2.2 copy-start.11
  616.8 120.2 %copy-start.5 = (bf16[96,768]{1,0:T(8,128)(2,1)S(1)}, bf16[96,768]{1,0:T(8,128)(2,1)}, u32[]{:S(2)}) copy-start(bf16[96,768]{1,0:T(8,128)(2,1)} %param.17) | copy-start | bytes 442372
  618.6 121.2 %copy-start.2 = (bf16[1024,768]{0,1:T(8,128)(2,1)S(1)}, bf16[1024,768]{0,1:T(8,128)(2,1)}, u32[]{:S(2)}) copy-start(bf16[1024,768]{0,1:T(8,128)(2,1)} %fusion) | copy-start | bytes 4718596
  739.8 2.0 copy-start.1
Sparse Core Ops, SparseCore 0:
  11.3 147.7 all-gather.3
  162.6 34.9 reduce-scatter.5
  225.0 216.6 reduce-scatter.7
  445.4 150.8 all-gather.7
  600.5 136.3 all-gather.5
  739.9 33.5 reduce-scatter.9
where the time goes:
time: 786 us; the launch traced here: 782 us
  waiting for transfers between devices  553 us (70%)
  blocking collectives  192 us (24%)
  between operations  14.3 us (2%)
  matrix products  13 us (2%)
    reduce_scatter x1, waiting for transfers between devices, local(): lax.psum_scatter(jnp.dot(piece, up_weight.T, preferred_element_type=jnp.f...  216 us
    all_gather x1, waiting for transfers between devices, local(): grad_rows = lax.all_gather(grad_out, 'cols', axis=0, tiled=True)  151 us
    all_gather x1, waiting for transfers between devices, local(): lax.all_gather(grad_stream_local, 'cols', axis=0, tiled=True)  118 us
    all_gather x1, blocking collectives, local(): lax.all_gather(stream_scale.astype(jnp.bfloat16), 'cols', axis=0, tiled=T...  90.7 us
    reduce_scatter x1, waiting for transfers between devices, local(): lax.psum_scatter(jnp.dot(piece, down_weight.T, preferred_element_type=jnp...  34.9 us
    unnamed x7, waiting for transfers between devices  31.9 us
    all_gather x1, blocking collectives, local(): grad_pre_all = lax.all_gather(grad_pre_local, 'rows', axis=0, tiled=True)  23.6 us
    all_gather x1, blocking collectives, local(): lax.all_gather(hidden_code, 'rows', axis=0, tiled=True)  21.7 us
  transfers between devices with their start and end apart: 6, of which 5 were waited for; matrix products, arithmetic and copies ran while one was open for 1% of the time, Pallas kernels for 0%

commit v1 on v0

v1 whole, which is shorter than its diff:
```python
import jax
import jax.numpy as jnp
from jax import lax
from jax.sharding import Mesh
from jax.sharding import PartitionSpec as P

QBLOCK = 32
ROWS = ("x", "yl")
COLS = ("yh", "z", "c")
SWAP = ((0, 1), (1, 0))


def restore(code, scale):
    count, width = code.shape
    blocks = code.astype(jnp.float32).reshape(count, width // QBLOCK, QBLOCK) * scale[:, :, None]
    return blocks.reshape(count, width).astype(jnp.bfloat16)


def dot_nt(left, right):
    return lax.dot_general(
        left, right, (((1,), (1,)), ((), ())), preferred_element_type=jnp.float32
    )


def dot_tn(left, right):
    return lax.dot_general(
        left, right, (((0,), (0,)), ((), ())), preferred_element_type=jnp.float32
    )


def local(
    grad_out,
    ctx_code,
    ctx_scale,
    stream_code,
    stream_scale,
    hidden_code,
    hidden_scale,
    out_weight,
    up_weight,
    down_weight,
):
    core = lax.axis_index("c")
    half = lax.axis_index("yh")
    n_rows, n_z = lax.axis_size(ROWS), lax.axis_size("z")
    per = grad_out.shape[0]
    runs = n_z * 2 // n_rows
    features = grad_out.shape[1]

    def own_first(block):
        width = block.shape[1]
        parts = block.reshape(runs, 2, per, width)
        one, two = parts[:, 0], parts[:, 1]
        first = jnp.where(core == 0, one, two)
        second = jnp.where(core == 0, two, one)
        return jnp.stack([first, second]).reshape(block.shape)

    def natural(block):
        width = block.shape[1]
        parts = block.reshape(2, runs, per, width)
        one = jnp.where(core == 0, parts[0], parts[1])
        two = jnp.where(core == 0, parts[1], parts[0])
        return jnp.stack([one, two], axis=1).reshape(block.shape)

    def swap(block, axis):
        return lax.ppermute(block, axis, SWAP)

    def scatter_rows(own, other):
        width = own.shape[1]
        sent = jnp.stack(
            [own.reshape(n_rows, -1, width), other.reshape(n_rows, -1, width)], axis=1
        )
        came = lax.all_to_all(sent, ROWS, 0, 0, tiled=True)
        return jnp.sum(came.astype(jnp.float32), axis=0).reshape(-1, width)

    def gather_z(pair):
        return lax.all_gather(pair, "z", axis=1).reshape(-1, features)

    stream = restore(stream_code, stream_scale)
    positive = jnp.maximum(
        own_first(restore(hidden_code, hidden_scale)).astype(jnp.float32), 0.0
    )
    act = (positive * positive).astype(jnp.bfloat16)
    context = own_first(restore(ctx_code, ctx_scale))
    hidden_width, ctx_width = act.shape[1], context.shape[1]
    padding = jnp.zeros((act.shape[0], 512 - hidden_width - ctx_width), jnp.bfloat16)
    saved = jnp.concatenate([act, context, padding], axis=1)
    saved_all = lax.all_gather(saved, ROWS, axis=0)

    both = lax.all_gather(jnp.stack([grad_out, stream]), "yh", axis=0)
    stream_all = lax.all_gather(both[:, 1], ("z", "c"), axis=0)
    grad_own = gather_z(both[:, 0])
    grad_other = swap(grad_own, "c")

    grad_act = scatter_rows(
        dot_nt(grad_own, down_weight).astype(jnp.bfloat16),
        dot_nt(grad_other, down_weight).astype(jnp.bfloat16),
    )
    grad_pre = (grad_act * 2.0 * positive).astype(jnp.bfloat16)
    copies = lax.optimization_barrier(
        jnp.broadcast_to(grad_pre[None], (n_rows,) + grad_pre.shape)
    )
    grad_pre_all = lax.all_to_all(copies, ROWS, 0, 0, tiled=True).reshape(
        n_rows, 2, -1, hidden_width
    )
    pre_own = grad_pre_all[:, 0].reshape(-1, hidden_width)
    pre_other = grad_pre_all[:, 1].reshape(-1, hidden_width)

    came = swap(dot_nt(pre_other, up_weight).astype(jnp.bfloat16), "c")
    part = (dot_nt(pre_own, up_weight) + came.astype(jnp.float32)).reshape(2, -1, features)
    keep = lax.dynamic_index_in_dim(part, half, 0, keepdims=False)
    send = lax.dynamic_index_in_dim(part, 1 - half, 0, keepdims=False).astype(jnp.bfloat16)
    part = (keep + swap(send, "yh").astype(jnp.float32)).astype(jnp.bfloat16)
    came = lax.all_to_all(part.reshape(n_z, per, features), "z", 0, 0, tiled=True)
    summed = jnp.sum(came.astype(jnp.float32), axis=0)
    grad_stream = (grad_out.astype(jnp.float32) + summed).astype(jnp.bfloat16)

    gs_own = gather_z(lax.all_gather(grad_stream, "yh", axis=0))
    gs_other = swap(gs_own, "c")
    grad_ctx = natural(
        scatter_rows(
            dot_nt(gs_own, out_weight).astype(jnp.bfloat16),
            dot_nt(gs_other, out_weight).astype(jnp.bfloat16),
        )
    ).astype(jnp.bfloat16)

    saved_own = saved_all.reshape(n_rows, 2, -1, 512)[:, 0].reshape(-1, 512)
    saved_other = saved_all.reshape(n_rows, 2, -1, 512)[:, 1].reshape(-1, 512)
    act_own, act_other = saved_own[:, :hidden_width], saved_other[:, :hidden_width]
    ctx_own = saved_own[:, hidden_width : hidden_width + ctx_width]
    ctx_other = saved_other[:, hidden_width : hidden_width + ctx_width]
    by_core = stream_all.reshape(n_z, 2, 2, per, features)
    stream_own = lax.dynamic_index_in_dim(by_core, core, 1, keepdims=False)
    stream_other = lax.dynamic_index_in_dim(by_core, 1 - core, 1, keepdims=False)
    stream_own = jnp.swapaxes(stream_own, 0, 1).reshape(-1, features)
    stream_other = jnp.swapaxes(stream_other, 0, 1).reshape(-1, features)

    grad_down = dot_tn(act_own, grad_own) + dot_tn(act_other, grad_other)
    grad_up = dot_tn(stream_own, pre_own) + dot_tn(stream_other, pre_other)
    grad_outw = dot_tn(ctx_own, gs_own) + dot_tn(ctx_other, gs_other)
    return (grad_ctx, grad_outw, grad_up, grad_down)


def solution(mesh):
    parts = Mesh(mesh.devices.reshape(4, 2, 2, 16, 2), ROWS + COLS)
    by_cols, by_rows = P(COLS, ROWS), P(ROWS, COLS)
    in_specs = (
        by_cols,
        by_rows,
        by_rows,
        by_cols,
        by_cols,
        by_rows,
        by_rows,
        by_cols,
        by_rows,
        by_cols,
    )
    out_specs = (by_rows, by_cols, by_rows, by_cols)
    return jax.shard_map(local, mesh=parts, in_specs=in_specs, out_specs=out_specs, check_vma=False)
```

time: 786 us -> 262 us (0.33)
  waiting for transfers between devices: 553 us -> 84.1 us
  blocking collectives: 192 us -> 86 us
  starting transfers between devices: 0.24 us -> 50.5 us
    reduce_scatter x2 -> x0, waiting for transfers between devices: 251 us -> none  [the longest x1 216 us: local(): lax.psum_scatter(jnp.dot(piece, up_weight.T, preferred_element_type=jnp.f...]
    all_gather x3 -> x2, waiting for transfers between devices: 269 us -> 56 us  [the longest x1 35.4 us: local(): saved_all = lax.all_gather(saved, ROWS, axis=0)]
    all_gather x6 -> x4, blocking collectives: 192 us -> 72.1 us  [the longest x2 61.3 us: gather_z(): return lax.all_gather(pair, 'z', axis=1).reshape(-1, features)]
    ppermute x0 -> x4, starting transfers between devices: none -> 35.6 us  [swap(): return lax.ppermute(block, axis, SWAP)]
    unnamed x7 -> x2, waiting for transfers between devices: 31.9 us -> 0.7 us
    all_to_all x0 -> x3, waiting for transfers between devices: none -> 15.6 us  [the longest x2 15.6 us: scatter_rows(): came = lax.all_to_all(sent, ROWS, 0, 0, tiled=True)]
    all_to_all x0 -> x3, starting transfers between devices: none -> 14.8 us  [the longest x2 8.57 us: scatter_rows(): came = lax.all_to_all(sent, ROWS, 0, 0, tiled=True)]
    all_to_all x0 -> x1, blocking collectives: none -> 13.8 us  [local(): lax.all_to_all(copies, ROWS, 0, 0, tiled=True)]
  transfers between devices with their start and end apart: 6 -> 9, of which waited for: 5 -> 7; matrix products, arithmetic and copies ran while one was open for 1% -> 7% of each run, Pallas kernels for 0% -> 0%
where the time goes in v1:
time: 262 us; the launch traced here: 261 us
  blocking collectives  86 us (33%)
  waiting for transfers between devices  84.1 us (32%)
  starting transfers between devices  50.5 us (19%)
  between operations  14.5 us (6%)
  matrix products  11.6 us (4%)
  local copies, waits for them, and re-layouts  9.65 us (4%)
  other arithmetic  4.4 us (2%)
    all_gather x2, blocking collectives, gather_z(): return lax.all_gather(pair, 'z', axis=1).reshape(-1, features)  61.3 us
    ppermute x4, starting transfers between devices, swap(): return lax.ppermute(block, axis, SWAP)  35.6 us
    all_gather x1, waiting for transfers between devices, local(): saved_all = lax.all_gather(saved, ROWS, axis=0)  35.4 us
    all_gather x1, waiting for transfers between devices, local(): stream_all = lax.all_gather(both[:, 1], ('z', 'c'), axis=0)  20.6 us
    all_to_all x2, waiting for transfers between devices, scatter_rows(): came = lax.all_to_all(sent, ROWS, 0, 0, tiled=True)  15.6 us
    all_to_all x1, blocking collectives, local(): lax.all_to_all(copies, ROWS, 0, 0, tiled=True)  13.8 us
    ppermute x4, waiting for transfers between devices, swap(): return lax.ppermute(block, axis, SWAP)  11.7 us
    all_to_all x2, starting transfers between devices, scatter_rows(): came = lax.all_to_all(sent, ROWS, 0, 0, tiled=True)  8.57 us
  transfers between devices with their start and end apart: 9, of which 7 were waited for; matrix products, arithmetic and copies ran while one was open for 7% of the time, Pallas kernels for 0%

profile of v1, /device:TPU:1, one launch (start us, length us, event | category | flops | bytes accessed | tf_op | source)
XLA Modules:
  0.0 260.7 jit_solution(12648872799093460517)
XLA Ops:
  7.2 0.9 mul.56
  8.2 0.7 fusion.12
  9.7 5.9 %all-gather = bf16[4,16,768]{2,1,0:T(8,128)(2,1)S(1)} all-gather(bf16[2,16,768]{2,1,0:T(8,128)(2,1)S(1)} %pad_maximum_fusion.2), channel_id=2, replica_groups=mesh['x'=4,'yl'=2,'yh'=2,'z'=16,'c'=2] {'yh'}, dimensions={0}, use_global_device_ids=true | all-gather | bytes 147456 | tf_op jit(solution)/shard_map/all_gather | solution.py:90
  16.2 33.2 %all_gather.32 = bf16[2,16,16,768]{3,2,1,0:T(8,128)(2,1)S(1)} all-gather(bf16[2,1,16,768]{3,2,1,0:T(8,128)(2,1)S(1)} %get-tuple-element.29), channel_id=1, replica_groups=mesh['x'=4,'yl'=2,'yh'=2,'z'=16,'c'=2] {'z'}, dimensions={1}, use_global_device_ids=true | all-gather | bytes 835584 | tf_op jit(solution)/shard_map/all_gather | solution.py:77
  49.4 10.8 %collective-permute-start = (bf16[512,768]{1,0:T(8,128)(2,1)S(1)}, bf16[512,768]{1,0:T(8,128)(2,1)S(1)}, u32[]{:S(2)}, u32[]{:S(2)}) collective-permute-start(bf16[512,768]{1,0:T(8,128)(2,1)S(1)} %bitcast.102), channel_id=1, source_target_pairs={{0,1},{1,0},{2,3},{3,2},{4,5},{5,4},{6,7},{7,6},{8,9},{9,8},{10,11... | collective-permute-start | bytes 2359304 | tf_op jit(solution)/shard_map/ppermute | solution.py:66
  60.9 1.3 collective-permute-done
  63.0 1.0 pad_maximum_fusion
  64.0 5.2 %all-to-all-start = ((bf16[8,2,64,384]{3,2,1,0:T(8,128)(2,1)}), bf16[8,2,64,384]{3,2,1,0:T(8,128)(2,1)S(1)}, u32[]{:S(2)}, u32[]{:S(2)}) async-start(bf16[8,2,64,384]{3,2,1,0:T(8,128)(2,1)} %pad_maximum_fusion), calls=%async_computation | async-start | bytes 1572864 | tf_op jit(solution)/shard_map/all_to_all | solution.py:73
  70.3 10.8 %all-to-all-done = bf16[8,2,64,384]{3,2,1,0:T(8,128)(2,1)S(1)} async-done(((bf16[8,2,64,384]{3,2,1,0:T(8,128)(2,1)}), bf16[8,2,64,384]{3,2,1,0:T(8,128)(2,1)S(1)}, u32[]{:S(2)}, u32[]{:S(2)}) %all-to-all-start) | async-done | bytes 786464 | tf_op jit(solution)/shard_map/all_to_all | solution.py:73
  81.3 13.8 %all_to_all.20 = bf16[8,128,384]{2,1,0:T(8,128)(2,1)S(1)} all-to-all(bf16[8,128,384]{2,1,0:T(8,128)(2,1)S(1)} %broadcast_in_dim.4), channel_id=1, replica_groups=mesh['x'=4,'yl'=2,'yh'=2,'z'=16,'c'=2] {'x','yl'}, dimensions={0} | all-to-all | bytes 1572864 | tf_op jit(solution)/shard_map/all_to_all | solution.py:103
  95.9 4.6 %collective-permute-start.1 = (bf16[512,768]{1,0:T(8,128)(2,1)S(1)}, bf16[512,768]{1,0:T(8,128)(2,1)}, u32[]{:S(2)}, u32[]{:S(2)}) collective-permute-start(bf16[512,768]{1,0:T(8,128)(2,1)S(1)} %convolution_convert_fusion), channel_id=1, source_target_pairs={{0,1},{1,0},{2,3},{3,2},{4,5},{5,4},{6,7},{7,6},{8,9},{9,8},{10,11... | collective-permute-start | bytes 2359304 | tf_op jit(solution)/shard_map/ppermute | solution.py:66
  101.5 1.0 collective-permute-done.1
  102.6 1.7 convert_add_fusion
  104.3 0.8 fusion.1
  105.1 4.5 %collective-permute-start.2 = (bf16[256,768]{1,0:T(8,128)(2,1)}, bf16[256,768]{1,0:T(8,128)(2,1)S(1)}, u32[]{:S(2)}, u32[]{:S(2)}) collective-permute-start(bf16[256,768]{1,0:T(8,128)(2,1)} %fusion.1), channel_id=1, source_target_pairs={{0,32},{32,0},{1,33},{33,1},{2,34},{34,2},{3,35},{35,3},{4,36},{36... | collective-permute-start | bytes 1179656 | tf_op jit(solution)/shard_map/ppermute | solution.py:66
  109.6 9.4 %collective-permute-done.2 = bf16[256,768]{1,0:T(8,128)(2,1)S(1)} collective-permute-done((bf16[256,768]{1,0:T(8,128)(2,1)}, bf16[256,768]{1,0:T(8,128)(2,1)S(1)}, u32[]{:S(2)}, u32[]{:S(2)}) %collective-permute-start.2) | collective-permute-done | bytes 393248 | tf_op jit(solution)/shard_map/ppermute | solution.py:66
  119.0 0.8 fusion
  119.8 6.2 %all-to-all-start.2 = ((bf16[16,16,768]{2,1,0:T(8,128)(2,1)}), bf16[16,16,768]{2,1,0:T(8,128)(2,1)S(1)}, u32[]{:S(2)}, u32[]{:S(2)}) async-start(bf16[16,16,768]{2,1,0:T(8,128)(2,1)} %bitcast.20), calls=%async_computation.2 | async-start | bytes 786432 | tf_op jit(solution)/shard_map/all_to_all | solution.py:114
  126.1 20.6 %all-gather.10.cloned.1.call-done = bf16[64,1,16,768]{3,2,1,0:T(8,128)(2,1)} async-done(((bf16[2,1,16,768]{3,2,1,0:T(8,128)(2,1)}), bf16[64,1,16,768]{3,2,1,0:T(8,128)(2,1)}) %all-gather.10.cloned.1.call-update) | async-done | bytes 1572880 | tf_op jit(solution)/shard_map/all_gather | solution.py:91
  146.7 1.5 dynamic-slice_bitcast_fusion
  148.9 1.6 convolution_add_fusion.1
  150.5 35.4 %all-gather.8.cloned.1.call-done = bf16[1024,512]{1,0:T(8,128)(2,1)} async-done(((bf16[128,512]{1,0:T(8,128)(2,1)}), bf16[1024,512]{1,0:T(8,128)(2,1)}) %all-gather.8.cloned.1.call-update) | async-done | bytes 1048592 | tf_op jit(solution)/shard_map/all_gather | solution.py:88
  185.9 2.1 fusion.13
  188.0 0.8 copy-done.4
  189.6 5.0 %all-gather.1 = bf16[32,768]{1,0:T(8,128)(2,1)S(1)} all-gather(bf16[16,768]{1,0:T(8,128)(2,1)S(1)} %add_convert_fusion), channel_id=3, replica_groups=mesh['x'=4,'yl'=2,'yh'=2,'z'=16,'c'=2] {'yh'}, dimensions={0}, use_global_device_ids=true | all-gather | bytes 73728 | tf_op jit(solution)/shard_map/all_gather | solution.py:118
  194.6 28.1 %all-gather.2 = bf16[2,256,768]{2,1,0:T(8,128)(2,1)S(1)} all-gather(bf16[2,16,768]{2,1,0:T(8,128)(2,1)S(1)} %bitcast.118), channel_id=4, replica_groups=mesh['x'=4,'yl'=2,'yh'=2,'z'=16,'c'=2] {'z'}, dimensions={1}, use_global_device_ids=true | all-gather | bytes 835584 | tf_op jit(solution)/shard_map/all_gather | solution.py:77
  222.6 15.7 %collective-permute-start.3 = (bf16[512,768]{1,0:T(8,128)(2,1)S(1)}, bf16[512,768]{1,0:T(8,128)(2,1)S(1)}, u32[]{:S(2)}, u32[]{:S(2)}) collective-permute-start(bf16[512,768]{1,0:T(8,128)(2,1)S(1)} %bitcast.91), channel_id=1, source_target_pairs={{0,1},{1,0},{2,3},{3,2},{4,5},{5,4},{6,7},{7,6},{8,9},{9,8},{10,11... | collective-permute-start | bytes 2359304 | tf_op jit(solution)/shard_map/ppermute | solution.py:66
  238.3 1.5 convolution_add_fusion
  240.3 1.2 fusion.9
  242.8 3.4 %all-to-all-start.3 = ((bf16[8,2,64,96]{3,2,1,0:T(8,128)(2,1)}), bf16[8,2,64,96]{3,2,1,0:T(8,128)(2,1)S(1)}, u32[]{:S(2)}, u32[]{:S(2)}) async-start(bf16[8,2,64,96]{3,2,1,0:T(8,128)(2,1)} %copy.56), calls=%async_computation.3 | async-start | bytes 524288 | tf_op jit(solution)/shard_map/all_to_all | solution.py:73
  246.3 1.9 convolution_add_fusion.2
  248.2 4.8 %all-to-all-done.3 = bf16[8,2,64,96]{3,2,1,0:T(8,128)(2,1)S(1)} async-done(((bf16[8,2,64,96]{3,2,1,0:T(8,128)(2,1)}), bf16[8,2,64,96]{3,2,1,0:T(8,128)(2,1)S(1)}, u32[]{:S(2)}, u32[]{:S(2)}) %all-to-all-start.3) | async-done | bytes 196640 | tf_op jit(solution)/shard_map/all_to_all | solution.py:73
  (73 shorter events, 9.8 us)
Async XLA Ops:
  7.2 88.1 %copy-start = (bf16[768,384]{1,0:T(8,128)(2,1)S(1)}, bf16[768,384]{1,0:T(8,128)(2,1)}, u32[]{:S(2)}) copy-start(bf16[768,384]{1,0:T(8,128)(2,1)} %param.18) | copy-start | bytes 1769476
  7.2 53.1 %copy-start.13 = (bf16[384,768]{1,0:T(8,128)(2,1)S(1)}, bf16[384,768]{1,0:T(8,128)(2,1)}, u32[]{:S(2)}) copy-start(bf16[384,768]{1,0:T(8,128)(2,1)} %param.19) | copy-start | bytes 1769476
  49.4 13.3 %copy-start.1 = (bf16[2,16,16,768]{3,2,1,0:T(8,128)(2,1)}, bf16[2,16,16,768]{3,2,1,0:T(8,128)(2,1)S(1)}, u32[]{:S(2)}) copy-start(bf16[2,16,16,768]{3,2,1,0:T(8,128)(2,1)S(1)} %all_gather.32) | copy-start | bytes 2359300
  49.4 12.7 %collective-permute-start = (bf16[512,768]{1,0:T(8,128)(2,1)S(1)}, bf16[512,768]{1,0:T(8,128)(2,1)S(1)}, u32[]{:S(2)}, u32[]{:S(2)}) collective-permute-start(bf16[512,768]{1,0:T(8,128)(2,1)S(1)} %bitcast.102), channel_id=1, source_target_pairs={{0,1},{1,0},{2,3},{3,2},{4,5},{5,4},{6,7},{7,6},{8,9},{9,8},{10,11... | collective-permute-start | bytes 2359304 | tf_op jit(solution)/shard_map/ppermute | solution.py:66
  62.1 0.9 copy-start.5
  64.0 6.0 %copy-start.8 = (bf16[128,384]{1,0:T(8,128)(2,1)S(1)}, bf16[128,384]{1,0:T(8,128)(2,1)}, u32[]{:S(2)}) copy-start(bf16[128,384]{1,0:T(8,128)(2,1)} %param.15) | copy-start | bytes 294916
  64.0 6.1 %copy-start.11 = (f32[128,12]{0,1:T(8,128)S(1)}, f32[128,12]{0,1:T(8,128)}, u32[]{:S(2)}) copy-start(f32[128,12]{0,1:T(8,128)} %param.16) | copy-start | bytes 18436
  64.0 17.1 %all-to-all-start = ((bf16[8,2,64,384]{3,2,1,0:T(8,128)(2,1)}), bf16[8,2,64,384]{3,2,1,0:T(8,128)(2,1)S(1)}, u32[]{:S(2)}, u32[]{:S(2)}) async-start(bf16[8,2,64,384]{3,2,1,0:T(8,128)(2,1)} %pad_maximum_fusion), calls=%async_computation | async-start | bytes 1572864 | tf_op jit(solution)/shard_map/all_to_all | solution.py:73
  69.2 77.5 %all-gather.10.cloned.1.call-start = ((), (), s32[]{:S(2)}) async-start(), calls=%async_computation.5 | async-start | bytes 1622016 | tf_op jit(solution)/shard_map/all_gather | solution.py:91
  69.9 116.0 %all-gather.8.cloned.1.call-start = ((), (), s32[]{:S(2)}) async-start(), calls=%async_computation.4 | async-start | bytes 1179648 | tf_op jit(solution)/shard_map/all_gather | solution.py:88
  95.3 5.3 %copy-start.10 = (bf16[128,96]{0,1:T(8,128)(2,1)S(1)}, bf16[128,96]{0,1:T(8,128)(2,1)}, u32[]{:S(2)}) copy-start(bf16[128,96]{0,1:T(8,128)(2,1)} %param.11) | copy-start | bytes 73732
  95.3 5.3 %copy-start.12 = (f32[128,3]{0,1:T(4,128)S(1)}, f32[128,3]{0,1:T(4,128)}, u32[]{:S(2)}) copy-start(f32[128,3]{0,1:T(4,128)} %param.12) | copy-start | bytes 4612
  95.9 6.7 %collective-permute-start.1 = (bf16[512,768]{1,0:T(8,128)(2,1)S(1)}, bf16[512,768]{1,0:T(8,128)(2,1)}, u32[]{:S(2)}, u32[]{:S(2)}) collective-permute-start(bf16[512,768]{1,0:T(8,128)(2,1)S(1)} %convolution_convert_fusion), channel_id=1, source_target_pairs={{0,1},{1,0},{2,3},{3,2},{4,5},{5,4},{6,7},{7,6},{8,9},{9,8},{10,11... | collective-permute-start | bytes 2359304 | tf_op jit(solution)/shard_map/ppermute | solution.py:66
  105.1 13.9 %collective-permute-start.2 = (bf16[256,768]{1,0:T(8,128)(2,1)}, bf16[256,768]{1,0:T(8,128)(2,1)S(1)}, u32[]{:S(2)}, u32[]{:S(2)}) collective-permute-start(bf16[256,768]{1,0:T(8,128)(2,1)} %fusion.1), channel_id=1, source_target_pairs={{0,32},{32,0},{1,33},{33,1},{2,34},{34,2},{3,35},{35,3},{4,36},{36... | collective-permute-start | bytes 1179656 | tf_op jit(solution)/shard_map/ppermute | solution.py:66
  119.8 69.5 %all-to-all-start.2 = ((bf16[16,16,768]{2,1,0:T(8,128)(2,1)}), bf16[16,16,768]{2,1,0:T(8,128)(2,1)S(1)}, u32[]{:S(2)}, u32[]{:S(2)}) async-start(bf16[16,16,768]{2,1,0:T(8,128)(2,1)} %bitcast.20), calls=%async_computation.2 | async-start | bytes 786432 | tf_op jit(solution)/shard_map/all_to_all | solution.py:114
  150.5 38.3 %copy-start.2 = (bf16[2,16,16,768]{3,2,1,0:T(8,128)(2,1)S(1)}, bf16[2,16,16,768]{3,2,1,0:T(8,128)(2,1)}, u32[]{:S(2)}) copy-start(bf16[2,16,16,768]{3,2,1,0:T(8,128)(2,1)} %copy-done.1) | copy-start | bytes 2359300
  188.0 0.8 copy-start.4
  188.8 0.7 copy-start.9
  189.3 49.0 %copy-start.3 = (bf16[8,1,64,512]{3,2,1,0:T(8,128)(2,1)S(1)}, bf16[8,1,64,512]{3,2,1,0:T(8,128)(2,1)}, u32[]{:S(2)}) copy-start(bf16[8,1,64,512]{3,2,1,0:T(8,128)(2,1)} %get-tuple-element.22) | copy-start | bytes 1572868
  189.3 49.0 %copy-start.6 = (bf16[512,768]{1,0:T(8,128)(2,1)S(1)}, bf16[512,768]{1,0:T(8,128)(2,1)}, u32[]{:S(2)}) copy-start(bf16[512,768]{1,0:T(8,128)(2,1)} %copy-done.5) | copy-start | bytes 2359300
  222.6 18.9 %collective-permute-start.3 = (bf16[512,768]{1,0:T(8,128)(2,1)S(1)}, bf16[512,768]{1,0:T(8,128)(2,1)S(1)}, u32[]{:S(2)}, u32[]{:S(2)}) collective-permute-start(bf16[512,768]{1,0:T(8,128)(2,1)S(1)} %bitcast.91), channel_id=1, source_target_pairs={{0,1},{1,0},{2,3},{3,2},{4,5},{5,4},{6,7},{7,6},{8,9},{9,8},{10,11... | collective-permute-start | bytes 2359304 | tf_op jit(solution)/shard_map/ppermute | solution.py:66
  238.3 1.5 copy-start.7
  242.8 10.2 %all-to-all-start.3 = ((bf16[8,2,64,96]{3,2,1,0:T(8,128)(2,1)}), bf16[8,2,64,96]{3,2,1,0:T(8,128)(2,1)S(1)}, u32[]{:S(2)}, u32[]{:S(2)}) async-start(bf16[8,2,64,96]{3,2,1,0:T(8,128)(2,1)} %copy.56), calls=%async_computation.3 | async-start | bytes 524288 | tf_op jit(solution)/shard_map/all_to_all | solution.py:73
Sparse Core Ops, SparseCore 0:
  72.7 73.9 all-gather.9
  149.3 36.5 all-gather.7

commit v2 on v1

--- a/solution.py
+++ b/solution.py
@@ -41,7 +41,6 @@
     down_weight,
 ):
     core = lax.axis_index("c")
-    half = lax.axis_index("yh")
     n_rows, n_z = lax.axis_size(ROWS), lax.axis_size("z")
     per = grad_out.shape[0]
     runs = n_z * 2 // n_rows
@@ -67,14 +66,29 @@
 
     def scatter_rows(own, other):
         width = own.shape[1]
-        sent = jnp.stack(
-            [own.reshape(n_rows, -1, width), other.reshape(n_rows, -1, width)], axis=1
-        )
+        sent = jnp.stack([by_row(own), by_row(other)], axis=1)
         came = lax.all_to_all(sent, ROWS, 0, 0, tiled=True)
         return jnp.sum(came.astype(jnp.float32), axis=0).reshape(-1, width)
 
+    def by_row(block):
+        width = block.shape[1]
+        parts = block.reshape(n_rows // 2, runs, 2, per, width)
+        return parts.transpose(2, 0, 1, 3, 4).reshape(n_rows, runs * per, width)
+
+    def by_z(block):
+        width = block.shape[-1]
+        parts = block.reshape(2, n_z, per, width)
+        return jnp.swapaxes(parts, 0, 1).reshape(-1, width)
+
     def gather_z(pair):
-        return lax.all_gather(pair, "z", axis=1).reshape(-1, features)
+        return lax.all_gather(pair.reshape(-1, features), "z", axis=0, tiled=True)
+
+    def gather_rows(block):
+        copies = lax.optimization_barrier(
+            jnp.broadcast_to(block[None], (n_rows,) + block.shape)
+        )
+        every = lax.all_to_all(copies, ROWS, 0, 0, tiled=True)
+        return every.reshape(n_rows, 2, -1, block.shape[1])
 
     stream = restore(stream_code, stream_scale)
     positive = jnp.maximum(
@@ -82,10 +96,8 @@
     )
     act = (positive * positive).astype(jnp.bfloat16)
     context = own_first(restore(ctx_code, ctx_scale))
-    hidden_width, ctx_width = act.shape[1], context.shape[1]
-    padding = jnp.zeros((act.shape[0], 512 - hidden_width - ctx_width), jnp.bfloat16)
-    saved = jnp.concatenate([act, context, padding], axis=1)
-    saved_all = lax.all_gather(saved, ROWS, axis=0)
+    hidden_width = act.shape[1]
+    saved = jnp.concatenate([act, context], axis=1)
 
     both = lax.all_gather(jnp.stack([grad_out, stream]), "yh", axis=0)
     stream_all = lax.all_gather(both[:, 1], ("z", "c"), axis=0)
@@ -97,25 +109,23 @@
         dot_nt(grad_other, down_weight).astype(jnp.bfloat16),
     )
     grad_pre = (grad_act * 2.0 * positive).astype(jnp.bfloat16)
-    copies = lax.optimization_barrier(
-        jnp.broadcast_to(grad_pre[None], (n_rows,) + grad_pre.shape)
-    )
-    grad_pre_all = lax.all_to_all(copies, ROWS, 0, 0, tiled=True).reshape(
-        n_rows, 2, -1, hidden_width
-    )
-    pre_own = grad_pre_all[:, 0].reshape(-1, hidden_width)
-    pre_other = grad_pre_all[:, 1].reshape(-1, hidden_width)
+    grad_pre_all = gather_rows(grad_pre)
+    pre_own = by_z(grad_pre_all[:, 0])
+    pre_other = by_z(grad_pre_all[:, 1])
 
     came = swap(dot_nt(pre_other, up_weight).astype(jnp.bfloat16), "c")
-    part = (dot_nt(pre_own, up_weight) + came.astype(jnp.float32)).reshape(2, -1, features)
-    keep = lax.dynamic_index_in_dim(part, half, 0, keepdims=False)
-    send = lax.dynamic_index_in_dim(part, 1 - half, 0, keepdims=False).astype(jnp.bfloat16)
-    part = (keep + swap(send, "yh").astype(jnp.float32)).astype(jnp.bfloat16)
-    came = lax.all_to_all(part.reshape(n_z, per, features), "z", 0, 0, tiled=True)
-    summed = jnp.sum(came.astype(jnp.float32), axis=0)
-    grad_stream = (grad_out.astype(jnp.float32) + summed).astype(jnp.bfloat16)
+    part = (dot_nt(pre_own, up_weight) + came.astype(jnp.float32)).astype(jnp.bfloat16)
+    part, saved = lax.optimization_barrier((part, saved))
+    saved_all = lax.all_gather(saved, ROWS, axis=0)
+    came = lax.all_to_all(part.reshape(n_z, 2 * per, features), "z", 0, 0, tiled=True)
+    came, saved_all = lax.optimization_barrier((came, saved_all))
+    part = jnp.sum(came.astype(jnp.float32), axis=0).astype(jnp.bfloat16)
+    summed = part.astype(jnp.float32) + swap(part, "yh").astype(jnp.float32)
+    pair_out = both[:, 0].reshape(2 * per, features).astype(jnp.float32)
+    grad_stream = (pair_out + summed).astype(jnp.bfloat16)
 
-    gs_own = gather_z(lax.all_gather(grad_stream, "yh", axis=0))
+    gs_own = gather_z(grad_stream)
+    stream_all, gs_late = lax.optimization_barrier((stream_all, gs_own))
     gs_other = swap(gs_own, "c")
     grad_ctx = natural(
         scatter_rows(
@@ -124,20 +134,20 @@
         )
     ).astype(jnp.bfloat16)
 
-    saved_own = saved_all.reshape(n_rows, 2, -1, 512)[:, 0].reshape(-1, 512)
-    saved_other = saved_all.reshape(n_rows, 2, -1, 512)[:, 1].reshape(-1, 512)
+    saved_pairs = saved_all.reshape(n_rows, 2, -1, saved_all.shape[-1])
+    saved_own, saved_other = by_z(saved_pairs[:, 0]), by_z(saved_pairs[:, 1])
     act_own, act_other = saved_own[:, :hidden_width], saved_other[:, :hidden_width]
-    ctx_own = saved_own[:, hidden_width : hidden_width + ctx_width]
-    ctx_other = saved_other[:, hidden_width : hidden_width + ctx_width]
-    by_core = stream_all.reshape(n_z, 2, 2, per, features)
+    ctx_own = saved_own[:, hidden_width:]
+    ctx_other = saved_other[:, hidden_width:]
+    by_core = stream_all.reshape(n_z, 2, 2 * per, features)
     stream_own = lax.dynamic_index_in_dim(by_core, core, 1, keepdims=False)
     stream_other = lax.dynamic_index_in_dim(by_core, 1 - core, 1, keepdims=False)
-    stream_own = jnp.swapaxes(stream_own, 0, 1).reshape(-1, features)
-    stream_other = jnp.swapaxes(stream_other, 0, 1).reshape(-1, features)
+    stream_own = stream_own.reshape(-1, features)
+    stream_other = stream_other.reshape(-1, features)
 
     grad_down = dot_tn(act_own, grad_own) + dot_tn(act_other, grad_other)
     grad_up = dot_tn(stream_own, pre_own) + dot_tn(stream_other, pre_other)
-    grad_outw = dot_tn(ctx_own, gs_own) + dot_tn(ctx_other, gs_other)
+    grad_outw = dot_tn(ctx_own, gs_late) + dot_tn(ctx_other, gs_other)
     return (grad_ctx, grad_outw, grad_up, grad_down)
 
 

time: 262 us -> 225 us (0.86)
  waiting for transfers between devices: 84.1 us -> 29.5 us
  blocking collectives: 86 us -> 112 us
  starting transfers between devices: 50.5 us -> 44.6 us
    all_gather x1 -> x0, waiting for transfers between devices: 35.4 us -> none  [local(): saved_all = lax.all_gather(saved, ROWS, axis=0)]
    all_gather x3, blocking collectives: 66.3 us -> 92.8 us  [the longest x2 67.1 us: gather_z(): return lax.all_gather(pair.reshape(-1, features), 'z', axis=0, tiled=True)]
    all_gather x1, waiting for transfers between devices: 20.6 us -> 0.02 us  [local(): stream_all = lax.all_gather(both[:, 1], ('z', 'c'), axis=0)]
    all_to_all x1, waiting for transfers between devices: 0.01 us -> 9.51 us  [local(): lax.all_to_all(part.reshape(n_z, 2 * per, features), 'z', 0, 0, tiled=True)]
    ppermute x4, waiting for transfers between devices: 11.7 us -> 2.85 us  [swap(): return lax.ppermute(block, axis, SWAP)]
    ppermute x4, starting transfers between devices: 35.6 us -> 29.8 us  [swap(): return lax.ppermute(block, axis, SWAP)]
  transfers between devices with their start and end apart: 9 -> 8, of which waited for: 7 -> 5; matrix products, arithmetic and copies ran while one was open for 7% -> 5% of each run, Pallas kernels for 0% -> 0%
where the time goes in v2:
time: 225 us; the launch traced here: 224 us
  blocking collectives  112 us (50%)
  starting transfers between devices  44.6 us (20%)
  waiting for transfers between devices  29.5 us (13%)
  between operations  14.5 us (6%)
  matrix products  11.1 us (5%)
  local copies, waits for them, and re-layouts  8.59 us (4%)
  other arithmetic  3.37 us (1%)
    all_gather x2, blocking collectives, gather_z(): return lax.all_gather(pair.reshape(-1, features), 'z', axis=0, tiled=True)  67.1 us
    ppermute x4, starting transfers between devices, swap(): return lax.ppermute(block, axis, SWAP)  29.8 us
    all_gather x1, blocking collectives, local(): saved_all = lax.all_gather(saved, ROWS, axis=0)  25.7 us
    all_to_all x2, waiting for transfers between devices, scatter_rows(): came = lax.all_to_all(sent, ROWS, 0, 0, tiled=True)  16.4 us
    all_to_all x1, blocking collectives, gather_rows(): every = lax.all_to_all(copies, ROWS, 0, 0, tiled=True)  13.8 us
    all_to_all x1, waiting for transfers between devices, local(): lax.all_to_all(part.reshape(n_z, 2 * per, features), 'z', 0, 0, tiled=True)  9.51 us
    all_to_all x2, starting transfers between devices, scatter_rows(): came = lax.all_to_all(sent, ROWS, 0, 0, tiled=True)  8.57 us
    dot_general x6, matrix products, dot_tn(): lax.dot_general(left, right, (((0,), (0,)), ((), ())), preferred_element_...  7.15 us
  transfers between devices with their start and end apart: 8, of which 5 were waited for; matrix products, arithmetic and copies ran while one was open for 5% of the time, Pallas kernels for 0%

profile of v2, /device:TPU:1, one launch (start us, length us, event | category | flops | bytes accessed | tf_op | source)
XLA Modules:
  0.0 224.2 jit_solution(11678068676405005468)
XLA Ops:
  7.2 0.9 mul.56
  8.2 0.7 fusion.10
  9.0 0.7 pad_maximum_fusion.3
  9.7 5.9 %all-gather = bf16[4,16,768]{2,1,0:T(8,128)(2,1)S(1)} all-gather(bf16[2,16,768]{2,1,0:T(8,128)(2,1)S(1)} %pad_maximum_fusion.3), channel_id=2, replica_groups=mesh['x'=4,'yl'=2,'yh'=2,'z'=16,'c'=2] {'yh'}, dimensions={0}, use_global_device_ids=true | all-gather | bytes 147456 | tf_op jit(solution)/shard_map/all_gather | solution.py:102
  16.2 33.2 %all_gather.23 = bf16[512,768]{1,0:T(8,128)(2,1)S(1)} all-gather(bf16[32,768]{1,0:T(8,128)(2,1)S(1)} %bitcast.120), channel_id=1, replica_groups=mesh['x'=4,'yl'=2,'yh'=2,'z'=16,'c'=2] {'z'}, dimensions={0}, use_global_device_ids=true | all-gather | bytes 835584 | tf_op jit(solution)/shard_map/all_gather | solution.py:84
  49.4 10.8 %collective-permute-start = (bf16[512,768]{1,0:T(8,128)(2,1)S(1)}, bf16[512,768]{1,0:T(8,128)(2,1)S(1)}, u32[]{:S(2)}, u32[]{:S(2)}) collective-permute-start(bf16[512,768]{1,0:T(8,128)(2,1)S(1)} %all_gather.23), channel_id=1, source_target_pairs={{0,1},{1,0},{2,3},{3,2},{4,5},{5,4},{6,7},{7,6},{8,9},{9,8},{10,11... | collective-permute-start | bytes 2359304 | tf_op jit(solution)/shard_map/ppermute | solution.py:65
  60.9 1.2 collective-permute-done
  63.2 1.0 copy.70
  64.2 5.2 %all-to-all-start = ((bf16[8,2,64,384]{3,2,1,0:T(8,128)(2,1)}), bf16[8,2,64,384]{3,2,1,0:T(8,128)(2,1)S(1)}, u32[]{:S(2)}, u32[]{:S(2)}) async-start(bf16[8,2,64,384]{3,2,1,0:T(8,128)(2,1)} %copy.70), calls=%async_computation | async-start | bytes 1572864 | tf_op jit(solution)/shard_map/all_to_all | solution.py:70
  69.7 11.6 %all-to-all-done = bf16[8,2,64,384]{3,2,1,0:T(8,128)(2,1)S(1)} async-done(((bf16[8,2,64,384]{3,2,1,0:T(8,128)(2,1)}), bf16[8,2,64,384]{3,2,1,0:T(8,128)(2,1)S(1)}, u32[]{:S(2)}, u32[]{:S(2)}) %all-to-all-start) | async-done | bytes 786464 | tf_op jit(solution)/shard_map/all_to_all | solution.py:70
  82.1 13.8 %all_to_all.20 = bf16[8,128,384]{2,1,0:T(8,128)(2,1)S(1)} all-to-all(bf16[8,128,384]{2,1,0:T(8,128)(2,1)S(1)} %broadcast_in_dim.2), channel_id=1, replica_groups=mesh['x'=4,'yl'=2,'yh'=2,'z'=16,'c'=2] {'x','yl'}, dimensions={0} | all-to-all | bytes 1572864 | tf_op jit(solution)/shard_map/all_to_all | solution.py:90
  96.8 4.6 %collective-permute-start.1 = (bf16[512,768]{1,0:T(8,128)(2,1)S(1)}, bf16[512,768]{1,0:T(8,128)(2,1)S(1)}, u32[]{:S(2)}, u32[]{:S(2)}) collective-permute-start(bf16[512,768]{1,0:T(8,128)(2,1)S(1)} %convolution_convert_fusion), channel_id=1, source_target_pairs={{0,1},{1,0},{2,3},{3,2},{4,5},{5,4},{6,7},{7,6},{8,9},{9,8},{10,11... | collective-permute-start | bytes 2359304 | tf_op jit(solution)/shard_map/ppermute | solution.py:65
  101.7 1.6 collective-permute-done.1
  103.3 1.5 add_convert_fusion
  104.8 6.2 %all-to-all-start.2 = ((bf16[16,32,768]{2,1,0:T(8,128)(2,1)}), bf16[16,32,768]{2,1,0:T(8,128)(2,1)S(1)}, u32[]{:S(2)}, u32[]{:S(2)}) async-start(bf16[16,32,768]{2,1,0:T(8,128)(2,1)} %bitcast.28), calls=%async_computation.2 | async-start | bytes 1572864 | tf_op jit(solution)/shard_map/all_to_all | solution.py:120
  111.0 0.7 all-gather.5.cloned.1.call-update
  111.7 25.7 %all-gather.1 = bf16[1024,480]{1,0:T(8,128)(2,1)S(1)} all-gather(bf16[128,480]{1,0:T(8,128)(2,1)S(1)} %pad_maximum_fusion.2), channel_id=3, replica_groups=mesh['x'=4,'yl'=2,'yh'=2,'z'=16,'c'=2] {'x','yl'}, dimensions={0}, use_global_device_ids=true | all-gather | bytes 1105920 | tf_op jit(solution)/shard_map/all_gather | solution.py:119
  137.4 9.5 %all-to-all-done.2 = bf16[16,32,768]{2,1,0:T(8,128)(2,1)S(1)} async-done(((bf16[16,32,768]{2,1,0:T(8,128)(2,1)}), bf16[16,32,768]{2,1,0:T(8,128)(2,1)S(1)}, u32[]{:S(2)}, u32[]{:S(2)}) %all-to-all-start.2) | async-done | bytes 786464 | tf_op jit(solution)/shard_map/all_to_all | solution.py:120
  147.0 0.9 copy.83
  147.9 0.7 reduce_sum.31
  148.6 4.5 %collective-permute-start.2 = (bf16[32,768]{1,0:T(8,128)(2,1)}, bf16[32,768]{1,0:T(8,128)(2,1)S(1)}, u32[]{:S(2)}, u32[]{:S(2)}) collective-permute-start(bf16[32,768]{1,0:T(8,128)(2,1)} %reduce_sum.31), channel_id=1, source_target_pairs={{0,32},{32,0},{1,33},{33,1},{2,34},{34,2},{3,35},{35,3},{4,36},{36... | collective-permute-start | bytes 147464 | tf_op jit(solution)/shard_map/ppermute | solution.py:65
  154.4 1.5 convolution_add_fusion
  155.9 33.9 %all_gather.26 = bf16[512,768]{1,0:T(8,128)(2,1)S(1)} all-gather(bf16[32,768]{1,0:T(8,128)(2,1)S(1)} %add_convert_fusion.1), channel_id=1, replica_groups=mesh['x'=4,'yl'=2,'yh'=2,'z'=16,'c'=2] {'z'}, dimensions={0}, use_global_device_ids=true | all-gather | bytes 835584 | tf_op jit(solution)/shard_map/all_gather | solution.py:84
  189.9 9.8 %collective-permute-start.3 = (bf16[512,768]{1,0:T(8,128)(2,1)S(1)}, bf16[512,768]{1,0:T(8,128)(2,1)S(1)}, u32[]{:S(2)}, u32[]{:S(2)}) collective-permute-start(bf16[512,768]{1,0:T(8,128)(2,1)S(1)} %all_gather.26), channel_id=1, source_target_pairs={{0,1},{1,0},{2,3},{3,2},{4,5},{5,4},{6,7},{7,6},{8,9},{9,8},{10,11... | collective-permute-start | bytes 2359304 | tf_op jit(solution)/shard_map/ppermute | solution.py:65
  199.8 1.0 fusion.7
  201.3 1.5 constant_dynamic-slice_fusion
  203.4 1.6 convolution_add_fusion.1
  205.6 0.7 copy.80
  206.4 3.4 %all-to-all-start.3 = ((bf16[8,2,64,96]{3,2,1,0:T(8,128)(2,1)}), bf16[8,2,64,96]{3,2,1,0:T(8,128)(2,1)S(1)}, u32[]{:S(2)}, u32[]{:S(2)}) async-start(bf16[8,2,64,96]{3,2,1,0:T(8,128)(2,1)} %copy.80), calls=%async_computation.3 | async-start | bytes 524288 | tf_op jit(solution)/shard_map/all_to_all | solution.py:70
  209.8 1.9 convolution_add_fusion.2
  211.7 4.8 %all-to-all-done.3 = bf16[8,2,64,96]{3,2,1,0:T(8,128)(2,1)S(1)} async-done(((bf16[8,2,64,96]{3,2,1,0:T(8,128)(2,1)}), bf16[8,2,64,96]{3,2,1,0:T(8,128)(2,1)S(1)}, u32[]{:S(2)}, u32[]{:S(2)}) %all-to-all-start.3) | async-done | bytes 196640 | tf_op jit(solution)/shard_map/all_to_all | solution.py:70
  216.7 0.7 copy.84
  (77 shorter events, 7.8 us)
Async XLA Ops:
  7.2 89.0 %copy-start = (bf16[768,384]{1,0:T(8,128)(2,1)S(1)}, bf16[768,384]{1,0:T(8,128)(2,1)}, u32[]{:S(2)}) copy-start(bf16[768,384]{1,0:T(8,128)(2,1)} %param.18) | copy-start | bytes 1769476
  7.2 53.1 %copy-start.15 = (bf16[384,768]{1,0:T(8,128)(2,1)S(1)}, bf16[384,768]{1,0:T(8,128)(2,1)}, u32[]{:S(2)}) copy-start(bf16[384,768]{1,0:T(8,128)(2,1)} %param.19) | copy-start | bytes 1769476
  49.4 11.5 %copy-start.1 = (bf16[512,768]{1,0:T(8,128)(2,1)}, bf16[512,768]{1,0:T(8,128)(2,1)S(1)}, u32[]{:S(2)}) copy-start(bf16[512,768]{1,0:T(8,128)(2,1)S(1)} %all_gather.23) | copy-start | bytes 2359300
  49.4 12.7 %collective-permute-start = (bf16[512,768]{1,0:T(8,128)(2,1)S(1)}, bf16[512,768]{1,0:T(8,128)(2,1)S(1)}, u32[]{:S(2)}, u32[]{:S(2)}) collective-permute-start(bf16[512,768]{1,0:T(8,128)(2,1)S(1)} %all_gather.23), channel_id=1, source_target_pairs={{0,1},{1,0},{2,3},{3,2},{4,5},{5,4},{6,7},{7,6},{8,9},{9,8},{10,11... | collective-permute-start | bytes 2359304 | tf_op jit(solution)/shard_map/ppermute | solution.py:65
  62.1 0.9 copy-start.5
  64.2 5.2 %copy-start.11 = (bf16[128,384]{1,0:T(8,128)(2,1)S(1)}, bf16[128,384]{1,0:T(8,128)(2,1)}, u32[]{:S(2)}) copy-start(bf16[128,384]{1,0:T(8,128)(2,1)} %param.15) | copy-start | bytes 294916
  64.2 5.3 %copy-start.13 = (f32[128,12]{0,1:T(8,128)S(1)}, f32[128,12]{0,1:T(8,128)}, u32[]{:S(2)}) copy-start(f32[128,12]{0,1:T(8,128)} %param.16) | copy-start | bytes 18436
  64.2 17.1 %all-to-all-start = ((bf16[8,2,64,384]{3,2,1,0:T(8,128)(2,1)}), bf16[8,2,64,384]{3,2,1,0:T(8,128)(2,1)S(1)}, u32[]{:S(2)}, u32[]{:S(2)}) async-start(bf16[8,2,64,384]{3,2,1,0:T(8,128)(2,1)} %copy.70), calls=%async_computation | async-start | bytes 1572864 | tf_op jit(solution)/shard_map/all_to_all | solution.py:70
  96.1 5.3 %copy-start.12 = (bf16[128,96]{0,1:T(8,128)(2,1)S(1)}, bf16[128,96]{0,1:T(8,128)(2,1)}, u32[]{:S(2)}) copy-start(bf16[128,96]{0,1:T(8,128)(2,1)} %param.11) | copy-start | bytes 73732
  96.1 5.3 %copy-start.14 = (f32[128,3]{0,1:T(4,128)S(1)}, f32[128,3]{0,1:T(4,128)}, u32[]{:S(2)}) copy-start(f32[128,3]{0,1:T(4,128)} %param.12) | copy-start | bytes 4612
  96.1 5.4 %copy-start.9 = (bf16[128,384]{1,0:T(8,128)(2,1)S(1)}, bf16[128,384]{1,0:T(8,128)(2,1)}, u32[]{:S(2)}) copy-start(bf16[128,384]{1,0:T(8,128)(2,1)} %get-tuple-element.38) | copy-start | bytes 294916
  96.8 6.5 %collective-permute-start.1 = (bf16[512,768]{1,0:T(8,128)(2,1)S(1)}, bf16[512,768]{1,0:T(8,128)(2,1)S(1)}, u32[]{:S(2)}, u32[]{:S(2)}) collective-permute-start(bf16[512,768]{1,0:T(8,128)(2,1)S(1)} %convolution_convert_fusion), channel_id=1, source_target_pairs={{0,1},{1,0},{2,3},{3,2},{4,5},{5,4},{6,7},{7,6},{8,9},{9,8},{10,11... | collective-permute-start | bytes 2359304 | tf_op jit(solution)/shard_map/ppermute | solution.py:65
  104.8 42.1 %all-to-all-start.2 = ((bf16[16,32,768]{2,1,0:T(8,128)(2,1)}), bf16[16,32,768]{2,1,0:T(8,128)(2,1)S(1)}, u32[]{:S(2)}, u32[]{:S(2)}) async-start(bf16[16,32,768]{2,1,0:T(8,128)(2,1)} %bitcast.28), calls=%async_computation.2 | async-start | bytes 1572864 | tf_op jit(solution)/shard_map/all_to_all | solution.py:120
  111.0 88.8 %all-gather.5.cloned.1.call-start = ((), (), s32[]{:S(2)}) async-start(), calls=%async_computation.4 | async-start | bytes 1622016 | tf_op jit(solution)/shard_map/all_gather | solution.py:103
  147.8 5.2 %copy-start.2 = (bf16[512,768]{1,0:T(8,128)(2,1)S(1)}, bf16[512,768]{1,0:T(8,128)(2,1)}, u32[]{:S(2)}) copy-start(bf16[512,768]{1,0:T(8,128)(2,1)} %copy-done.1) | copy-start | bytes 2359300
  148.6 7.3 %collective-permute-start.2 = (bf16[32,768]{1,0:T(8,128)(2,1)}, bf16[32,768]{1,0:T(8,128)(2,1)S(1)}, u32[]{:S(2)}, u32[]{:S(2)}) collective-permute-start(bf16[32,768]{1,0:T(8,128)(2,1)} %reduce_sum.31), channel_id=1, source_target_pairs={{0,32},{32,0},{1,33},{33,1},{2,34},{34,2},{3,35},{35,3},{4,36},{36... | collective-permute-start | bytes 147464 | tf_op jit(solution)/shard_map/ppermute | solution.py:65
  153.1 1.0 copy-start.3
  153.1 1.3 copy-start.6
  154.4 1.5 copy-start.10
  189.9 15.1 %collective-permute-start.3 = (bf16[512,768]{1,0:T(8,128)(2,1)S(1)}, bf16[512,768]{1,0:T(8,128)(2,1)S(1)}, u32[]{:S(2)}, u32[]{:S(2)}) collective-permute-start(bf16[512,768]{1,0:T(8,128)(2,1)S(1)} %all_gather.26), channel_id=1, source_target_pairs={{0,1},{1,0},{2,3},{3,2},{4,5},{5,4},{6,7},{7,6},{8,9},{9,8},{10,11... | collective-permute-start | bytes 2359304 | tf_op jit(solution)/shard_map/ppermute | solution.py:65
  199.8 1.0 copy-start.7
  203.4 1.6 copy-start.8
  205.4 4.4 %copy-start.4 = (f32[96,768]{1,0:T(8,128)S(1)}, f32[96,768]{1,0:T(8,128)}, u32[]{:S(2)}) copy-start(f32[96,768]{1,0:T(8,128)} %fusion.7) | copy-start | bytes 884740
  206.4 10.2 %all-to-all-start.3 = ((bf16[8,2,64,96]{3,2,1,0:T(8,128)(2,1)}), bf16[8,2,64,96]{3,2,1,0:T(8,128)(2,1)S(1)}, u32[]{:S(2)}, u32[]{:S(2)}) async-start(bf16[8,2,64,96]{3,2,1,0:T(8,128)(2,1)} %copy.80), calls=%async_computation.3 | async-start | bytes 524288 | tf_op jit(solution)/shard_map/all_to_all | solution.py:70
Sparse Core Ops, SparseCore 0:
  114.0 78.1 all-gather.4

commit v3 on v2

--- a/solution.py
+++ b/solution.py
@@ -97,35 +97,59 @@
     act = (positive * positive).astype(jnp.bfloat16)
     context = own_first(restore(ctx_code, ctx_scale))
     hidden_width = act.shape[1]
-    saved = jnp.concatenate([act, context], axis=1)
+    padding = jnp.zeros((act.shape[0], 512 - hidden_width - context.shape[1]), jnp.bfloat16)
+    saved = jnp.concatenate([act, context, padding], axis=1)
 
     both = lax.all_gather(jnp.stack([grad_out, stream]), "yh", axis=0)
     stream_all = lax.all_gather(both[:, 1], ("z", "c"), axis=0)
-    grad_own = gather_z(both[:, 0])
-    grad_other = swap(grad_own, "c")
 
-    grad_act = scatter_rows(
-        dot_nt(grad_own, down_weight).astype(jnp.bfloat16),
-        dot_nt(grad_other, down_weight).astype(jnp.bfloat16),
-    )
-    grad_pre = (grad_act * 2.0 * positive).astype(jnp.bfloat16)
-    grad_pre_all = gather_rows(grad_pre)
+    def first_half(pair):
+        grad_own = gather_z(pair)
+        grad_other = swap(grad_own, "c")
+        grad_act = scatter_rows(
+            dot_nt(grad_own, down_weight).astype(jnp.bfloat16),
+            dot_nt(grad_other, down_weight).astype(jnp.bfloat16),
+        )
+        grad_pre = (grad_act * 2.0 * positive).astype(jnp.bfloat16)
+        return grad_own, grad_other, gather_rows(grad_pre)
+
+    def skip(pair):
+        wide = jnp.zeros((n_z * 2 * per, features), jnp.bfloat16)
+        return wide, wide, jnp.zeros((n_rows, 2, runs * per, hidden_width), jnp.bfloat16)
+
+    always = lax.optimization_barrier(jnp.bool_(True))
+    grad_own, grad_other, grad_pre_all = lax.cond(always, first_half, skip, both[:, 0])
     pre_own = by_z(grad_pre_all[:, 0])
     pre_other = by_z(grad_pre_all[:, 1])
 
     came = swap(dot_nt(pre_other, up_weight).astype(jnp.bfloat16), "c")
     part = (dot_nt(pre_own, up_weight) + came.astype(jnp.float32)).astype(jnp.bfloat16)
-    part, saved = lax.optimization_barrier((part, saved))
+    pair_out = both[:, 0].reshape(2 * per, features).astype(jnp.float32)
+    by_core = stream_all.reshape(n_z, 2, 2 * per, features)
+    part, saved, by_core = lax.optimization_barrier((part, saved, by_core))
     saved_all = lax.all_gather(saved, ROWS, axis=0)
-    came = lax.all_to_all(part.reshape(n_z, 2 * per, features), "z", 0, 0, tiled=True)
-    came, saved_all = lax.optimization_barrier((came, saved_all))
-    part = jnp.sum(came.astype(jnp.float32), axis=0).astype(jnp.bfloat16)
-    summed = part.astype(jnp.float32) + swap(part, "yh").astype(jnp.float32)
-    pair_out = both[:, 0].reshape(2 * per, features).astype(jnp.float32)
-    grad_stream = (pair_out + summed).astype(jnp.bfloat16)
+
+    def second_half(part, by_core):
+        came = lax.all_to_all(part.reshape(n_z, 2 * per, features), "z", 0, 0, tiled=True)
+        stream_own = lax.dynamic_index_in_dim(by_core, core, 1, keepdims=False)
+        stream_other = lax.dynamic_index_in_dim(by_core, 1 - core, 1, keepdims=False)
+        stream_own = stream_own.reshape(-1, features)
+        stream_other = stream_other.reshape(-1, features)
+        grad_up = dot_tn(stream_own, pre_own) + dot_tn(stream_other, pre_other)
+        part = jnp.sum(came.astype(jnp.float32), axis=0).astype(jnp.bfloat16)
+        summed = part.astype(jnp.float32) + swap(part, "yh").astype(jnp.float32)
+        return (pair_out + summed).astype(jnp.bfloat16), grad_up
+
+    def skip_second(part, by_core):
+        return (
+            jnp.zeros((2 * per, features), jnp.bfloat16),
+            jnp.zeros((features, hidden_width), jnp.float32),
+        )
+
+    grad_stream, grad_up = lax.cond(always, second_half, skip_second, part, by_core)
+    grad_stream, saved_all = lax.optimization_barrier((grad_stream, saved_all))
 
     gs_own = gather_z(grad_stream)
-    stream_all, gs_late = lax.optimization_barrier((stream_all, gs_own))
     gs_other = swap(gs_own, "c")
     grad_ctx = natural(
         scatter_rows(
@@ -137,17 +161,10 @@
     saved_pairs = saved_all.reshape(n_rows, 2, -1, saved_all.shape[-1])
     saved_own, saved_other = by_z(saved_pairs[:, 0]), by_z(saved_pairs[:, 1])
     act_own, act_other = saved_own[:, :hidden_width], saved_other[:, :hidden_width]
-    ctx_own = saved_own[:, hidden_width:]
-    ctx_other = saved_other[:, hidden_width:]
-    by_core = stream_all.reshape(n_z, 2, 2 * per, features)
-    stream_own = lax.dynamic_index_in_dim(by_core, core, 1, keepdims=False)
-    stream_other = lax.dynamic_index_in_dim(by_core, 1 - core, 1, keepdims=False)
-    stream_own = stream_own.reshape(-1, features)
-    stream_other = stream_other.reshape(-1, features)
-
+    ctx_own = saved_own[:, hidden_width : hidden_width + context.shape[1]]
+    ctx_other = saved_other[:, hidden_width : hidden_width + context.shape[1]]
     grad_down = dot_tn(act_own, grad_own) + dot_tn(act_other, grad_other)
-    grad_up = dot_tn(stream_own, pre_own) + dot_tn(stream_other, pre_other)
-    grad_outw = dot_tn(ctx_own, gs_late) + dot_tn(ctx_other, gs_other)
+    grad_outw = dot_tn(ctx_own, gs_own) + dot_tn(ctx_other, gs_other)
     return (grad_ctx, grad_outw, grad_up, grad_down)
 
 

time: 225 us -> 229 us (1.018)
  blocking collectives: 112 us -> 101 us
  waiting for transfers between devices: 29.5 us -> 39.2 us
  local copies, waits for them, and re-layouts: 8.59 us -> 14 us
    all_gather x1 -> x0, blocking collectives: 25.7 us -> none  [local(): saved_all = lax.all_gather(saved, ROWS, axis=0)]
    all_to_all x1, waiting for transfers between devices: 9.51 us -> 31.3 us  [second_half(): lax.all_to_all(part.reshape(n_z, 2 * per, features), 'z', 0, 0, tiled=True)]
    all_to_all x0 -> x1, blocking collectives: none -> 16.3 us  [scatter_rows(): came = lax.all_to_all(sent, ROWS, 0, 0, tiled=True)]
    all_to_all x2 -> x1, waiting for transfers between devices: 16.4 us -> 5.75 us  [scatter_rows(): came = lax.all_to_all(sent, ROWS, 0, 0, tiled=True)]
    all_to_all x2 -> x1, starting transfers between devices: 8.57 us -> 3.41 us  [scatter_rows(): came = lax.all_to_all(sent, ROWS, 0, 0, tiled=True)]
    ppermute x4, starting transfers between devices: 29.8 us -> 34.4 us  [swap(): return lax.ppermute(block, axis, SWAP)]
    all_gather x2, blocking collectives: 67.1 us -> 64.3 us  [gather_z(): return lax.all_gather(pair.reshape(-1, features), 'z', axis=0, tiled=True)]
  transfers between devices with their start and end apart: 8 -> 8, of which waited for: 5 -> 4; matrix products, arithmetic and copies ran while one was open for 5% -> 9% of each run, Pallas kernels for 0% -> 0%
where the time goes in v3:
time: 229 us; the launch traced here: 228 us
  blocking collectives  101 us (44%)
  starting transfers between devices  43.3 us (19%)
  waiting for transfers between devices  39.2 us (17%)
  between operations  14.4 us (6%)
  local copies, waits for them, and re-layouts  14 us (6%)
  matrix products  12.9 us (6%)
  other arithmetic  2.8 us (1%)
    all_gather x2, blocking collectives, gather_z(): return lax.all_gather(pair.reshape(-1, features), 'z', axis=0, tiled=True)  64.3 us
    ppermute x4, starting transfers between devices, swap(): return lax.ppermute(block, axis, SWAP)  34.4 us
    all_to_all x1, waiting for transfers between devices, second_half(): lax.all_to_all(part.reshape(n_z, 2 * per, features), 'z', 0, 0, tiled=True)  31.3 us
    all_to_all x1, blocking collectives, scatter_rows(): came = lax.all_to_all(sent, ROWS, 0, 0, tiled=True)  16.3 us
    all_to_all x1, blocking collectives, gather_rows(): every = lax.all_to_all(copies, ROWS, 0, 0, tiled=True)  14.3 us
    dot_general x6, matrix products, dot_tn(): lax.dot_general(left, right, (((0,), (0,)), ((), ())), preferred_element_...  8.28 us
    all_gather x1, blocking collectives, local(): both = lax.all_gather(jnp.stack([grad_out, stream]), 'yh', axis=0)  5.86 us
    all_to_all x1, waiting for transfers between devices, scatter_rows(): came = lax.all_to_all(sent, ROWS, 0, 0, tiled=True)  5.75 us
  transfers between devices with their start and end apart: 8, of which 4 were waited for; matrix products, arithmetic and copies ran while one was open for 9% of the time, Pallas kernels for 0%

profile of v3, /device:TPU:1, one launch (start us, length us, event | category | flops | bytes accessed | tf_op | source)
XLA Modules:
  0.0 227.6 jit_solution(3019230595481294953)
XLA Ops:
  7.2 0.9 mul.45
  8.3 0.7 fusion.10
  9.0 0.7 pad_maximum_fusion.2
  9.7 5.9 %all-gather = bf16[4,16,768]{2,1,0:T(8,128)(2,1)S(1)} all-gather(bf16[2,16,768]{2,1,0:T(8,128)(2,1)S(1)} %pad_maximum_fusion.2), channel_id=2, replica_groups=mesh['x'=4,'yl'=2,'yh'=2,'z'=16,'c'=2] {'yh'}, dimensions={0}, use_global_device_ids=true | all-gather | bytes 147456 | tf_op jit(solution)/shard_map/all_gather | solution.py:103
  16.3 1.0 copy.85
  17.6 78.8 %conditional.2 = (bf16[512,768]{1,0:T(8,128)(2,1)}, bf16[512,768]{1,0:T(8,128)(2,1)}, bf16[8,2,64,384]{3,2,1,0:T(8,128)(2,1)S(1)}) conditional(s32[]{:T(128)} %convert_element_type.81, () %tuple.27, (bf16[2,1,16,768]{3,2,1,0:T(8,128)(2,1)S(1)}, bf16[384,768]{1,0:T(8,128)(2,1)S(1)}, f32[128,384]{1,0:T(8,128)S(1)}) %tuple.55), branch_computations={%region_0.1_spmd, %region_1.3_spmd} | conditional | flops 605650944 | bytes 24428664 | solution.py:121
  17.6 34.4 %all_gather.14 = bf16[512,768]{1,0:T(8,128)(2,1)S(1)} all-gather(bf16[32,768]{1,0:T(8,128)(2,1)S(1)} %bitcast.131), channel_id=1, replica_groups=mesh['x'=4,'yl'=2,'yh'=2,'z'=16,'c'=2] {'z'}, dimensions={0}, use_global_device_ids=true | all-gather | bytes 835584 | tf_op jit(solution)/shard_map/cond/branch_1_fun/all_gather | solution.py:84
  51.9 10.6 %collective-permute-start = (bf16[512,768]{1,0:T(8,128)(2,1)S(1)}, bf16[512,768]{1,0:T(8,128)(2,1)S(1)}, u32[]{:S(2)}, u32[]{:S(2)}) collective-permute-start(bf16[512,768]{1,0:T(8,128)(2,1)S(1)} %all_gather.14), channel_id=1, source_target_pairs={{0,1},{1,0},{2,3},{3,2},{4,5},{5,4},{6,7},{7,6},{8,9},{9,8},{10,11... | collective-permute-start | bytes 2359304 | tf_op jit(solution)/shard_map/cond/branch_1_fun/ppermute | solution.py:65
  63.2 1.2 collective-permute-done
  65.5 16.3 %all_to_all.17 = bf16[8,2,64,384]{3,2,1,0:T(8,128)(2,1)S(1)} all-to-all(bf16[8,2,64,384]{3,2,1,0:T(8,128)(2,1)S(1)} %copy.84), channel_id=1, replica_groups=mesh['x'=4,'yl'=2,'yh'=2,'z'=16,'c'=2] {'x','yl'}, dimensions={0} | all-to-all | bytes 1572864 | tf_op jit(solution)/shard_map/cond/branch_1_fun/all_to_all | solution.py:70
  82.0 14.3 %all_to_all.18 = bf16[8,128,384]{2,1,0:T(8,128)(2,1)S(1)} all-to-all(bf16[8,128,384]{2,1,0:T(8,128)(2,1)S(1)} %broadcast_in_dim.0), channel_id=1, replica_groups=mesh['x'=4,'yl'=2,'yh'=2,'z'=16,'c'=2] {'x','yl'}, dimensions={0} | all-to-all | bytes 1572864 | tf_op jit(solution)/shard_map/cond/branch_1_fun/all_to_all | solution.py:90
  97.1 4.7 %collective-permute-start.2 = (bf16[512,768]{1,0:T(8,128)(2,1)S(1)}, bf16[512,768]{1,0:T(8,128)(2,1)S(1)}, u32[]{:S(2)}, u32[]{:S(2)}) collective-permute-start(bf16[512,768]{1,0:T(8,128)(2,1)S(1)} %convolution_convert_fusion.2), channel_id=1, source_target_pairs={{0,1},{1,0},{2,3},{3,2},{4,5},{5,4},{6,7},{7,6},{8,9},{9,8},{10,11... | collective-permute-start | bytes 2359304 | tf_op jit(solution)/shard_map/ppermute | solution.py:65
  102.9 0.9 collective-permute-done.2
  103.7 1.5 add_convert_fusion
  105.2 47.6 %conditional.3 = (bf16[32,768]{1,0:T(8,128)(2,1)S(1)}, f32[768,384]{1,0:T(8,128)}) conditional(s32[]{:T(128)} %convert_element_type.81, () %tuple.26, (bf16[2,1,16,768]{3,2,1,0:T(8,128)(2,1)S(1)}, bf16[512,768]{1,0:T(8,128)(2,1)}, s32[]{:T(128)}, bf16[16,2,32,768]{3,2,1,0:T(8,128)(2,1)}, bf16[512,384]{1,0:T(8,128)(2,1)S(1)}, ...), branch_computations={%region_3.4_spmd, %region_4.6_spmd} | conditional | flops 604790784 | bytes 12632242 | solution.py:149
  105.2 5.4 %all-to-all-start.2 = ((bf16[16,32,768]{2,1,0:T(8,128)(2,1)}), bf16[16,32,768]{2,1,0:T(8,128)(2,1)S(1)}, u32[]{:S(2)}, u32[]{:S(2)}) async-start(bf16[16,32,768]{2,1,0:T(8,128)(2,1)} %bitcast.10), calls=%async_computation.2 | async-start | bytes 1572864 | tf_op jit(solution)/shard_map/cond/branch_1_fun/all_to_all | solution.py:133
  110.6 2.4 %constant_dynamic-slice_fusion = (bf16[16,1,32,768]{3,2,1,0:T(8,128)(2,1)}, bf16[16,1,32,768]{3,2,1,0:T(8,128)(2,1)S(1)}) fusion(bf16[16,2,32,768]{3,2,1,0:T(8,128)(2,1)} %get-tuple-element.25, s32[]{:T(128)S(6)} %select_n.87, s32[]{:T(128)S(6)} %select_n.86), kind=kLoop, calls=%fused_computation.10 | loop fusion | bytes 3145736 | tf_op jit(solution)/shard_map/cond/branch_1_fun/jit(dynamic_index_in_dim)/dynamic_slice | solution.py:135
  113.6 31.3 %all-to-all-done.2 = bf16[16,32,768]{2,1,0:T(8,128)(2,1)S(1)} async-done(((bf16[16,32,768]{2,1,0:T(8,128)(2,1)}), bf16[16,32,768]{2,1,0:T(8,128)(2,1)S(1)}, u32[]{:S(2)}, u32[]{:S(2)}) %all-to-all-start.2) | async-done | bytes 786464 | tf_op jit(solution)/shard_map/cond/branch_1_fun/all_to_all | solution.py:133
  145.0 5.0 %collective-permute-start.1 = (bf16[32,768]{1,0:T(8,128)(2,1)S(1)}, bf16[32,768]{1,0:T(8,128)(2,1)S(1)}, u32[]{:S(2)}, u32[]{:S(2)}) collective-permute-start(bf16[32,768]{1,0:T(8,128)(2,1)S(1)} %reduce_sum.28), channel_id=1, source_target_pairs={{0,32},{32,0},{1,33},{33,1},{2,34},{34,2},{3,35},{35,3},{4,36},{36... | collective-permute-start | bytes 147464 | tf_op jit(solution)/shard_map/cond/branch_1_fun/ppermute | solution.py:65
  150.0 2.8 %convolution_add_fusion = f32[768,384]{1,0:T(8,128)} fusion(f32[768,384]{1,0:T(8,128)S(1)} %fusion.16, bf16[512,768]{1,0:T(8,128)(2,1)} %bitcast.111, bf16[512,384]{1,0:T(8,128)(2,1)S(1)} %get-tuple-element.28), kind=kOutput, calls=%fused_computation.7 | convolution fusion | flops 302284800 | bytes 3538944 | tf_op jit(solution)/shard_map/cond/branch_1_fun/dot_general | solution.py:26
  152.9 1.3 fusion.13
  154.2 0.9 copy.100
  155.1 30.0 %all_gather.26 = bf16[512,768]{1,0:T(8,128)(2,1)S(1)} all-gather(bf16[32,768]{1,0:T(8,128)(2,1)S(1)} %get-tuple-element.48), channel_id=1, replica_groups=mesh['x'=4,'yl'=2,'yh'=2,'z'=16,'c'=2] {'z'}, dimensions={0}, use_global_device_ids=true | all-gather | bytes 835584 | tf_op jit(solution)/shard_map/all_gather | solution.py:84
  185.0 14.2 %collective-permute-start.3 = (bf16[512,768]{1,0:T(8,128)(2,1)S(1)}, bf16[512,768]{1,0:T(8,128)(2,1)S(1)}, u32[]{:S(2)}, u32[]{:S(2)}) collective-permute-start(bf16[512,768]{1,0:T(8,128)(2,1)S(1)} %all_gather.26), channel_id=1, source_target_pairs={{0,1},{1,0},{2,3},{3,2},{4,5},{5,4},{6,7},{7,6},{8,9},{9,8},{10,11... | collective-permute-start | bytes 2359304 | tf_op jit(solution)/shard_map/ppermute | solution.py:65
  199.2 1.0 convolution_convert_fusion.4
  200.2 1.7 copy.94
  201.9 1.6 copy.95
  203.5 1.9 fusion.7
  206.6 1.5 convolution_add_fusion.1
  209.8 3.4 %all-to-all-start.3 = ((bf16[8,2,64,96]{3,2,1,0:T(8,128)(2,1)}), bf16[8,2,64,96]{3,2,1,0:T(8,128)(2,1)S(1)}, u32[]{:S(2)}, u32[]{:S(2)}) async-start(bf16[8,2,64,96]{3,2,1,0:T(8,128)(2,1)} %copy.98), calls=%async_computation.3 | async-start | bytes 524288 | tf_op jit(solution)/shard_map/all_to_all | solution.py:70
  213.2 1.0 convolution_add_fusion.2
  214.2 5.8 %all-to-all-done.3 = bf16[8,2,64,96]{3,2,1,0:T(8,128)(2,1)S(1)} async-done(((bf16[8,2,64,96]{3,2,1,0:T(8,128)(2,1)}), bf16[8,2,64,96]{3,2,1,0:T(8,128)(2,1)S(1)}, u32[]{:S(2)}, u32[]{:S(2)}) %all-to-all-start.3) | async-done | bytes 196640 | tf_op jit(solution)/shard_map/all_to_all | solution.py:70
  (80 shorter events, 9.0 us)
Async XLA Ops:
  7.2 89.3 %copy-start = (bf16[768,384]{1,0:T(8,128)(2,1)S(1)}, bf16[768,384]{1,0:T(8,128)(2,1)}, u32[]{:S(2)}) copy-start(bf16[768,384]{1,0:T(8,128)(2,1)} %param.22) | copy-start | bytes 1769476
  7.2 10.2 %copy-start.11 = (f32[128,12]{0,1:T(8,128)S(1)}, f32[128,12]{0,1:T(8,128)}, u32[]{:S(2)}) copy-start(f32[128,12]{0,1:T(8,128)} %param.20) | copy-start | bytes 18436
  7.2 10.4 %copy-start.13 = (bf16[384,768]{1,0:T(8,128)(2,1)S(1)}, bf16[384,768]{1,0:T(8,128)(2,1)}, u32[]{:S(2)}) copy-start(bf16[384,768]{1,0:T(8,128)(2,1)} %param.23) | copy-start | bytes 1769476
  7.2 98.0 %all-gather.6.cloned.1.call-start = ((), (), s32[]{:S(2)}) async-start(), calls=%async_computation.4 | async-start | bytes 1622016 | tf_op jit(solution)/shard_map/all_gather | solution.py:104
  16.3 136.6 %all-gather.8.cloned.1.call-start = ((), (), s32[]{:S(2)}) async-start(), calls=%async_computation.5 | async-start | bytes 1179648 | tf_op jit(solution)/shard_map/all_gather | solution.py:130
  51.9 11.2 %copy-start.3 = (bf16[512,768]{1,0:T(8,128)(2,1)}, bf16[512,768]{1,0:T(8,128)(2,1)S(1)}, u32[]{:S(2)}) copy-start(bf16[512,768]{1,0:T(8,128)(2,1)S(1)} %all_gather.14) | copy-start | bytes 2359300 | tf_op jit(solution)/shard_map/cond
  51.9 12.5 %collective-permute-start = (bf16[512,768]{1,0:T(8,128)(2,1)S(1)}, bf16[512,768]{1,0:T(8,128)(2,1)S(1)}, u32[]{:S(2)}, u32[]{:S(2)}) collective-permute-start(bf16[512,768]{1,0:T(8,128)(2,1)S(1)} %all_gather.14), channel_id=1, source_target_pairs={{0,1},{1,0},{2,3},{3,2},{4,5},{5,4},{6,7},{7,6},{8,9},{9,8},{10,11... | collective-permute-start | bytes 2359304 | tf_op jit(solution)/shard_map/cond/branch_1_fun/ppermute | solution.py:65
  64.4 0.9 copy-start.1
  96.5 5.4 %copy-start.10 = (bf16[128,96]{0,1:T(8,128)(2,1)S(1)}, bf16[128,96]{0,1:T(8,128)(2,1)}, u32[]{:S(2)}) copy-start(bf16[128,96]{0,1:T(8,128)(2,1)} %param.15) | copy-start | bytes 73732
  96.5 5.4 %copy-start.12 = (f32[128,3]{0,1:T(4,128)S(1)}, f32[128,3]{0,1:T(4,128)}, u32[]{:S(2)}) copy-start(f32[128,3]{0,1:T(4,128)} %param.16) | copy-start | bytes 4612
  97.1 6.6 %collective-permute-start.2 = (bf16[512,768]{1,0:T(8,128)(2,1)S(1)}, bf16[512,768]{1,0:T(8,128)(2,1)S(1)}, u32[]{:S(2)}, u32[]{:S(2)}) collective-permute-start(bf16[512,768]{1,0:T(8,128)(2,1)S(1)} %convolution_convert_fusion.2), channel_id=1, source_target_pairs={{0,1},{1,0},{2,3},{3,2},{4,5},{5,4},{6,7},{7,6},{8,9},{9,8},{10,11... | collective-permute-start | bytes 2359304 | tf_op jit(solution)/shard_map/ppermute | solution.py:65
  105.2 39.7 %all-to-all-start.2 = ((bf16[16,32,768]{2,1,0:T(8,128)(2,1)}), bf16[16,32,768]{2,1,0:T(8,128)(2,1)S(1)}, u32[]{:S(2)}, u32[]{:S(2)}) async-start(bf16[16,32,768]{2,1,0:T(8,128)(2,1)} %bitcast.10), calls=%async_computation.2 | async-start | bytes 1572864 | tf_op jit(solution)/shard_map/cond/branch_1_fun/all_to_all | solution.py:133
  145.0 7.8 %collective-permute-start.1 = (bf16[32,768]{1,0:T(8,128)(2,1)S(1)}, bf16[32,768]{1,0:T(8,128)(2,1)S(1)}, u32[]{:S(2)}, u32[]{:S(2)}) collective-permute-start(bf16[32,768]{1,0:T(8,128)(2,1)S(1)} %reduce_sum.28), channel_id=1, source_target_pairs={{0,32},{32,0},{1,33},{33,1},{2,34},{34,2},{3,35},{35,3},{4,36},{36... | collective-permute-start | bytes 147464 | tf_op jit(solution)/shard_map/cond/branch_1_fun/ppermute | solution.py:65
  155.0 44.2 %copy-start.7 = (bf16[96,768]{1,0:T(8,128)(2,1)S(1)}, bf16[96,768]{1,0:T(8,128)(2,1)}, u32[]{:S(2)}) copy-start(bf16[96,768]{1,0:T(8,128)(2,1)} %param.21) | copy-start | bytes 442372
  185.0 20.4 %copy-start.4 = (bf16[512,768]{1,0:T(8,128)(2,1)S(1)}, bf16[512,768]{1,0:T(8,128)(2,1)}, u32[]{:S(2)}) copy-start(bf16[512,768]{1,0:T(8,128)(2,1)} %get-tuple-element.51) | copy-start | bytes 2359300
  185.0 23.1 %collective-permute-start.3 = (bf16[512,768]{1,0:T(8,128)(2,1)S(1)}, bf16[512,768]{1,0:T(8,128)(2,1)S(1)}, u32[]{:S(2)}, u32[]{:S(2)}) collective-permute-start(bf16[512,768]{1,0:T(8,128)(2,1)S(1)} %all_gather.26), channel_id=1, source_target_pairs={{0,1},{1,0},{2,3},{3,2},{4,5},{5,4},{6,7},{7,6},{8,9},{9,8},{10,11... | collective-permute-start | bytes 2359304 | tf_op jit(solution)/shard_map/ppermute | solution.py:65
  201.9 3.5 %copy-start.5 = (bf16[16,2,16,512]{3,2,1,0:T(8,128)(2,1)S(1)}, bf16[16,2,16,512]{3,2,1,0:T(8,128)(2,1)}, u32[]{:S(2)}) copy-start(bf16[16,2,16,512]{3,2,1,0:T(8,128)(2,1)} %copy.100) | copy-start | bytes 1572868
  205.4 1.1 copy-start.2
  206.6 1.5 copy-start.8
  208.1 0.9 copy-start.9
  208.5 4.7 %copy-start.6 = (f32[96,768]{1,0:T(8,128)S(1)}, f32[96,768]{1,0:T(8,128)}, u32[]{:S(2)}) copy-start(f32[96,768]{1,0:T(8,128)} %fusion.7) | copy-start | bytes 884740
  209.8 10.2 %all-to-all-start.3 = ((bf16[8,2,64,96]{3,2,1,0:T(8,128)(2,1)}), bf16[8,2,64,96]{3,2,1,0:T(8,128)(2,1)S(1)}, u32[]{:S(2)}, u32[]{:S(2)}) async-start(bf16[8,2,64,96]{3,2,1,0:T(8,128)(2,1)} %copy.98), calls=%async_computation.3 | async-start | bytes 524288 | tf_op jit(solution)/shard_map/all_to_all | solution.py:70
Sparse Core Ops, SparseCore 0:
  16.4 77.4 all-gather.5
  105.3 35.9 all-gather.7

commit v4 on v3

--- a/solution.py
+++ b/solution.py
@@ -41,6 +41,7 @@
     down_weight,
 ):
     core = lax.axis_index("c")
+    half = lax.axis_index("yh")
     n_rows, n_z = lax.axis_size(ROWS), lax.axis_size("z")
     per = grad_out.shape[0]
     runs = n_z * 2 // n_rows
@@ -64,11 +65,12 @@
     def swap(block, axis):
         return lax.ppermute(block, axis, SWAP)
 
-    def scatter_rows(own, other):
-        width = own.shape[1]
-        sent = jnp.stack([by_row(own), by_row(other)], axis=1)
+    def blocks_of(own, other):
+        return jnp.stack([by_row(own), by_row(other)], axis=1)
+
+    def scatter_rows(sent):
         came = lax.all_to_all(sent, ROWS, 0, 0, tiled=True)
-        return jnp.sum(came.astype(jnp.float32), axis=0).reshape(-1, width)
+        return jnp.sum(came.astype(jnp.float32), axis=0).reshape(-1, sent.shape[-1])
 
     def by_row(block):
         width = block.shape[1]
@@ -103,66 +105,70 @@
     both = lax.all_gather(jnp.stack([grad_out, stream]), "yh", axis=0)
     stream_all = lax.all_gather(both[:, 1], ("z", "c"), axis=0)
 
-    def first_half(pair):
-        grad_own = gather_z(pair)
+    def first_half(both):
+        grad_own = gather_z(both[:, 0])
         grad_other = swap(grad_own, "c")
-        grad_act = scatter_rows(
+        sent = blocks_of(
             dot_nt(grad_own, down_weight).astype(jnp.bfloat16),
             dot_nt(grad_other, down_weight).astype(jnp.bfloat16),
         )
+        grad_act = scatter_rows(sent)
         grad_pre = (grad_act * 2.0 * positive).astype(jnp.bfloat16)
         return grad_own, grad_other, gather_rows(grad_pre)
 
-    def skip(pair):
+    def skip(both):
         wide = jnp.zeros((n_z * 2 * per, features), jnp.bfloat16)
         return wide, wide, jnp.zeros((n_rows, 2, runs * per, hidden_width), jnp.bfloat16)
 
     always = lax.optimization_barrier(jnp.bool_(True))
-    grad_own, grad_other, grad_pre_all = lax.cond(always, first_half, skip, both[:, 0])
+    grad_own, grad_other, grad_pre_all = lax.cond(always, first_half, skip, both)
     pre_own = by_z(grad_pre_all[:, 0])
     pre_other = by_z(grad_pre_all[:, 1])
 
     came = swap(dot_nt(pre_other, up_weight).astype(jnp.bfloat16), "c")
-    part = (dot_nt(pre_own, up_weight) + came.astype(jnp.float32)).astype(jnp.bfloat16)
-    pair_out = both[:, 0].reshape(2 * per, features).astype(jnp.float32)
+    part = (dot_nt(pre_own, up_weight) + came.astype(jnp.float32)).reshape(n_z, 2, per, features)
+    keep = lax.dynamic_index_in_dim(part, half, 1, keepdims=False)
+    send = lax.dynamic_index_in_dim(part, 1 - half, 1, keepdims=False).astype(jnp.bfloat16)
     by_core = stream_all.reshape(n_z, 2, 2 * per, features)
-    part, saved, by_core = lax.optimization_barrier((part, saved, by_core))
+    send, saved, by_core = lax.optimization_barrier((send, saved, by_core))
     saved_all = lax.all_gather(saved, ROWS, axis=0)
 
-    def second_half(part, by_core):
-        came = lax.all_to_all(part.reshape(n_z, 2 * per, features), "z", 0, 0, tiled=True)
+    def second_half(keep, send, by_core):
+        part = (keep + swap(send, "yh").astype(jnp.float32)).astype(jnp.bfloat16)
+        came = lax.all_to_all(part, "z", 0, 0, tiled=True)
         stream_own = lax.dynamic_index_in_dim(by_core, core, 1, keepdims=False)
         stream_other = lax.dynamic_index_in_dim(by_core, 1 - core, 1, keepdims=False)
         stream_own = stream_own.reshape(-1, features)
         stream_other = stream_other.reshape(-1, features)
         grad_up = dot_tn(stream_own, pre_own) + dot_tn(stream_other, pre_other)
-        part = jnp.sum(came.astype(jnp.float32), axis=0).astype(jnp.bfloat16)
-        summed = part.astype(jnp.float32) + swap(part, "yh").astype(jnp.float32)
-        return (pair_out + summed).astype(jnp.bfloat16), grad_up
+        summed = jnp.sum(came.astype(jnp.float32), axis=0)
+        grad_stream = (grad_out.astype(jnp.float32) + summed).astype(jnp.bfloat16)
+        return lax.all_gather(grad_stream, "yh", axis=0), grad_up
 
-    def skip_second(part, by_core):
+    def skip_second(keep, send, by_core):
         return (
-            jnp.zeros((2 * per, features), jnp.bfloat16),
+            jnp.zeros((2, per, features), jnp.bfloat16),
             jnp.zeros((features, hidden_width), jnp.float32),
         )
 
-    grad_stream, grad_up = lax.cond(always, second_half, skip_second, part, by_core)
+    grad_stream, grad_up = lax.cond(always, second_half, skip_second, keep, send, by_core)
     grad_stream, saved_all = lax.optimization_barrier((grad_stream, saved_all))
 
     gs_own = gather_z(grad_stream)
     gs_other = swap(gs_own, "c")
-    grad_ctx = natural(
-        scatter_rows(
-            dot_nt(gs_own, out_weight).astype(jnp.bfloat16),
-            dot_nt(gs_other, out_weight).astype(jnp.bfloat16),
-        )
-    ).astype(jnp.bfloat16)
+    ctx_width = out_weight.shape[0]
+    wide = jnp.pad(out_weight, ((0, -ctx_width % 128), (0, 0)))
+    sent = blocks_of(
+        dot_nt(gs_own, wide).astype(jnp.bfloat16), dot_nt(gs_other, wide).astype(jnp.bfloat16)
+    )
+    sent, saved_all = lax.optimization_barrier((sent, saved_all))
+    grad_ctx = natural(scatter_rows(sent)[:, :ctx_width].astype(jnp.bfloat16))
 
     saved_pairs = saved_all.reshape(n_rows, 2, -1, saved_all.shape[-1])
     saved_own, saved_other = by_z(saved_pairs[:, 0]), by_z(saved_pairs[:, 1])
     act_own, act_other = saved_own[:, :hidden_width], saved_other[:, :hidden_width]
-    ctx_own = saved_own[:, hidden_width : hidden_width + context.shape[1]]
-    ctx_other = saved_other[:, hidden_width : hidden_width + context.shape[1]]
+    ctx_own = saved_own[:, hidden_width : hidden_width + ctx_width]
+    ctx_other = saved_other[:, hidden_width : hidden_width + ctx_width]
     grad_down = dot_tn(act_own, grad_own) + dot_tn(act_other, grad_other)
     grad_outw = dot_tn(ctx_own, gs_own) + dot_tn(ctx_other, gs_other)
     return (grad_ctx, grad_outw, grad_up, grad_down)

time: 229 us -> 222 us (0.969)
  waiting for transfers between devices: 39.2 us -> 30.4 us
  local copies, waits for them, and re-layouts: 14 us -> 8.62 us
  blocking collectives: 101 us -> 106 us
  other arithmetic: 2.8 us -> 6.16 us
    all_to_all x1, waiting for transfers between devices: 31.3 us -> 13.8 us  [second_half(): came = lax.all_to_all(part, 'z', 0, 0, tiled=True)]
    ppermute x4, waiting for transfers between devices: 2.1 us -> 14.5 us  [swap(): return lax.ppermute(block, axis, SWAP)]
    all_gather x0 -> x1, blocking collectives: none -> 5.25 us  [second_half(): return (lax.all_gather(grad_stream, 'yh', axis=0), grad_up)]
    all_to_all x1, waiting for transfers between devices: 5.75 us -> 2.07 us  [scatter_rows(): came = lax.all_to_all(sent, ROWS, 0, 0, tiled=True)]
  transfers between devices with their start and end apart: 8 -> 8, of which waited for: 4 -> 6; matrix products, arithmetic and copies ran while one was open for 9% -> 8% of each run, Pallas kernels for 0% -> 0%
where the time goes in v4:
time: 222 us; the launch traced here: 221 us
  blocking collectives  106 us (48%)
  starting transfers between devices  42.8 us (19%)
  waiting for transfers between devices  30.4 us (14%)
  between operations  14.4 us (6%)
  matrix products  12.4 us (6%)
  local copies, waits for them, and re-layouts  8.62 us (4%)
  other arithmetic  6.16 us (3%)
    all_gather x2, blocking collectives, gather_z(): return lax.all_gather(pair.reshape(-1, features), 'z', axis=0, tiled=True)  64.3 us
    ppermute x4, starting transfers between devices, swap(): return lax.ppermute(block, axis, SWAP)  33.9 us
    all_to_all x1, blocking collectives, scatter_rows(): came = lax.all_to_all(sent, ROWS, 0, 0, tiled=True)  16.7 us
    ppermute x4, waiting for transfers between devices, swap(): return lax.ppermute(block, axis, SWAP)  14.5 us
    all_to_all x1, blocking collectives, gather_rows(): every = lax.all_to_all(copies, ROWS, 0, 0, tiled=True)  14.3 us
    all_to_all x1, waiting for transfers between devices, second_half(): came = lax.all_to_all(part, 'z', 0, 0, tiled=True)  13.8 us
    dot_general x6, matrix products, dot_tn(): lax.dot_general(left, right, (((0,), (0,)), ((), ())), preferred_element_...  8.19 us
    all_gather x1, blocking collectives, local(): both = lax.all_gather(jnp.stack([grad_out, stream]), 'yh', axis=0)  5.86 us
  transfers between devices with their start and end apart: 8, of which 6 were waited for; matrix products, arithmetic and copies ran while one was open for 8% of the time, Pallas kernels for 0%

profile of v4, /device:TPU:1, one launch (start us, length us, event | category | flops | bytes accessed | tf_op | source)
XLA Modules:
  0.0 221.4 jit_solution(12558924422645019343)
XLA Ops:
  7.2 0.9 mul.45
  9.7 5.9 %all-gather.1 = bf16[4,16,768]{2,1,0:T(8,128)(2,1)S(1)} all-gather(bf16[2,16,768]{2,1,0:T(8,128)(2,1)S(1)} %pad_maximum_fusion.2), channel_id=3, replica_groups=mesh['x'=4,'yl'=2,'yh'=2,'z'=16,'c'=2] {'yh'}, dimensions={0}, use_global_device_ids=true | all-gather | bytes 147456 | tf_op jit(solution)/shard_map/all_gather | solution.py:105
  16.3 1.0 copy.83
  18.2 79.0 %conditional.2 = (bf16[512,768]{1,0:T(8,128)(2,1)}, bf16[512,768]{1,0:T(8,128)(2,1)}, bf16[8,2,64,384]{3,2,1,0:T(8,128)(2,1)S(1)}) conditional(s32[]{:T(128)} %convert_element_type.80, () %tuple.29, (bf16[2,2,16,768]{3,2,1,0:T(8,128)(2,1)S(1)}, bf16[384,768]{1,0:T(8,128)(2,1)S(1)}, f32[128,384]{1,0:T(8,128)S(1)}) %tuple.59), branch_computations={%region_0.1_spmd, %region_1.3_spmd} | conditional | flops 605650944 | bytes 24526968 | solution.py:124
  18.3 34.1 %all_gather.18 = bf16[512,768]{1,0:T(8,128)(2,1)S(1)} all-gather(bf16[32,768]{1,0:T(8,128)(2,1)S(1)} %bitcast.150), channel_id=1, replica_groups=mesh['x'=4,'yl'=2,'yh'=2,'z'=16,'c'=2] {'z'}, dimensions={0}, use_global_device_ids=true | all-gather | bytes 835584 | tf_op jit(solution)/shard_map/cond/branch_1_fun/all_gather | solution.py:86
  52.3 10.7 %collective-permute-start = (bf16[512,768]{1,0:T(8,128)(2,1)S(1)}, bf16[512,768]{1,0:T(8,128)(2,1)S(1)}, u32[]{:S(2)}, u32[]{:S(2)}) collective-permute-start(bf16[512,768]{1,0:T(8,128)(2,1)S(1)} %all_gather.18), channel_id=1, source_target_pairs={{0,1},{1,0},{2,3},{3,2},{4,5},{5,4},{6,7},{7,6},{8,9},{9,8},{10,11... | collective-permute-start | bytes 2359304 | tf_op jit(solution)/shard_map/cond/branch_1_fun/ppermute | solution.py:66
  63.7 1.2 collective-permute-done
  66.0 16.7 %all_to_all.17 = bf16[8,2,64,384]{3,2,1,0:T(8,128)(2,1)S(1)} all-to-all(bf16[8,2,64,384]{3,2,1,0:T(8,128)(2,1)S(1)} %copy.82), channel_id=1, replica_groups=mesh['x'=4,'yl'=2,'yh'=2,'z'=16,'c'=2] {'x','yl'}, dimensions={0} | all-to-all | bytes 1572864 | tf_op jit(solution)/shard_map/cond/branch_1_fun/all_to_all | solution.py:72
  83.0 14.3 %all_to_all.18 = bf16[8,128,384]{2,1,0:T(8,128)(2,1)S(1)} all-to-all(bf16[8,128,384]{2,1,0:T(8,128)(2,1)S(1)} %broadcast_in_dim.0), channel_id=1, replica_groups=mesh['x'=4,'yl'=2,'yh'=2,'z'=16,'c'=2] {'x','yl'}, dimensions={0} | all-to-all | bytes 1572864 | tf_op jit(solution)/shard_map/cond/branch_1_fun/all_to_all | solution.py:92
  98.0 4.6 %collective-permute-start.2 = (bf16[512,768]{1,0:T(8,128)(2,1)S(1)}, bf16[512,768]{1,0:T(8,128)(2,1)S(1)}, u32[]{:S(2)}, u32[]{:S(2)}) collective-permute-start(bf16[512,768]{1,0:T(8,128)(2,1)S(1)} %convolution_convert_fusion.2), channel_id=1, source_target_pairs={{0,1},{1,0},{2,3},{3,2},{4,5},{5,4},{6,7},{7,6},{8,9},{9,8},{10,11... | collective-permute-start | bytes 2359304 | tf_op jit(solution)/shard_map/ppermute | solution.py:66
  103.7 0.8 collective-permute-done.2
  104.5 0.9 copy-done.7
  105.4 1.7 convert_add_fusion
  107.3 45.1 %conditional.3 = (bf16[2,16,768]{2,1,0:T(8,128)(2,1)S(1)}, f32[768,384]{1,0:T(8,128)}) conditional(s32[]{:T(128)} %convert_element_type.80, () %tuple.28, (bf16[16,768]{1,0:T(8,128)(2,1)}, s32[]{:T(128)}, f32[16,2,16,768]{3,2,1,0:T(8,128)S(1)}, bf16[16,16,768]{2,1,0:T(8,128)(2,1)S(1)}, s32[]{:T(128)}, /*index=5*/bf16[16,2,32,768]{3,2,1,0:T(8,128)(2,1)}, ...), branch_computations={%region_3.4_spmd, %region_4.6_spmd} | conditional | flops 605282304 | bytes 14082290 | solution.py:154
  107.3 4.7 %collective-permute-start.1 = (bf16[16,16,768]{2,1,0:T(8,128)(2,1)S(1)}, bf16[16,16,768]{2,1,0:T(8,128)(2,1)}, u32[]{:S(2)}, u32[]{:S(2)}) collective-permute-start(bf16[16,16,768]{2,1,0:T(8,128)(2,1)S(1)} %get-tuple-element.38), channel_id=1, source_target_pairs={{0,32},{32,0},{1,33},{33,1},{2,34},{34,2},{3,35},{35,3},{4,36},{36... | collective-permute-start | bytes 1179656 | tf_op jit(solution)/shard_map/cond/branch_1_fun/ppermute | solution.py:66
  112.0 10.9 %collective-permute-done.1 = bf16[16,16,768]{2,1,0:T(8,128)(2,1)} collective-permute-done((bf16[16,16,768]{2,1,0:T(8,128)(2,1)S(1)}, bf16[16,16,768]{2,1,0:T(8,128)(2,1)}, u32[]{:S(2)}, u32[]{:S(2)}) %collective-permute-start.1) | collective-permute-done | bytes 393248 | tf_op jit(solution)/shard_map/cond/branch_1_fun/ppermute | solution.py:66
  122.9 1.8 fusion.1
  124.7 4.8 %all-to-all-start.2 = ((bf16[16,16,768]{2,1,0:T(8,128)(2,1)}), bf16[16,16,768]{2,1,0:T(8,128)(2,1)S(1)}, u32[]{:S(2)}, u32[]{:S(2)}) async-start(bf16[16,16,768]{2,1,0:T(8,128)(2,1)} %fusion.1), calls=%async_computation.2 | async-start | bytes 786432 | tf_op jit(solution)/shard_map/cond/branch_1_fun/all_to_all | solution.py:138
  129.6 1.5 constant_dynamic-slice_fusion
  131.7 1.6 convolution_add_fusion
  133.3 13.8 %all-to-all-done.2 = bf16[16,16,768]{2,1,0:T(8,128)(2,1)S(1)} async-done(((bf16[16,16,768]{2,1,0:T(8,128)(2,1)}), bf16[16,16,768]{2,1,0:T(8,128)(2,1)S(1)}, u32[]{:S(2)}, u32[]{:S(2)}) %all-to-all-start.2) | async-done | bytes 393248 | tf_op jit(solution)/shard_map/cond/branch_1_fun/all_to_all | solution.py:138
  147.1 5.2 %all-gather = bf16[32,768]{1,0:T(8,128)(2,1)S(1)} all-gather(bf16[16,768]{1,0:T(8,128)(2,1)S(1)} %add_convert_fusion), channel_id=2, replica_groups=mesh['x'=4,'yl'=2,'yh'=2,'z'=16,'c'=2] {'yh'}, dimensions={0}, use_global_device_ids=true | all-gather | bytes 73728 | tf_op jit(solution)/shard_map/cond/branch_1_fun/all_gather | solution.py:146
  152.4 30.2 %all_gather.32 = bf16[512,768]{1,0:T(8,128)(2,1)S(1)} all-gather(bf16[32,768]{1,0:T(8,128)(2,1)S(1)} %bitcast.149), channel_id=1, replica_groups=mesh['x'=4,'yl'=2,'yh'=2,'z'=16,'c'=2] {'z'}, dimensions={0}, use_global_device_ids=true | all-gather | bytes 835584 | tf_op jit(solution)/shard_map/all_gather | solution.py:86
  182.6 13.9 %collective-permute-start.3 = (bf16[512,768]{1,0:T(8,128)(2,1)S(1)}, bf16[512,768]{1,0:T(8,128)(2,1)S(1)}, u32[]{:S(2)}, u32[]{:S(2)}) collective-permute-start(bf16[512,768]{1,0:T(8,128)(2,1)S(1)} %all_gather.32), channel_id=1, source_target_pairs={{0,1},{1,0},{2,3},{3,2},{4,5},{5,4},{6,7},{7,6},{8,9},{9,8},{10,11... | collective-permute-start | bytes 2359304 | tf_op jit(solution)/shard_map/ppermute | solution.py:66
  197.0 1.5 collective-permute-done.3
  199.0 1.0 fusion.10
  200.6 0.9 copy.98
  202.2 4.1 %all-to-all-start.3 = ((bf16[8,2,64,128]{3,2,1,0:T(8,128)(2,1)}), bf16[8,2,64,128]{3,2,1,0:T(8,128)(2,1)}, u32[]{:S(2)}, u32[]{:S(2)}) async-start(bf16[8,2,64,128]{3,2,1,0:T(8,128)(2,1)} %copy.95), calls=%async_computation.3 | async-start | bytes 524288 | tf_op jit(solution)/shard_map/all_to_all | solution.py:72
  206.3 2.6 %convolution_add_fusion.1 = f32[384,768]{1,0:T(8,128)} fusion(f32[384,768]{1,0:T(8,128)S(1)} %fusion.4, bf16[512,768]{1,0:T(8,128)(2,1)S(1)} %copy-done.2, bf16[512,512]{1,0:T(8,128)(2,1)} %bitcast.124), kind=kOutput, calls=%fused_computation.15 | convolution fusion | flops 302284800 | bytes 3538944 | tf_op jit(solution)/shard_map/dot_general | solution.py:26
  208.8 1.9 convolution_add_fusion.2
  210.8 2.1 all-to-all-done.3
  212.8 1.0 reduce
  (80 shorter events, 10.5 us)
Async XLA Ops:
  7.2 90.2 %copy-start = (bf16[768,384]{1,0:T(8,128)(2,1)S(1)}, bf16[768,384]{1,0:T(8,128)(2,1)}, u32[]{:S(2)}) copy-start(bf16[768,384]{1,0:T(8,128)(2,1)} %param.22) | copy-start | bytes 1769476
  7.2 11.1 %copy-start.12 = (bf16[384,768]{1,0:T(8,128)(2,1)S(1)}, bf16[384,768]{1,0:T(8,128)(2,1)}, u32[]{:S(2)}) copy-start(bf16[384,768]{1,0:T(8,128)(2,1)} %param.23) | copy-start | bytes 1769476
  7.2 100.0 %all-gather.7.cloned.1.call-start = ((), (), s32[]{:S(2)}) async-start(), calls=%async_computation.4 | async-start | bytes 1622016 | tf_op jit(solution)/shard_map/all_gather | solution.py:106
  16.3 136.1 %all-gather.9.cloned.1.call-start = ((), (), s32[]{:S(2)}) async-start(), calls=%async_computation.5 | async-start | bytes 1179648 | tf_op jit(solution)/shard_map/all_gather | solution.py:134
  52.3 11.3 %copy-start.3 = (bf16[512,768]{1,0:T(8,128)(2,1)}, bf16[512,768]{1,0:T(8,128)(2,1)S(1)}, u32[]{:S(2)}) copy-start(bf16[512,768]{1,0:T(8,128)(2,1)S(1)} %all_gather.18) | copy-start | bytes 2359300 | tf_op jit(solution)/shard_map/cond
  52.3 12.6 %collective-permute-start = (bf16[512,768]{1,0:T(8,128)(2,1)S(1)}, bf16[512,768]{1,0:T(8,128)(2,1)S(1)}, u32[]{:S(2)}, u32[]{:S(2)}) collective-permute-start(bf16[512,768]{1,0:T(8,128)(2,1)S(1)} %all_gather.18), channel_id=1, source_target_pairs={{0,1},{1,0},{2,3},{3,2},{4,5},{5,4},{6,7},{7,6},{8,9},{9,8},{10,11... | collective-permute-start | bytes 2359304 | tf_op jit(solution)/shard_map/cond/branch_1_fun/ppermute | solution.py:66
  64.9 0.9 copy-start.1
  97.4 5.3 %copy-start.10 = (bf16[128,96]{0,1:T(8,128)(2,1)S(1)}, bf16[128,96]{0,1:T(8,128)(2,1)}, u32[]{:S(2)}) copy-start(bf16[128,96]{0,1:T(8,128)(2,1)} %param.15) | copy-start | bytes 73732
  97.4 5.3 %copy-start.11 = (f32[128,3]{0,1:T(4,128)S(1)}, f32[128,3]{0,1:T(4,128)}, u32[]{:S(2)}) copy-start(f32[128,3]{0,1:T(4,128)} %param.16) | copy-start | bytes 4612
  98.0 6.5 %collective-permute-start.2 = (bf16[512,768]{1,0:T(8,128)(2,1)S(1)}, bf16[512,768]{1,0:T(8,128)(2,1)S(1)}, u32[]{:S(2)}, u32[]{:S(2)}) collective-permute-start(bf16[512,768]{1,0:T(8,128)(2,1)S(1)} %convolution_convert_fusion.2), channel_id=1, source_target_pairs={{0,1},{1,0},{2,3},{3,2},{4,5},{5,4},{6,7},{7,6},{8,9},{9,8},{10,11... | collective-permute-start | bytes 2359304 | tf_op jit(solution)/shard_map/ppermute | solution.py:66
  104.5 0.9 copy-start.7
  107.2 89.3 %copy-start.8 = (bf16[96,768]{1,0:T(8,128)(2,1)S(1)}, bf16[96,768]{1,0:T(8,128)(2,1)}, u32[]{:S(2)}) copy-start(bf16[96,768]{1,0:T(8,128)(2,1)} %param.21) | copy-start | bytes 442372
  107.3 15.6 %collective-permute-start.1 = (bf16[16,16,768]{2,1,0:T(8,128)(2,1)S(1)}, bf16[16,16,768]{2,1,0:T(8,128)(2,1)}, u32[]{:S(2)}, u32[]{:S(2)}) collective-permute-start(bf16[16,16,768]{2,1,0:T(8,128)(2,1)S(1)} %get-tuple-element.38), channel_id=1, source_target_pairs={{0,32},{32,0},{1,33},{33,1},{2,34},{34,2},{3,35},{35,3},{4,36},{36... | collective-permute-start | bytes 1179656 | tf_op jit(solution)/shard_map/cond/branch_1_fun/ppermute | solution.py:66
  124.7 22.3 %all-to-all-start.2 = ((bf16[16,16,768]{2,1,0:T(8,128)(2,1)}), bf16[16,16,768]{2,1,0:T(8,128)(2,1)S(1)}, u32[]{:S(2)}, u32[]{:S(2)}) async-start(bf16[16,16,768]{2,1,0:T(8,128)(2,1)} %fusion.1), calls=%async_computation.2 | async-start | bytes 786432 | tf_op jit(solution)/shard_map/cond/branch_1_fun/all_to_all | solution.py:138
  131.7 15.5 %copy-start.9 = (bf16[16,768]{1,0:T(8,128)(2,1)S(1)}, bf16[16,768]{1,0:T(8,128)(2,1)}, u32[]{:S(2)}) copy-start(bf16[16,768]{1,0:T(8,128)(2,1)} %get-tuple-element.35) | copy-start | bytes 73732 | tf_op jit(solution)/shard_map/cond
  182.6 15.8 %collective-permute-start.3 = (bf16[512,768]{1,0:T(8,128)(2,1)S(1)}, bf16[512,768]{1,0:T(8,128)(2,1)S(1)}, u32[]{:S(2)}, u32[]{:S(2)}) collective-permute-start(bf16[512,768]{1,0:T(8,128)(2,1)S(1)} %all_gather.32), channel_id=1, source_target_pairs={{0,1},{1,0},{2,3},{3,2},{4,5},{5,4},{6,7},{7,6},{8,9},{9,8},{10,11... | collective-permute-start | bytes 2359304 | tf_op jit(solution)/shard_map/ppermute | solution.py:66
  196.9 1.9 copy-start.6
  199.0 1.1 copy-start.4
  200.6 5.7 %copy-start.2 = (bf16[512,768]{1,0:T(8,128)(2,1)S(1)}, bf16[512,768]{1,0:T(8,128)(2,1)}, u32[]{:S(2)}) copy-start(bf16[512,768]{1,0:T(8,128)(2,1)} %get-tuple-element.70) | copy-start | bytes 2359300
  202.2 10.6 %all-to-all-start.3 = ((bf16[8,2,64,128]{3,2,1,0:T(8,128)(2,1)}), bf16[8,2,64,128]{3,2,1,0:T(8,128)(2,1)}, u32[]{:S(2)}, u32[]{:S(2)}) async-start(bf16[8,2,64,128]{3,2,1,0:T(8,128)(2,1)} %copy.95), calls=%async_computation.3 | async-start | bytes 524288 | tf_op jit(solution)/shard_map/all_to_all | solution.py:72
  206.3 2.6 %copy-start.5 = (f32[96,768]{1,0:T(8,128)S(1)}, f32[96,768]{1,0:T(8,128)}, u32[]{:S(2)}) copy-start(f32[96,768]{1,0:T(8,128)} %fusion.10) | copy-start | bytes 884740
Sparse Core Ops, SparseCore 0:
  16.4 77.5 all-gather.6
  107.4 36.9 all-gather.8

commit v5 on v4

--- a/solution.py
+++ b/solution.py
@@ -1,10 +1,13 @@
 import jax
 import jax.numpy as jnp
 from jax import lax
+from jax.experimental import pallas as pl
+from jax.experimental.pallas import tpu as pltpu
 from jax.sharding import Mesh
 from jax.sharding import PartitionSpec as P
 
 QBLOCK = 32
+PER = 16
 ROWS = ("x", "yl")
 COLS = ("yh", "z", "c")
 SWAP = ((0, 1), (1, 0))
@@ -26,6 +29,78 @@
     return lax.dot_general(
         left, right, (((0,), (0,)), ((), ())), preferred_element_type=jnp.float32
     )
+
+
+def outgoing_kernel(grad_ref, code_ref, scale_ref, out_ref):
+    blocks, width = scale_ref.shape[1], code_ref.shape[1]
+    row = lax.broadcasted_iota(jnp.int32, (blocks, width), 0)
+    column = lax.broadcasted_iota(jnp.int32, (blocks, width), 1)
+    first = row * QBLOCK
+    spread = jnp.where((column >= first) & (column < first + QBLOCK), 1.0, 0.0)
+    scale = jnp.dot(
+        scale_ref[...],
+        spread.astype(jnp.float32),
+        precision=lax.Precision.HIGHEST,
+        preferred_element_type=jnp.float32,
+    )
+    out_ref[0] = grad_ref[...]
+    out_ref[1] = (code_ref[...].astype(jnp.float32) * scale).astype(jnp.bfloat16)
+
+
+def outgoing(grad_out, code, scale):
+    return pl.pallas_call(
+        outgoing_kernel,
+        out_shape=jax.ShapeDtypeStruct((2,) + grad_out.shape, jnp.bfloat16),
+        in_specs=[pl.BlockSpec(memory_space=pltpu.VMEM)] * 3,
+        out_specs=pl.BlockSpec(memory_space=pltpu.VMEM),
+    )(grad_out, code, scale)
+
+
+def last_kernel(
+    saved_ref, grad_own_ref, grad_other_ref, gs_own_ref, gs_other_ref, down_ref, out_ref, rows_ref
+):
+    n_rows, _, block, wide = saved_ref.shape
+    runs, per = rows_ref.shape[0] * 2 // n_rows, rows_ref.shape[2]
+    hidden_width, ctx_width = down_ref.shape[0], out_ref.shape[0]
+    for side, grad_ref, gs_ref in (
+        (0, grad_own_ref, gs_own_ref),
+        (1, grad_other_ref, gs_other_ref),
+    ):
+        for row in range(n_rows):
+            half, first = row // (n_rows // 2), row % (n_rows // 2) * runs
+            for run in range(runs):
+                rows_ref[first + run, half] = saved_ref[row, side, pl.ds(run * per, per), :]
+        rows = rows_ref[...].reshape(-1, wide)
+        down = dot_tn(rows[:, :hidden_width], grad_ref[...])
+        out = dot_tn(rows[:, hidden_width:], gs_ref[...])[:ctx_width]
+        if side == 0:
+            down_ref[...] = down
+            out_ref[...] = out
+        else:
+            down_ref[...] += down
+            out_ref[...] += out
+
+
+def last_products(saved_all, grad_own, grad_other, gs_own, gs_other, hidden_width, ctx_width):
+    features = grad_own.shape[1]
+    return pl.pallas_call(
+        last_kernel,
+        out_shape=(
+            jax.ShapeDtypeStruct((hidden_width, features), jnp.float32),
+            jax.ShapeDtypeStruct((ctx_width, features), jnp.float32),
+        ),
+        in_specs=[pl.BlockSpec(memory_space=pltpu.VMEM)] * 5,
+        out_specs=(pl.BlockSpec(memory_space=pltpu.VMEM),) * 2,
+        scratch_shapes=[
+            pltpu.VMEM((grad_own.shape[0] // (2 * PER), 2, PER, saved_all.shape[3]), jnp.bfloat16)
+        ],
+        compiler_params=pltpu.CompilerParams(vmem_limit_bytes=32 * 2**20),
+        cost_estimate=pl.CostEstimate(
+            flops=4 * grad_own.size * saved_all.shape[3],
+            bytes_accessed=8 * grad_own.size + 2 * saved_all.size,
+            transcendentals=0,
+        ),
+    )(saved_all, grad_own, grad_other, gs_own, gs_other)
 
 
 def local(
@@ -46,6 +121,7 @@
     per = grad_out.shape[0]
     runs = n_z * 2 // n_rows
     features = grad_out.shape[1]
+    hidden_width, ctx_width = hidden_code.shape[1], ctx_code.shape[1]
 
     def own_first(block):
         width = block.shape[1]
@@ -92,17 +168,7 @@
         every = lax.all_to_all(copies, ROWS, 0, 0, tiled=True)
         return every.reshape(n_rows, 2, -1, block.shape[1])
 
-    stream = restore(stream_code, stream_scale)
-    positive = jnp.maximum(
-        own_first(restore(hidden_code, hidden_scale)).astype(jnp.float32), 0.0
-    )
-    act = (positive * positive).astype(jnp.bfloat16)
-    context = own_first(restore(ctx_code, ctx_scale))
-    hidden_width = act.shape[1]
-    padding = jnp.zeros((act.shape[0], 512 - hidden_width - context.shape[1]), jnp.bfloat16)
-    saved = jnp.concatenate([act, context, padding], axis=1)
-
-    both = lax.all_gather(jnp.stack([grad_out, stream]), "yh", axis=0)
+    both = lax.all_gather(outgoing(grad_out, stream_code, stream_scale), "yh", axis=0)
     stream_all = lax.all_gather(both[:, 1], ("z", "c"), axis=0)
 
     def first_half(both):
@@ -113,15 +179,23 @@
             dot_nt(grad_other, down_weight).astype(jnp.bfloat16),
         )
         grad_act = scatter_rows(sent)
+        positive = jnp.maximum(
+            own_first(restore(hidden_code, hidden_scale)).astype(jnp.float32), 0.0
+        )
+        act = (positive * positive).astype(jnp.bfloat16)
         grad_pre = (grad_act * 2.0 * positive).astype(jnp.bfloat16)
-        return grad_own, grad_other, gather_rows(grad_pre)
+        return grad_own, grad_other, gather_rows(grad_pre), act
 
     def skip(both):
         wide = jnp.zeros((n_z * 2 * per, features), jnp.bfloat16)
-        return wide, wide, jnp.zeros((n_rows, 2, runs * per, hidden_width), jnp.bfloat16)
+        pre = jnp.zeros((n_rows, 2, runs * per, hidden_width), jnp.bfloat16)
+        return wide, wide, pre, jnp.zeros(hidden_code.shape, jnp.bfloat16)
 
     always = lax.optimization_barrier(jnp.bool_(True))
-    grad_own, grad_other, grad_pre_all = lax.cond(always, first_half, skip, both)
+    grad_own, grad_other, grad_pre_all, act = lax.cond(always, first_half, skip, both)
+    context = own_first(restore(ctx_code, ctx_scale))
+    padding = jnp.zeros((act.shape[0], 512 - hidden_width - ctx_width), jnp.bfloat16)
+    saved = jnp.concatenate([act, context, padding], axis=1)
     pre_own = by_z(grad_pre_all[:, 0])
     pre_other = by_z(grad_pre_all[:, 1])
 
@@ -130,11 +204,12 @@
     keep = lax.dynamic_index_in_dim(part, half, 1, keepdims=False)
     send = lax.dynamic_index_in_dim(part, 1 - half, 1, keepdims=False).astype(jnp.bfloat16)
     by_core = stream_all.reshape(n_z, 2, 2 * per, features)
-    send, saved, by_core = lax.optimization_barrier((send, saved, by_core))
+    part = (keep + swap(send, "yh").astype(jnp.float32)).astype(jnp.bfloat16)
+    part, saved, by_core = lax.optimization_barrier((part, saved, by_core))
     saved_all = lax.all_gather(saved, ROWS, axis=0)
-
-    def second_half(keep, send, by_core):
-        part = (keep + swap(send, "yh").astype(jnp.float32)).astype(jnp.bfloat16)
+    padded_out = jnp.pad(out_weight, ((0, -ctx_width % 128), (0, 0)))
+
+    def second_half(part, by_core):
         came = lax.all_to_all(part, "z", 0, 0, tiled=True)
         stream_own = lax.dynamic_index_in_dim(by_core, core, 1, keepdims=False)
         stream_other = lax.dynamic_index_in_dim(by_core, 1 - core, 1, keepdims=False)
@@ -143,34 +218,35 @@
         grad_up = dot_tn(stream_own, pre_own) + dot_tn(stream_other, pre_other)
         summed = jnp.sum(came.astype(jnp.float32), axis=0)
         grad_stream = (grad_out.astype(jnp.float32) + summed).astype(jnp.bfloat16)
-        return lax.all_gather(grad_stream, "yh", axis=0), grad_up
-
-    def skip_second(keep, send, by_core):
+        gs_own = gather_z(lax.all_gather(grad_stream, "yh", axis=0))
+        gs_other = swap(gs_own, "c")
+        sent = blocks_of(
+            dot_nt(gs_own, padded_out).astype(jnp.bfloat16),
+            dot_nt(gs_other, padded_out).astype(jnp.bfloat16),
+        )
+        return gs_own, gs_other, sent, grad_up
+
+    def skip_second(part, by_core):
+        wide = jnp.zeros((n_z * 2 * per, features), jnp.bfloat16)
         return (
-            jnp.zeros((2, per, features), jnp.bfloat16),
+            wide,
+            wide,
+            jnp.zeros((n_rows, 2, runs * per, padded_out.shape[0]), jnp.bfloat16),
             jnp.zeros((features, hidden_width), jnp.float32),
         )
 
-    grad_stream, grad_up = lax.cond(always, second_half, skip_second, keep, send, by_core)
-    grad_stream, saved_all = lax.optimization_barrier((grad_stream, saved_all))
-
-    gs_own = gather_z(grad_stream)
-    gs_other = swap(gs_own, "c")
-    ctx_width = out_weight.shape[0]
-    wide = jnp.pad(out_weight, ((0, -ctx_width % 128), (0, 0)))
-    sent = blocks_of(
-        dot_nt(gs_own, wide).astype(jnp.bfloat16), dot_nt(gs_other, wide).astype(jnp.bfloat16)
-    )
+    gs_own, gs_other, sent, grad_up = lax.cond(always, second_half, skip_second, part, by_core)
     sent, saved_all = lax.optimization_barrier((sent, saved_all))
     grad_ctx = natural(scatter_rows(sent)[:, :ctx_width].astype(jnp.bfloat16))
-
-    saved_pairs = saved_all.reshape(n_rows, 2, -1, saved_all.shape[-1])
-    saved_own, saved_other = by_z(saved_pairs[:, 0]), by_z(saved_pairs[:, 1])
-    act_own, act_other = saved_own[:, :hidden_width], saved_other[:, :hidden_width]
-    ctx_own = saved_own[:, hidden_width : hidden_width + ctx_width]
-    ctx_other = saved_other[:, hidden_width : hidden_width + ctx_width]
-    grad_down = dot_tn(act_own, grad_own) + dot_tn(act_other, grad_other)
-    grad_outw = dot_tn(ctx_own, gs_own) + dot_tn(ctx_other, gs_other)
+    grad_down, grad_outw = last_products(
+        saved_all.reshape(n_rows, 2, -1, saved_all.shape[-1]),
+        grad_own,
+        grad_other,
+        gs_own,
+        gs_other,
+        hidden_width,
+        ctx_width,
+    )
     return (grad_ctx, grad_outw, grad_up, grad_down)
 
 

time: 222 us -> 222 us (level)
  blocking collectives: 106 us -> 95.5 us
  waiting for transfers between devices: 30.4 us -> 39.6 us
  Pallas kernels: 0 us -> 5.34 us
  other arithmetic: 6.16 us -> 2.97 us
  starting transfers between devices: 42.8 us -> 45.5 us
  matrix products: 12.4 us -> 9.76 us
    all_to_all x1 -> x0, blocking collectives: 16.7 us -> none  [scatter_rows(): came = lax.all_to_all(sent, ROWS, 0, 0, tiled=True)]
    all_to_all x1 -> x2, waiting for transfers between devices: 2.07 us -> 13.4 us  [scatter_rows(): came = lax.all_to_all(sent, ROWS, 0, 0, tiled=True)]
    dot_general x6 -> x2, matrix products: 8.19 us -> 2.23 us  [dot_tn(): lax.dot_general(left, right, (((0,), (0,)), ((), ())), preferred_element_...]
    pallas_call x0 -> x2, Pallas kernels: none -> 5.34 us  [the longest x1 3.72 us: last_products(): pl.pallas_call(last_kernel, out_shape=(jax.ShapeDtypeStruct((hidden_width...]
    all_to_all x1 -> x2, starting transfers between devices: 4.06 us -> 9.16 us  [scatter_rows(): came = lax.all_to_all(sent, ROWS, 0, 0, tiled=True)]
    all_gather x2, blocking collectives: 64.3 us -> 68.8 us  [gather_z(): return lax.all_gather(pair.reshape(-1, features), 'z', axis=0, tiled=True)]
    ppermute x4, starting transfers between devices: 33.9 us -> 30.2 us  [swap(): return lax.ppermute(block, axis, SWAP)]
    ppermute x4, waiting for transfers between devices: 14.5 us -> 11 us  [swap(): return lax.ppermute(block, axis, SWAP)]
  transfers between devices with their start and end apart: 8 -> 9, of which waited for: 6 -> 6; matrix products, arithmetic and copies ran while one was open for 8% -> 8% of each run, Pallas kernels for 0% -> 2%
where the time goes in v5:
time: 222 us
  blocking collectives  95.5 us (43%)
  starting transfers between devices  45.5 us (20%)
  waiting for transfers between devices  39.6 us (18%)
  between operations  14.3 us (6%)
  matrix products  9.76 us (4%)
  local copies, waits for them, and re-layouts  8.39 us (4%)
  Pallas kernels  5.34 us (2%)
  other arithmetic  2.97 us (1%)
    all_gather x2, blocking collectives, gather_z(): return lax.all_gather(pair.reshape(-1, features), 'z', axis=0, tiled=True)  68.8 us
    ppermute x4, starting transfers between devices, swap(): return lax.ppermute(block, axis, SWAP)  30.2 us
    all_to_all x1, waiting for transfers between devices, second_half(): came = lax.all_to_all(part, 'z', 0, 0, tiled=True)  15.1 us
    all_to_all x1, blocking collectives, gather_rows(): every = lax.all_to_all(copies, ROWS, 0, 0, tiled=True)  14.2 us
    all_to_all x2, waiting for transfers between devices, scatter_rows(): came = lax.all_to_all(sent, ROWS, 0, 0, tiled=True)  13.4 us
    ppermute x4, waiting for transfers between devices, swap(): return lax.ppermute(block, axis, SWAP)  11 us
    all_to_all x2, starting transfers between devices, scatter_rows(): came = lax.all_to_all(sent, ROWS, 0, 0, tiled=True)  9.16 us
    dot_general x6, matrix products, dot_nt(): lax.dot_general(left, right, (((1,), (1,)), ((), ())), preferred_element_...  7.54 us
  transfers between devices with their start and end apart: 9, of which 6 were waited for; matrix products, arithmetic and copies ran while one was open for 8% of the time, Pallas kernels for 2%

profile of v5, /device:TPU:1, one launch (start us, length us, event | category | flops | bytes accessed | tf_op | source)
XLA Modules:
  0.0 221.5 jit_solution(18302353962814724104)
XLA Ops:
  7.2 1.6 shard_map.133
  8.8 6.1 %all-gather.1 = bf16[4,16,768]{2,1,0:T(8,128)(2,1)S(1)} all-gather(bf16[2,16,768]{2,1,0:T(8,128)(2,1)} %shard_map.133), channel_id=3, replica_groups=mesh['x'=4,'yl'=2,'yh'=2,'z'=16,'c'=2] {'yh'}, dimensions={0}, use_global_device_ids=true | all-gather | bytes 147456 | tf_op jit(solution)/shard_map/all_gather | solution.py:171
  15.7 80.7 %conditional.2 = (bf16[512,768]{1,0:T(8,128)(2,1)}, bf16[512,768]{1,0:T(8,128)(2,1)}, bf16[8,2,64,384]{3,2,1,0:T(8,128)(2,1)S(1)}, bf16[128,384]{1,0:T(8,128)(2,1)S(1)}) conditional(s32[]{:T(128)} %convert_element_type.82, () %tuple.27, (bf16[2,2,16,768]{3,2,1,0:T(8,128)(2,1)S(1)}, bf16[384,768]{1,0:T(8,128)(2,1)}, s32[]{:T(128)}, ...), branch_computations={%region_0.0_spmd, %region_1.3_spmd} | conditional | flops 606093312 | bytes 29276414 | solution.py:195
  15.7 35.5 %all_gather.18 = bf16[512,768]{1,0:T(8,128)(2,1)S(1)} all-gather(bf16[32,768]{1,0:T(8,128)(2,1)S(1)} %bitcast.127), channel_id=1, replica_groups=mesh['x'=4,'yl'=2,'yh'=2,'z'=16,'c'=2] {'z'}, dimensions={0}, use_global_device_ids=true | all-gather | bytes 835584 | tf_op jit(solution)/shard_map/cond/branch_1_fun/all_gather | solution.py:162
  51.2 9.9 %collective-permute-start = (bf16[512,768]{1,0:T(8,128)(2,1)S(1)}, bf16[512,768]{1,0:T(8,128)(2,1)S(1)}, u32[]{:S(2)}, u32[]{:S(2)}) collective-permute-start(bf16[512,768]{1,0:T(8,128)(2,1)S(1)} %all_gather.18), channel_id=1, source_target_pairs={{0,1},{1,0},{2,3},{3,2},{4,5},{5,4},{6,7},{7,6},{8,9},{9,8},{10,11... | collective-permute-start | bytes 2359304 | tf_op jit(solution)/shard_map/cond/branch_1_fun/ppermute | solution.py:142
  61.1 1.7 convolution_convert_fusion.1
  63.9 1.0 copy.67
  64.9 5.1 %all-to-all-start = ((bf16[8,2,64,384]{3,2,1,0:T(8,128)(2,1)}), bf16[8,2,64,384]{3,2,1,0:T(8,128)(2,1)S(1)}, u32[]{:S(2)}, u32[]{:S(2)}) async-start(bf16[8,2,64,384]{3,2,1,0:T(8,128)(2,1)} %copy.67), calls=%async_computation | async-start | bytes 1572864 | tf_op jit(solution)/shard_map/cond/branch_1_fun/all_to_all | solution.py:148
  70.4 11.6 %all-to-all-done = bf16[8,2,64,384]{3,2,1,0:T(8,128)(2,1)S(1)} async-done(((bf16[8,2,64,384]{3,2,1,0:T(8,128)(2,1)}), bf16[8,2,64,384]{3,2,1,0:T(8,128)(2,1)S(1)}, u32[]{:S(2)}, u32[]{:S(2)}) %all-to-all-start) | async-done | bytes 786464 | tf_op jit(solution)/shard_map/cond/branch_1_fun/all_to_all | solution.py:148
  82.2 14.2 %all_to_all.17 = bf16[8,128,384]{2,1,0:T(8,128)(2,1)S(1)} all-to-all(bf16[8,128,384]{2,1,0:T(8,128)(2,1)S(1)} %broadcast_in_dim.0), channel_id=1, replica_groups=mesh['x'=4,'yl'=2,'yh'=2,'z'=16,'c'=2] {'x','yl'}, dimensions={0} | all-to-all | bytes 1572864 | tf_op jit(solution)/shard_map/cond/branch_1_fun/all_to_all | solution.py:168
  97.1 4.4 %collective-permute-start.2 = (bf16[512,768]{1,0:T(8,128)(2,1)S(1)}, bf16[512,768]{1,0:T(8,128)(2,1)}, u32[]{:S(2)}, u32[]{:S(2)}) collective-permute-start(bf16[512,768]{1,0:T(8,128)(2,1)S(1)} %convolution_convert_fusion.4), channel_id=1, source_target_pairs={{0,1},{1,0},{2,3},{3,2},{4,5},{5,4},{6,7},{7,6},{8,9},{9,8},{10,11... | collective-permute-start | bytes 2359304 | tf_op jit(solution)/shard_map/ppermute | solution.py:142
  101.8 1.8 collective-permute-done.2
  103.6 1.7 convert_add_fusion
  105.3 0.8 fusion.8
  106.1 4.2 %collective-permute-start.3 = (bf16[16,16,768]{2,1,0:T(8,128)(2,1)}, bf16[16,16,768]{2,1,0:T(8,128)(2,1)}, u32[]{:S(2)}, u32[]{:S(2)}) collective-permute-start(bf16[16,16,768]{2,1,0:T(8,128)(2,1)} %fusion.8), channel_id=1, source_target_pairs={{0,32},{32,0},{1,33},{33,1},{2,34},{34,2},{3,35},{35,3},{4,36},{36... | collective-permute-start | bytes 1179656 | tf_op jit(solution)/shard_map/ppermute | solution.py:142
  111.1 9.0 %collective-permute-done.3 = bf16[16,16,768]{2,1,0:T(8,128)(2,1)} collective-permute-done((bf16[16,16,768]{2,1,0:T(8,128)(2,1)}, bf16[16,16,768]{2,1,0:T(8,128)(2,1)}, u32[]{:S(2)}, u32[]{:S(2)}) %collective-permute-start.3) | collective-permute-done | bytes 393248 | tf_op jit(solution)/shard_map/ppermute | solution.py:142
  120.1 1.1 fusion.7
  121.3 81.8 %conditional.3 = (bf16[512,768]{1,0:T(8,128)(2,1)}, bf16[512,768]{1,0:T(8,128)(2,1)}, bf16[8,2,64,128]{3,2,1,0:T(8,128)(2,1)}, f32[768,384]{1,0:T(8,128)}) conditional(s32[]{:T(128)} %convert_element_type.82, () %tuple.26, (bf16[16,768]{1,0:T(8,128)(2,1)S(1)}, bf16[16,16,768]{2,1,0:T(8,128)(2,1)S(1)}, bf16[96,768]{1,0:T(8,128)(2,1)S(1)}, s32[]{:T(128)}, ...), branch_computations={%region_3.4_spmd, %region_4.6_spmd} | conditional | flops 806281216 | bytes 22716664 | solution.py:238
  122.1 6.1 %all-to-all-start.2 = ((bf16[16,16,768]{2,1,0:T(8,128)(2,1)}), bf16[16,16,768]{2,1,0:T(8,128)(2,1)S(1)}, u32[]{:S(2)}, u32[]{:S(2)}) async-start(bf16[16,16,768]{2,1,0:T(8,128)(2,1)} %copy-done.6), calls=%async_computation.2 | async-start | bytes 786432 | tf_op jit(solution)/shard_map/cond/branch_1_fun/all_to_all | solution.py:213
  128.2 2.4 %constant_dynamic-slice_fusion = (bf16[16,1,32,768]{3,2,1,0:T(8,128)(2,1)S(1)}, bf16[16,1,32,768]{3,2,1,0:T(8,128)(2,1)}) fusion(bf16[16,2,32,768]{3,2,1,0:T(8,128)(2,1)} %get-tuple-element.34, s32[]{:T(128)S(6)} %select_n.95, s32[]{:T(128)S(6)} %select_n.94), kind=kLoop, calls=%fused_computation.22 | loop fusion | bytes 3145736 | tf_op jit(solution)/shard_map/cond/branch_1_fun/jit(dynamic_index_in_dim)/dynamic_slice | solution.py:215
  130.5 15.1 %all-to-all-done.2 = bf16[16,16,768]{2,1,0:T(8,128)(2,1)S(1)} async-done(((bf16[16,16,768]{2,1,0:T(8,128)(2,1)}), bf16[16,16,768]{2,1,0:T(8,128)(2,1)S(1)}, u32[]{:S(2)}, u32[]{:S(2)}) %all-to-all-start.2) | async-done | bytes 393248 | tf_op jit(solution)/shard_map/cond/branch_1_fun/all_to_all | solution.py:213
  145.8 6.4 %all-gather = bf16[32,768]{1,0:T(8,128)(2,1)S(1)} all-gather(bf16[16,768]{1,0:T(8,128)(2,1)S(1)} %add_convert_fusion), channel_id=2, replica_groups=mesh['x'=4,'yl'=2,'yh'=2,'z'=16,'c'=2] {'yh'}, dimensions={0}, use_global_device_ids=true | all-gather | bytes 73728 | tf_op jit(solution)/shard_map/cond/branch_1_fun/all_gather | solution.py:221
  152.2 33.3 %all_gather.21 = bf16[512,768]{1,0:T(8,128)(2,1)} all-gather(bf16[32,768]{1,0:T(8,128)(2,1)S(1)} %all-gather), channel_id=1, replica_groups=mesh['x'=4,'yl'=2,'yh'=2,'z'=16,'c'=2] {'z'}, dimensions={0}, use_global_device_ids=true | all-gather | bytes 835584 | tf_op jit(solution)/shard_map/cond/branch_1_fun/all_gather | solution.py:162
  185.5 11.6 %collective-permute-start.1 = (bf16[512,768]{1,0:T(8,128)(2,1)}, bf16[512,768]{1,0:T(8,128)(2,1)}, u32[]{:S(2)}, u32[]{:S(2)}) collective-permute-start(bf16[512,768]{1,0:T(8,128)(2,1)} %all_gather.21), channel_id=1, source_target_pairs={{0,1},{1,0},{2,3},{3,2},{4,5},{5,4},{6,7},{7,6},{8,9},{9,8},{10,11... | collective-permute-start | bytes 2359304 | tf_op jit(solution)/shard_map/cond/branch_1_fun/ppermute | solution.py:142
  197.7 1.6 convolution_add_fusion
  199.3 1.5 convolution_convert_fusion.3
  200.8 1.5 convolution_convert_fusion.2
  202.4 0.7 pad_maximum_fusion.1
  203.1 4.1 %all-to-all-start.3 = ((bf16[8,2,64,128]{3,2,1,0:T(8,128)(2,1)}), bf16[8,2,64,128]{3,2,1,0:T(8,128)(2,1)S(1)}, u32[]{:S(2)}, u32[]{:S(2)}) async-start(bf16[8,2,64,128]{3,2,1,0:T(8,128)(2,1)} %get-tuple-element.63), calls=%async_computation.3 | async-start | bytes 524288 | tf_op jit(solution)/shard_map/all_to_all | solution.py:148
  207.2 1.2 copy-done.1
  208.4 3.7 %shard_map.134 = (f32[384,768]{1,0:T(8,128)}, f32[96,768]{1,0:T(8,128)}) custom-call(bf16[8,2,64,512]{3,2,1,0:T(8,128)(2,1)S(1)} %bitcast.101, bf16[512,768]{1,0:T(8,128)(2,1)S(1)} %copy-done.3, bf16[512,768]{1,0:T(8,128)(2,1)} %get-tuple-element.66.grad_other_ref, bf16[512,768]{1,0:T(8,128)(2,1)} %get-tuple-element.67.gs_own_ref, ...), custom_call_target="tpu_custom_call" | custom-call | flops 805306368 | bytes 4194304 | tf_op jit(solution)/shard_map/pallas_call | solution.py:86
  212.1 1.8 all-to-all-done.3
  (72 shorter events, 6.3 us)
Async XLA Ops:
  7.2 89.4 %copy-start = (bf16[768,384]{1,0:T(8,128)(2,1)S(1)}, bf16[768,384]{1,0:T(8,128)(2,1)}, u32[]{:S(2)}) copy-start(bf16[768,384]{1,0:T(8,128)(2,1)} %param.22) | copy-start | bytes 1769476
  7.2 114.1 %all-gather.7.cloned.1.call-start = ((), (), s32[]{:S(2)}) async-start(), calls=%async_computation.4 | async-start | bytes 1622016 | tf_op jit(solution)/shard_map/all_gather | solution.py:172
  15.6 187.5 %all-gather.9.cloned.1.call-start = ((), (), s32[]{:S(2)}) async-start(), calls=%async_computation.5 | async-start | bytes 1179648 | tf_op jit(solution)/shard_map/all_gather | solution.py:209
  15.7 47.3 %copy-start.13 = (bf16[384,768]{1,0:T(8,128)(2,1)S(1)}, bf16[384,768]{1,0:T(8,128)(2,1)}, u32[]{:S(2)}) copy-start(bf16[384,768]{1,0:T(8,128)(2,1)} %get-tuple-element.75) | copy-start | bytes 1769476 | tf_op jit(solution)/shard_map/cond
  51.2 12.5 %copy-start.2 = (bf16[512,768]{1,0:T(8,128)(2,1)}, bf16[512,768]{1,0:T(8,128)(2,1)S(1)}, u32[]{:S(2)}) copy-start(bf16[512,768]{1,0:T(8,128)(2,1)S(1)} %all_gather.18) | copy-start | bytes 2359300 | tf_op jit(solution)/shard_map/cond
  51.2 11.8 %collective-permute-start = (bf16[512,768]{1,0:T(8,128)(2,1)S(1)}, bf16[512,768]{1,0:T(8,128)(2,1)S(1)}, u32[]{:S(2)}, u32[]{:S(2)}) collective-permute-start(bf16[512,768]{1,0:T(8,128)(2,1)S(1)} %all_gather.18), channel_id=1, source_target_pairs={{0,1},{1,0},{2,3},{3,2},{4,5},{5,4},{6,7},{7,6},{8,9},{9,8},{10,11... | collective-permute-start | bytes 2359304 | tf_op jit(solution)/shard_map/cond/branch_1_fun/ppermute | solution.py:142
  63.0 0.9 copy-start.4
  63.9 6.1 %copy-start.8 = (bf16[128,384]{1,0:T(8,128)(2,1)S(1)}, bf16[128,384]{1,0:T(8,128)(2,1)}, u32[]{:S(2)}) copy-start(bf16[128,384]{1,0:T(8,128)(2,1)} %get-tuple-element.106) | copy-start | bytes 294916 | tf_op jit(solution)/shard_map/cond
  63.9 6.2 %copy-start.11 = (f32[128,12]{0,1:T(8,128)S(1)}, f32[128,12]{0,1:T(8,128)}, u32[]{:S(2)}) copy-start(f32[128,12]{0,1:T(8,128)} %get-tuple-element.77) | copy-start | bytes 18436 | tf_op jit(solution)/shard_map/cond
  64.9 17.0 %all-to-all-start = ((bf16[8,2,64,384]{3,2,1,0:T(8,128)(2,1)}), bf16[8,2,64,384]{3,2,1,0:T(8,128)(2,1)S(1)}, u32[]{:S(2)}, u32[]{:S(2)}) async-start(bf16[8,2,64,384]{3,2,1,0:T(8,128)(2,1)} %copy.67), calls=%async_computation | async-start | bytes 1572864 | tf_op jit(solution)/shard_map/cond/branch_1_fun/all_to_all | solution.py:148
  96.4 5.2 %copy-start.10 = (bf16[128,96]{0,1:T(8,128)(2,1)S(1)}, bf16[128,96]{0,1:T(8,128)(2,1)}, u32[]{:S(2)}) copy-start(bf16[128,96]{0,1:T(8,128)(2,1)} %param.15) | copy-start | bytes 73732
  96.5 5.2 %copy-start.12 = (f32[128,3]{0,1:T(4,128)S(1)}, f32[128,3]{0,1:T(4,128)}, u32[]{:S(2)}) copy-start(f32[128,3]{0,1:T(4,128)} %param.16) | copy-start | bytes 4612
  97.1 6.4 %collective-permute-start.2 = (bf16[512,768]{1,0:T(8,128)(2,1)S(1)}, bf16[512,768]{1,0:T(8,128)(2,1)}, u32[]{:S(2)}, u32[]{:S(2)}) collective-permute-start(bf16[512,768]{1,0:T(8,128)(2,1)S(1)} %convolution_convert_fusion.4), channel_id=1, source_target_pairs={{0,1},{1,0},{2,3},{3,2},{4,5},{5,4},{6,7},{7,6},{8,9},{9,8},{10,11... | collective-permute-start | bytes 2359304 | tf_op jit(solution)/shard_map/ppermute | solution.py:142
  105.3 16.0 %copy-start.7 = (bf16[96,768]{1,0:T(8,128)(2,1)S(1)}, bf16[96,768]{1,0:T(8,128)(2,1)}, u32[]{:S(2)}) copy-start(bf16[96,768]{1,0:T(8,128)(2,1)} %param.21) | copy-start | bytes 442372
  105.3 16.0 %copy-start.9 = (bf16[16,768]{1,0:T(8,128)(2,1)S(1)}, bf16[16,768]{1,0:T(8,128)(2,1)}, u32[]{:S(2)}) copy-start(bf16[16,768]{1,0:T(8,128)(2,1)} %grad_ref.1) | copy-start | bytes 73732
  106.1 14.0 %collective-permute-start.3 = (bf16[16,16,768]{2,1,0:T(8,128)(2,1)}, bf16[16,16,768]{2,1,0:T(8,128)(2,1)}, u32[]{:S(2)}, u32[]{:S(2)}) collective-permute-start(bf16[16,16,768]{2,1,0:T(8,128)(2,1)} %fusion.8), channel_id=1, source_target_pairs={{0,32},{32,0},{1,33},{33,1},{2,34},{34,2},{3,35},{35,3},{4,36},{36... | collective-permute-start | bytes 1179656 | tf_op jit(solution)/shard_map/ppermute | solution.py:142
  121.3 85.9 %copy-start.3 = (bf16[512,768]{1,0:T(8,128)(2,1)S(1)}, bf16[512,768]{1,0:T(8,128)(2,1)}, u32[]{:S(2)}) copy-start(bf16[512,768]{1,0:T(8,128)(2,1)} %get-tuple-element.65.grad_own_ref) | copy-start | bytes 2359300
  121.3 0.7 copy-start.6
  122.1 23.6 %all-to-all-start.2 = ((bf16[16,16,768]{2,1,0:T(8,128)(2,1)}), bf16[16,16,768]{2,1,0:T(8,128)(2,1)S(1)}, u32[]{:S(2)}, u32[]{:S(2)}) async-start(bf16[16,16,768]{2,1,0:T(8,128)(2,1)} %copy-done.6), calls=%async_computation.2 | async-start | bytes 786432 | tf_op jit(solution)/shard_map/cond/branch_1_fun/all_to_all | solution.py:213
  145.7 51.4 %copy-start.5 = (bf16[16,1,32,768]{3,2,1,0:T(8,128)(2,1)S(1)}, bf16[16,1,32,768]{3,2,1,0:T(8,128)(2,1)}, u32[]{:S(2)}) copy-start(bf16[16,1,32,768]{3,2,1,0:T(8,128)(2,1)} %get-tuple-element.117) | copy-start | bytes 2359300 | tf_op jit(solution)/shard_map/cond
  185.5 15.4 %collective-permute-start.1 = (bf16[512,768]{1,0:T(8,128)(2,1)}, bf16[512,768]{1,0:T(8,128)(2,1)}, u32[]{:S(2)}, u32[]{:S(2)}) collective-permute-start(bf16[512,768]{1,0:T(8,128)(2,1)} %all_gather.21), channel_id=1, source_target_pairs={{0,1},{1,0},{2,3},{3,2},{4,5},{5,4},{6,7},{7,6},{8,9},{9,8},{10,11... | collective-permute-start | bytes 2359304 | tf_op jit(solution)/shard_map/cond/branch_1_fun/ppermute | solution.py:142
  203.1 10.8 %all-to-all-start.3 = ((bf16[8,2,64,128]{3,2,1,0:T(8,128)(2,1)}), bf16[8,2,64,128]{3,2,1,0:T(8,128)(2,1)S(1)}, u32[]{:S(2)}, u32[]{:S(2)}) async-start(bf16[8,2,64,128]{3,2,1,0:T(8,128)(2,1)} %get-tuple-element.63), calls=%async_computation.3 | async-start | bytes 524288 | tf_op jit(solution)/shard_map/all_to_all | solution.py:148
  207.2 1.2 copy-start.1
Sparse Core Ops, SparseCore 0:
  15.7 77.4 all-gather.6
  121.4 36.5 all-gather.8

commit v6 on v5

v6 whole, which is shorter than its diff:
```python
import jax
import jax.numpy as jnp
from jax import lax
from jax.experimental import pallas as pl
from jax.experimental.pallas import tpu as pltpu
from jax.sharding import Mesh
from jax.sharding import PartitionSpec as P

QBLOCK = 32
PER = 16
ROWS = ("x", "yl")
COLS = ("yh", "z", "c")
SWAP = ((0, 1), (1, 0))


def restore(code, scale):
    count, width = code.shape
    blocks = code.astype(jnp.float32).reshape(count, width // QBLOCK, QBLOCK) * scale[:, :, None]
    return blocks.reshape(count, width).astype(jnp.bfloat16)


def dot_nt(left, right):
    return lax.dot_general(
        left, right, (((1,), (1,)), ((), ())), preferred_element_type=jnp.float32
    )


def dot_tn(left, right):
    return lax.dot_general(
        left, right, (((0,), (0,)), ((), ())), preferred_element_type=jnp.float32
    )


def outgoing_kernel(grad_ref, code_ref, scale_ref, out_ref):
    blocks, width = scale_ref.shape[1], code_ref.shape[1]
    row = lax.broadcasted_iota(jnp.int32, (blocks, width), 0)
    column = lax.broadcasted_iota(jnp.int32, (blocks, width), 1)
    first = row * QBLOCK
    spread = jnp.where((column >= first) & (column < first + QBLOCK), 1.0, 0.0)
    scale = jnp.dot(
        scale_ref[...],
        spread.astype(jnp.float32),
        precision=lax.Precision.HIGHEST,
        preferred_element_type=jnp.float32,
    )
    out_ref[0] = grad_ref[...]
    out_ref[1] = (code_ref[...].astype(jnp.float32) * scale).astype(jnp.bfloat16)


def outgoing(grad_out, code, scale):
    return pl.pallas_call(
        outgoing_kernel,
        out_shape=jax.ShapeDtypeStruct((2,) + grad_out.shape, jnp.bfloat16),
        in_specs=[pl.BlockSpec(memory_space=pltpu.VMEM)] * 3,
        out_specs=pl.BlockSpec(memory_space=pltpu.VMEM),
    )(grad_out, code, scale)


def last_kernel(
    saved_ref, grad_own_ref, grad_other_ref, gs_own_ref, gs_other_ref, down_ref, out_ref, rows_ref
):
    n_rows, _, block, wide = saved_ref.shape
    runs, per = rows_ref.shape[0] * 2 // n_rows, rows_ref.shape[2]
    hidden_width = down_ref.shape[0]
    for side, grad_ref, gs_ref in (
        (0, grad_own_ref, gs_own_ref),
        (1, grad_other_ref, gs_other_ref),
    ):
        for row in range(n_rows):
            half, first = row // (n_rows // 2), row % (n_rows // 2) * runs
            for run in range(runs):
                rows_ref[first + run, half] = saved_ref[row, side, pl.ds(run * per, per), :]
        rows = rows_ref[...].reshape(-1, wide)
        down = dot_tn(rows[:, :hidden_width], grad_ref[...])
        out = dot_tn(rows[:, hidden_width:], gs_ref[...])
        if side == 0:
            down_ref[...] = down
            out_ref[...] = out
        else:
            down_ref[...] += down
            out_ref[...] += out


def last_products(saved_all, grad_own, grad_other, gs_own, gs_other, hidden_width):
    features = grad_own.shape[1]
    return pl.pallas_call(
        last_kernel,
        out_shape=(
            jax.ShapeDtypeStruct((hidden_width, features), jnp.float32),
            jax.ShapeDtypeStruct((saved_all.shape[3] - hidden_width, gs_own.shape[1]), jnp.float32),
        ),
        in_specs=[pl.BlockSpec(memory_space=pltpu.VMEM)] * 5,
        out_specs=(pl.BlockSpec(memory_space=pltpu.VMEM),) * 2,
        scratch_shapes=[
            pltpu.VMEM((grad_own.shape[0] // (2 * PER), 2, PER, saved_all.shape[3]), jnp.bfloat16)
        ],
        compiler_params=pltpu.CompilerParams(vmem_limit_bytes=32 * 2**20),
        cost_estimate=pl.CostEstimate(
            flops=4 * grad_own.size * hidden_width,
            bytes_accessed=8 * grad_own.size + 2 * saved_all.size,
            transcendentals=0,
        ),
    )(saved_all, grad_own, grad_other, gs_own, gs_other)


def local(
    grad_out,
    ctx_code,
    ctx_scale,
    stream_code,
    stream_scale,
    hidden_code,
    hidden_scale,
    out_weight,
    up_weight,
    down_weight,
):
    core, half = lax.axis_index("c"), lax.axis_index("yh")
    n_rows, n_z = lax.axis_size(ROWS), lax.axis_size("z")
    per, features = grad_out.shape
    runs = n_z * 2 // n_rows
    hidden_width, ctx_width = hidden_code.shape[1], ctx_code.shape[1]
    span = features // 2
    padded = ctx_width + -ctx_width % 128

    def own_first(block):
        width = block.shape[1]
        parts = block.reshape(runs, 2, per, width)
        one, two = parts[:, 0], parts[:, 1]
        first = jnp.where(core == 0, one, two)
        second = jnp.where(core == 0, two, one)
        return jnp.stack([first, second]).reshape(block.shape)

    def natural(block):
        width = block.shape[1]
        parts = block.reshape(2, runs, per, width)
        one = jnp.where(core == 0, parts[0], parts[1])
        two = jnp.where(core == 0, parts[1], parts[0])
        return jnp.stack([one, two], axis=1).reshape(block.shape)

    def swap(block, axis):
        return lax.ppermute(block, axis, SWAP)

    def by_half(mine, theirs):
        return jnp.where(half == 0, mine, theirs), jnp.where(half == 0, theirs, mine)

    def columns(block, which):
        return lax.dynamic_slice_in_dim(block, which * span, span, axis=1)

    def by_row(block):
        width = block.shape[1]
        parts = block.reshape(n_rows // 2, runs, 2, per, width)
        return parts.transpose(2, 0, 1, 3, 4).reshape(n_rows, runs * per, width)

    def by_z(block):
        width = block.shape[-1]
        parts = block.reshape(2, n_z, per, width)
        return jnp.swapaxes(parts, 0, 1).reshape(-1, width)

    def summed(came):
        return jnp.sum(came.astype(jnp.float32), axis=0)

    both = lax.all_gather(outgoing(grad_out, stream_code, stream_scale), "yh", axis=0)
    stream_all = lax.all_gather(both[:, 1], ("z", "c"), axis=0)

    def first_half(both):
        context = own_first(restore(ctx_code, ctx_scale))
        grad_own = lax.all_gather(both[:, 0].reshape(-1, features), "z", axis=0, tiled=True)
        grad_other = swap(grad_own, "c")
        up_sent = lax.dynamic_slice_in_dim(up_weight, (1 - half) * span, span, axis=0)
        wide_ctx = jnp.pad(context, ((0, 0), (0, hidden_width - ctx_width)))
        sent = jnp.concatenate([up_sent, columns(out_weight, 1 - half), wide_ctx])
        swapped = swap(sent, "yh")
        sent = jnp.stack(
            [
                by_row(dot_nt(grad_own, down_weight).astype(jnp.bfloat16)),
                by_row(dot_nt(grad_other, down_weight).astype(jnp.bfloat16)),
            ],
            axis=1,
        )
        grad_act = summed(lax.all_to_all(sent, ROWS, 0, 0, tiled=True)).reshape(-1, hidden_width)
        grad_act, swapped = lax.optimization_barrier((grad_act, swapped))
        positive = jnp.maximum(
            own_first(restore(hidden_code, hidden_scale)).astype(jnp.float32), 0.0
        )
        act = (positive * positive).astype(jnp.bfloat16)
        grad_pre = (grad_act * 2.0 * positive).astype(jnp.bfloat16)
        copies = lax.optimization_barrier(
            jnp.broadcast_to(grad_pre[None], (2 * n_rows,) + grad_pre.shape)
        )
        pre_all = lax.all_to_all(copies, ROWS + ("yh",), 0, 0, tiled=True)
        pre_all = pre_all.reshape(n_rows, 2, 2, runs * per, hidden_width)
        return grad_own, grad_other, pre_all, act, context, swapped

    def skip_first(both):
        wide = jnp.zeros((n_z * 2 * per, features), jnp.bfloat16)
        pre_all = jnp.zeros((n_rows, 2, 2, runs * per, hidden_width), jnp.bfloat16)
        act = jnp.zeros(hidden_code.shape, jnp.bfloat16)
        swapped = jnp.zeros((span + ctx_width + act.shape[0], hidden_width), jnp.bfloat16)
        return wide, wide, pre_all, act, jnp.zeros(ctx_code.shape, jnp.bfloat16), swapped

    always = lax.optimization_barrier(jnp.bool_(True))
    grad_own, grad_other, pre_all, act, context, swapped = lax.cond(
        always, first_half, skip_first, both
    )
    up_kept = lax.dynamic_slice_in_dim(up_weight, half * span, span, axis=0)
    up_halves = by_half(up_kept, swapped[:span])
    out_halves = by_half(columns(out_weight, half), swapped[span : span + ctx_width])
    ctx_swapped = swapped[span + ctx_width :, :ctx_width]
    gap = ((0, 0), (0, padded - ctx_width))
    saved = jnp.concatenate([act, jnp.pad(context, gap), jnp.pad(ctx_swapped, gap)], axis=1)
    out_wide = jnp.concatenate(
        [jnp.pad(part, ((0, padded - ctx_width), (0, 0))) for part in out_halves]
    )

    def stream_part(side):
        one = pre_all[:, 0, side].reshape(-1, hidden_width)
        two = pre_all[:, 1, side].reshape(-1, hidden_width)
        return dot_nt(one, up_halves[0]) + dot_nt(two, up_halves[1])

    came = swap(stream_part(1).astype(jnp.bfloat16), "c")
    part = by_z((stream_part(0) + came.astype(jnp.float32)).astype(jnp.bfloat16))
    by_core = stream_all.reshape(n_z, 2, 2 * per, features)
    part, saved, by_core = lax.optimization_barrier((part, saved, by_core))
    saved_all = lax.all_gather(saved, ROWS, axis=0)
    kept_out = columns(both[:, 0].reshape(-1, features), half).astype(jnp.float32)

    def second_half(part, by_core):
        came = lax.all_to_all(part.reshape(n_z, 2 * per, span), "z", 0, 0, tiled=True)
        stream_own = lax.dynamic_index_in_dim(by_core, core, 1, keepdims=False)
        stream_other = lax.dynamic_index_in_dim(by_core, 1 - core, 1, keepdims=False)
        pre = lax.dynamic_index_in_dim(pre_all, half, 1, keepdims=False)
        grad_up = dot_tn(stream_own.reshape(-1, features), by_z(pre[:, 0])) + dot_tn(
            stream_other.reshape(-1, features), by_z(pre[:, 1])
        )
        came, grad_up = lax.optimization_barrier((came, grad_up))
        grad_stream = (kept_out + summed(came)).astype(jnp.bfloat16)
        gs_own = lax.all_gather(grad_stream, "z", axis=0, tiled=True)
        gs_other = swap(gs_own, "c")
        sides = [
            by_row(dot_nt(rows, out_wide).astype(jnp.bfloat16)).reshape(n_rows, -1, 2, padded)
            for rows in (gs_own, gs_other)
        ]
        sent = jnp.stack([jnp.swapaxes(side, 1, 2) for side in sides], axis=2)
        return gs_own, gs_other, sent, grad_up

    def skip_second(part, by_core):
        wide = jnp.zeros((n_z * 2 * per, span), jnp.bfloat16)
        return (
            wide,
            wide,
            jnp.zeros((n_rows, 2, 2, runs * per, padded), jnp.bfloat16),
            jnp.zeros((features, hidden_width), jnp.float32),
        )

    gs_own, gs_other, sent, grad_up = lax.cond(always, second_half, skip_second, part, by_core)
    sent, saved_all = lax.optimization_barrier((sent, saved_all))
    sent = sent.reshape(2 * n_rows, 2, runs * per, padded)
    came = summed(lax.all_to_all(sent, ROWS + ("yh",), 0, 0, tiled=True)).reshape(-1, padded)
    grad_ctx = natural(came[:, :ctx_width].astype(jnp.bfloat16))

    def weights(saved_all):
        grad_down, products = last_products(
            saved_all.reshape(n_rows, 2, -1, saved_all.shape[-1]),
            grad_own,
            grad_other,
            gs_own,
            gs_other,
            hidden_width,
        )
        mine = products[:ctx_width]
        theirs = swap(products[padded : padded + ctx_width], "yh")
        return grad_down, jnp.concatenate(by_half(mine, theirs), axis=1)

    def skip_weights(saved_all):
        return (
            jnp.zeros((hidden_width, features), jnp.float32),
            jnp.zeros((ctx_width, features), jnp.float32),
        )

    grad_down, grad_outw = lax.cond(always, weights, skip_weights, saved_all)
    return (grad_ctx, grad_outw, grad_up, grad_down)


def solution(mesh):
    parts = Mesh(mesh.devices.reshape(4, 2, 2, 16, 2), ROWS + COLS)
    by_cols, by_rows = P(COLS, ROWS), P(ROWS, COLS)
    in_specs = (
        by_cols,
        by_rows,
        by_rows,
        by_cols,
        by_cols,
        by_rows,
        by_rows,
        by_cols,
        by_rows,
        by_cols,
    )
    out_specs = (by_rows, by_cols, by_rows, by_cols)
    return jax.shard_map(local, mesh=parts, in_specs=in_specs, out_specs=out_specs, check_vma=False)
```

time: 222 us -> 237 us (1.068)
  blocking collectives: 95.5 us -> 73.1 us
  waiting for transfers between devices: 39.6 us -> 55.3 us
  starting transfers between devices: 45.5 us -> 57.5 us
  local copies, waits for them, and re-layouts: 8.39 us -> 15.7 us
    all_to_all x1 -> x0, blocking collectives: 14.2 us -> none  [gather_rows(): every = lax.all_to_all(copies, ROWS, 0, 0, tiled=True)]
    all_to_all x3 -> x4, waiting for transfers between devices: 28.5 us -> 38.9 us  [the longest x1 20.1 us: first_half(): pre_all = lax.all_to_all(copies, ROWS + ('yh',), 0, 0, tiled=True)]
    all_gather x3 -> x2, blocking collectives: 75.2 us -> 67 us  [the longest x1 35.5 us: first_half(): lax.all_gather(both[:, 0].reshape(-1, features), 'z', axis=0, tiled=True)]
    all_to_all x3 -> x4, starting transfers between devices: 15.3 us -> 22.3 us  [the longest x1 6.44 us: second_half(): lax.all_to_all(part.reshape(n_z, 2 * per, span), 'z', 0, 0, tiled=True)]
    ppermute x4 -> x5, waiting for transfers between devices: 11 us -> 16.4 us  [swap(): return lax.ppermute(block, axis, SWAP)]
    ppermute x4 -> x5, starting transfers between devices: 30.2 us -> 35.1 us  [swap(): return lax.ppermute(block, axis, SWAP)]
    slice x3 -> x8, local copies, waits for them, and re-layouts: 0.7 us -> 5.56 us  [the longest x1 1.58 us: stream_part(): two = pre_all[:, 1, side].reshape(-1, hidden_width)]
    transpose x0 -> x3, local copies, waits for them, and re-layouts: none -> 2.41 us  [by_z(): return jnp.swapaxes(parts, 0, 1).reshape(-1, width)]
  transfers between devices with their start and end apart: 9 -> 11, of which waited for: 6 -> 7; matrix products, arithmetic and copies ran while one was open for 8% -> 11% of each run, Pallas kernels for 2% -> 2%
where the time goes in v6:
time: 237 us; the launch traced here: 236 us
  blocking collectives  73.1 us (31%)
  starting transfers between devices  57.5 us (24%)
  waiting for transfers between devices  55.3 us (23%)
  local copies, waits for them, and re-layouts  15.7 us (7%)
  between operations  14.2 us (6%)
  matrix products  10.6 us (4%)
  Pallas kernels  5.18 us (2%)
  other arithmetic  3.81 us (2%)
    all_gather x1, blocking collectives, first_half(): lax.all_gather(both[:, 0].reshape(-1, features), 'z', axis=0, tiled=True)  35.5 us
    ppermute x5, starting transfers between devices, swap(): return lax.ppermute(block, axis, SWAP)  35.1 us
    all_gather x1, blocking collectives, second_half(): gs_own = lax.all_gather(grad_stream, 'z', axis=0, tiled=True)  31.5 us
    all_to_all x1, waiting for transfers between devices, first_half(): pre_all = lax.all_to_all(copies, ROWS + ('yh',), 0, 0, tiled=True)  20.1 us
    ppermute x5, waiting for transfers between devices, swap(): return lax.ppermute(block, axis, SWAP)  16.4 us
    all_to_all x1, waiting for transfers between devices, second_half(): lax.all_to_all(part.reshape(n_z, 2 * per, span), 'z', 0, 0, tiled=True)  11 us
    dot_general x8, matrix products, dot_nt(): lax.dot_general(left, right, (((1,), (1,)), ((), ())), preferred_element_...  8.36 us
    all_to_all x1, waiting for transfers between devices, first_half(): lax.all_to_all(sent, ROWS, 0, 0, tiled=True)  7.77 us
  transfers between devices with their start and end apart: 11, of which 7 were waited for; matrix products, arithmetic and copies ran while one was open for 11% of the time, Pallas kernels for 2%

profile of v6, /device:TPU:1, one launch (start us, length us, event | category | flops | bytes accessed | tf_op | source)
XLA Modules:
  0.0 235.9 jit_solution(18431435274449504407)
XLA Ops:
  7.2 1.6 shard_map.134
  8.8 6.1 %all-gather = bf16[4,16,768]{2,1,0:T(8,128)(2,1)S(1)} all-gather(bf16[2,16,768]{2,1,0:T(8,128)(2,1)} %shard_map.134), channel_id=2, replica_groups=mesh['x'=4,'yl'=2,'yh'=2,'z'=16,'c'=2] {'yh'}, dimensions={0}, use_global_device_ids=true | all-gather | bytes 147456 | tf_op jit(solution)/shard_map/all_gather | solution.py:163
  15.6 108.3 %conditional.3 = (bf16[512,768]{1,0:T(8,128)(2,1)S(1)}, bf16[512,768]{1,0:T(8,128)(2,1)S(1)}, bf16[8,2,2,64,384]{4,3,2,1,0:T(8,128)(2,1)}, bf16[128,384]{1,0:T(8...) conditional(s32[]{:T(128)} %convert_element_type.72, () %tuple.41, ...), branch_computations={%region_0.0_spmd, %region_1.3_spmd} | conditional | flops 608022528 | bytes 46620712 | solution.py:203
  15.7 35.5 %all_gather.14 = bf16[512,768]{1,0:T(8,128)(2,1)S(1)} all-gather(bf16[32,768]{1,0:T(8,128)(2,1)S(1)} %bitcast.128), channel_id=1, replica_groups=mesh['x'=4,'yl'=2,'yh'=2,'z'=16,'c'=2] {'z'}, dimensions={0}, use_global_device_ids=true | all-gather | bytes 835584 | tf_op jit(solution)/shard_map/cond/branch_1_fun/all_gather | solution.py:168
  51.2 9.8 %collective-permute-start.1 = (bf16[512,768]{1,0:T(8,128)(2,1)S(1)}, bf16[512,768]{1,0:T(8,128)(2,1)S(1)}, u32[]{:S(2)}, u32[]{:S(2)}) collective-permute-start(bf16[512,768]{1,0:T(8,128)(2,1)S(1)} %all_gather.14), channel_id=1, source_target_pairs={{0,1},{1,0},{2,3},{3,2},{4,5},{5,4},{6,7},{7,6},{8,9},{9,8},{10,11... | collective-permute-start | bytes 2359304 | tf_op jit(solution)/shard_map/cond/branch_1_fun/ppermute | solution.py:142
  61.8 1.7 convolution_convert_fusion.1
  65.5 5.2 %all-to-all-start = ((bf16[8,2,64,384]{3,2,1,0:T(8,128)(2,1)}), bf16[8,2,64,384]{3,2,1,0:T(8,128)(2,1)S(1)}, u32[]{:S(2)}, u32[]{:S(2)}) async-start(bf16[8,2,64,384]{3,2,1,0:T(8,128)(2,1)} %copy.64), calls=%async_computation | async-start | bytes 1572864 | tf_op jit(solution)/shard_map/cond/branch_1_fun/all_to_all | solution.py:181
  70.8 4.6 %collective-permute-start.2 = (bf16[608,384]{1,0:T(8,128)(2,1)S(1)}, bf16[608,384]{1,0:T(8,128)(2,1)}, u32[]{:S(2)}, u32[]{:S(2)}) collective-permute-start(bf16[608,384]{1,0:T(8,128)(2,1)S(1)} %fusion.1), channel_id=1, source_target_pairs={{0,32},{32,0},{1,33},{33,1},{2,34},{34,2},{3,35},{35,3},{4,36},{36... | collective-permute-start | bytes 1400840 | tf_op jit(solution)/shard_map/cond/branch_1_fun/ppermute | solution.py:142
  75.8 7.8 %all-to-all-done = bf16[8,2,64,384]{3,2,1,0:T(8,128)(2,1)S(1)} async-done(((bf16[8,2,64,384]{3,2,1,0:T(8,128)(2,1)}), bf16[8,2,64,384]{3,2,1,0:T(8,128)(2,1)S(1)}, u32[]{:S(2)}, u32[]{:S(2)}) %all-to-all-start) | async-done | bytes 786464 | tf_op jit(solution)/shard_map/cond/branch_1_fun/all_to_all | solution.py:181
  83.6 9.3 %collective-permute-done.2 = bf16[608,384]{1,0:T(8,128)(2,1)} collective-permute-done((bf16[608,384]{1,0:T(8,128)(2,1)S(1)}, bf16[608,384]{1,0:T(8,128)(2,1)}, u32[]{:S(2)}, u32[]{:S(2)}) %collective-permute-start.2) | collective-permute-done | bytes 466976 | tf_op jit(solution)/shard_map/cond/branch_1_fun/ppermute | solution.py:142
  93.0 1.3 broadcast_in_dim.0
  94.3 5.5 %all-to-all-start.1 = ((bf16[16,128,384]{2,1,0:T(8,128)(2,1)}), bf16[16,128,384]{2,1,0:T(8,128)(2,1)}, u32[]{:S(2)}, u32[]{:S(2)}) async-start(bf16[16,128,384]{2,1,0:T(8,128)(2,1)} %broadcast_in_dim.0), calls=%async_computation.1 | async-start | bytes 3145728 | tf_op jit(solution)/shard_map/cond/branch_1_fun/all_to_all | solution.py:191
  99.9 1.4 slice.66
  103.9 20.1 %all-to-all-done.1 = bf16[16,128,384]{2,1,0:T(8,128)(2,1)} async-done(((bf16[16,128,384]{2,1,0:T(8,128)(2,1)}), bf16[16,128,384]{2,1,0:T(8,128)(2,1)}, u32[]{:S(2)}, u32[]{:S(2)}) %all-to-all-start.1) | async-done | bytes 1572896 | tf_op jit(solution)/shard_map/cond/branch_1_fun/all_to_all | solution.py:191
  124.0 1.6 fusion.17
  126.0 1.2 fusion.6
  127.2 3.6 %collective-permute-start.4 = (bf16[512,384]{1,0:T(8,128)(2,1)}, bf16[512,384]{1,0:T(8,128)(2,1)}, u32[]{:S(2)}, u32[]{:S(2)}) collective-permute-start(bf16[512,384]{1,0:T(8,128)(2,1)} %fusion.6), channel_id=1, source_target_pairs={{0,1},{1,0},{2,3},{3,2},{4,5},{5,4},{6,7},{7,6},{8,9},{9,8},{10,11... | collective-permute-start | bytes 1179656 | tf_op jit(solution)/shard_map/ppermute | solution.py:142
  132.5 1.5 add_convert_fusion.1
  134.9 72.4 %conditional.4 = (bf16[512,384]{1,0:T(8,128)(2,1)}, bf16[512,384]{1,0:T(8,128)(2,1)}, bf16[8,2,2,64,128]{4,1,3,0,2:T(2,128)(2,1)S(1)}, f32[768,384]{1,0:T(8,128)}) conditional(s32[]{:T(128)} %convert_element_type.72, () %tuple.40, (bf16[512,384]{1,0:T(8,128)(2,1)}, s32[]{:T(128)}, bf16[16,2,32,768]{3,2,1,0:T(8,128)(2,1)}, s32[]{:T(128)}, ...), branch_computations={%region_3.4_spmd, %region_4.6_spmd} | conditional | flops 806531072 | bytes 31785272 | solution.py:256
  134.9 6.4 %all-to-all-start.2 = ((bf16[16,32,384]{2,1,0:T(8,128)(2,1)}), bf16[16,32,384]{2,1,0:T(8,128)(2,1)}, u32[]{:S(2)}, u32[]{:S(2)}) async-start(bf16[16,32,384]{2,1,0:T(8,128)(2,1)} %bitcast.19), calls=%async_computation.2 | async-start | bytes 786432 | tf_op jit(solution)/shard_map/cond/branch_1_fun/all_to_all | solution.py:229
  141.3 1.2 dynamic-slice_bitcast_fusion
  145.9 1.6 convolution_add_fusion
  147.5 11.0 %all-to-all-done.2 = bf16[16,32,384]{2,1,0:T(8,128)(2,1)} async-done(((bf16[16,32,384]{2,1,0:T(8,128)(2,1)}), bf16[16,32,384]{2,1,0:T(8,128)(2,1)}, u32[]{:S(2)}, u32[]{:S(2)}) %all-to-all-start.2) | async-done | bytes 393248 | tf_op jit(solution)/shard_map/cond/branch_1_fun/all_to_all | solution.py:229
  159.6 31.5 %all_gather.15 = bf16[512,384]{1,0:T(8,128)(2,1)} all-gather(bf16[32,384]{1,0:T(8,128)(2,1)S(1)} %add_convert_fusion), channel_id=1, replica_groups=mesh['x'=4,'yl'=2,'yh'=2,'z'=16,'c'=2] {'z'}, dimensions={0}, use_global_device_ids=true | all-gather | bytes 417792 | tf_op jit(solution)/shard_map/cond/branch_1_fun/all_gather | solution.py:238
  191.1 12.4 %collective-permute-start.3 = (bf16[512,384]{1,0:T(8,128)(2,1)}, bf16[512,384]{1,0:T(8,128)(2,1)}, u32[]{:S(2)}, u32[]{:S(2)}) collective-permute-start(bf16[512,384]{1,0:T(8,128)(2,1)} %all_gather.15), channel_id=1, source_target_pairs={{0,1},{1,0},{2,3},{3,2},{4,5},{5,4},{6,7},{7,6},{8,9},{9,8},{10,11... | collective-permute-start | bytes 1179656 | tf_op jit(solution)/shard_map/cond/branch_1_fun/ppermute | solution.py:142
  203.5 1.3 convolution_convert_fusion.3
  205.1 1.3 convolution_convert_fusion.2
  208.2 5.2 %all-to-all-start.3 = ((bf16[16,2,64,128]{3,2,1,0:T(8,128)(2,1)}), bf16[16,2,64,128]{3,2,1,0:T(8,128)(2,1)S(1)}, u32[]{:S(2)}, u32[]{:S(2)}) async-start(bf16[16,2,64,128]{3,2,1,0:T(8,128)(2,1)} %bitcast.49), calls=%async_computation.3 | async-start | bytes 1048576 | tf_op jit(solution)/shard_map/all_to_all | solution.py:259
  213.4 14.8 %conditional.5 = (f32[384,768]{1,0:T(8,128)}, f32[96,768]{1,0:T(8,128)S(1)}) conditional(s32[]{:T(128)} %convert_element_type.72, () %tuple.46, (bf16[8,128,640]{2,1,0:T(8,128)(2,1)}, bf16[512,768]{1,0:T(8,128)(2,1)S(1)}, bf16[512,768]{1,0:T(8,128)(2,1)S(1)}, bf16[512,384]{1,0:T(8,128)(2,1)}, bf16[512,384]{1,0:T(8,128)(2,1)}, ...), branch_computations={%region_7.8_spmd, %region_8.9_spmd} | conditional | flops 604127232 | bytes 6520898 | solution.py:281
  213.4 3.6 %branch_1_fun.1 = (f32[384,768]{1,0:T(8,128)}, f32[256,384]{1,0:T(8,128)S(1)}) custom-call(bf16[8,2,64,640]{3,2,1,0:T(8,128)(2,1)} %bitcast.115, bf16[512,768]{1,0:T(8,128)(2,1)S(1)} %get-tuple-element.73.grad_own_ref, bf16[512,768]{1,0:T(8,128)(2,1)S(1)} %get-tuple-element.74.grad_other_ref, bf16[512,384]{1,0:T(8,128)(2,1)} %get-tuple-element.75.gs_own_ref, ...), custom_call_target="tpu_custom_call" | custom-call | flops 603979776 | bytes 4456448 | tf_op jit(solution)/shard_map/cond/branch_1_fun/pallas_call | solution.py:86
  217.0 4.8 %collective-permute-start = (f32[96,384]{1,0:T(8,128)S(1)}, f32[96,384]{1,0:T(8,128)S(1)}, u32[]{:S(2)}, u32[]{:S(2)}) collective-permute-start(f32[96,384]{1,0:T(8,128)S(1)} %slice.71), channel_id=1, source_target_pairs={{0,32},{32,0},{1,33},{33,1},{2,34},{34,2},{3,35},{35,3},{4,36},{36... | collective-permute-start | bytes 442376 | tf_op jit(solution)/shard_map/cond/branch_1_fun/ppermute | solution.py:142
  221.8 6.3 %collective-permute-done = f32[96,384]{1,0:T(8,128)S(1)} collective-permute-done((f32[96,384]{1,0:T(8,128)S(1)}, f32[96,384]{1,0:T(8,128)S(1)}, u32[]{:S(2)}, u32[]{:S(2)}) %collective-permute-start) | collective-permute-done | bytes 147488 | tf_op jit(solution)/shard_map/cond/branch_1_fun/ppermute | solution.py:142
  (93 shorter events, 17.0 us)
Async XLA Ops:
  7.2 127.6 %all-gather.6.cloned.1.call-start = ((), (), s32[]{:S(2)}) async-start(), calls=%async_computation.4 | async-start | bytes 1622016 | tf_op jit(solution)/shard_map/all_gather | solution.py:164
  15.6 191.8 %all-gather.8.cloned.1.call-start = ((), (), s32[]{:S(2)}) async-start(), calls=%async_computation.5 | async-start | bytes 1474560 | tf_op jit(solution)/shard_map/all_gather | solution.py:225
  51.2 13.1 %copy-start.2 = (bf16[512,768]{1,0:T(8,128)(2,1)}, bf16[512,768]{1,0:T(8,128)(2,1)S(1)}, u32[]{:S(2)}) copy-start(bf16[512,768]{1,0:T(8,128)(2,1)S(1)} %all_gather.14) | copy-start | bytes 2359300 | tf_op jit(solution)/shard_map/cond
  51.2 12.4 %copy-start.11 = (bf16[96,768]{1,0:T(8,128)(2,1)S(1)}, bf16[96,768]{1,0:T(8,128)(2,1)}, u32[]{:S(2)}) copy-start(bf16[96,768]{1,0:T(8,128)(2,1)} %get-tuple-element.55) | copy-start | bytes 442372 | tf_op jit(solution)/shard_map/cond
  51.2 12.5 %copy-start.14 = (bf16[384,768]{1,0:T(8,128)(2,1)S(1)}, bf16[384,768]{1,0:T(8,128)(2,1)}, u32[]{:S(2)}) copy-start(bf16[384,768]{1,0:T(8,128)(2,1)} %get-tuple-element.127) | copy-start | bytes 1769476 | tf_op jit(solution)/shard_map/cond
  51.2 12.5 %collective-permute-start.1 = (bf16[512,768]{1,0:T(8,128)(2,1)S(1)}, bf16[512,768]{1,0:T(8,128)(2,1)S(1)}, u32[]{:S(2)}, u32[]{:S(2)}) collective-permute-start(bf16[512,768]{1,0:T(8,128)(2,1)S(1)} %all_gather.14), channel_id=1, source_target_pairs={{0,1},{1,0},{2,3},{3,2},{4,5},{5,4},{6,7},{7,6},{8,9},{9,8},{10,11... | collective-permute-start | bytes 2359304 | tf_op jit(solution)/shard_map/cond/branch_1_fun/ppermute | solution.py:142
  63.6 0.9 copy-start.4
  64.5 6.2 %copy-start.1 = (bf16[768,384]{1,0:T(8,128)(2,1)S(1)}, bf16[768,384]{1,0:T(8,128)(2,1)}, u32[]{:S(2)}) copy-start(bf16[768,384]{1,0:T(8,128)(2,1)} %get-tuple-element.53) | copy-start | bytes 1769476 | tf_op jit(solution)/shard_map/cond
  65.5 9.9 %copy-start.12 = (bf16[128,384]{1,0:T(8,128)(2,1)S(1)}, bf16[128,384]{1,0:T(8,128)(2,1)}, u32[]{:S(2)}) copy-start(bf16[128,384]{1,0:T(8,128)(2,1)} %get-tuple-element.185) | copy-start | bytes 294916 | tf_op jit(solution)/shard_map/cond
  65.5 10.1 %copy-start.13 = (f32[128,12]{0,1:T(8,128)S(1)}, f32[128,12]{0,1:T(8,128)}, u32[]{:S(2)}) copy-start(f32[128,12]{0,1:T(8,128)} %get-tuple-element.131) | copy-start | bytes 18436 | tf_op jit(solution)/shard_map/cond
  65.5 18.0 %all-to-all-start = ((bf16[8,2,64,384]{3,2,1,0:T(8,128)(2,1)}), bf16[8,2,64,384]{3,2,1,0:T(8,128)(2,1)S(1)}, u32[]{:S(2)}, u32[]{:S(2)}) async-start(bf16[8,2,64,384]{3,2,1,0:T(8,128)(2,1)} %copy.64), calls=%async_computation | async-start | bytes 1572864 | tf_op jit(solution)/shard_map/cond/branch_1_fun/all_to_all | solution.py:181
  70.8 22.1 %collective-permute-start.2 = (bf16[608,384]{1,0:T(8,128)(2,1)S(1)}, bf16[608,384]{1,0:T(8,128)(2,1)}, u32[]{:S(2)}, u32[]{:S(2)}) collective-permute-start(bf16[608,384]{1,0:T(8,128)(2,1)S(1)} %fusion.1), channel_id=1, source_target_pairs={{0,32},{32,0},{1,33},{33,1},{2,34},{34,2},{3,35},{35,3},{4,36},{36... | collective-permute-start | bytes 1400840 | tf_op jit(solution)/shard_map/cond/branch_1_fun/ppermute | solution.py:142
  94.3 29.6 %copy-start.3 = (bf16[512,768]{1,0:T(8,128)(2,1)S(1)}, bf16[512,768]{1,0:T(8,128)(2,1)}, u32[]{:S(2)}) copy-start(bf16[512,768]{1,0:T(8,128)(2,1)} %copy-done.2) | copy-start | bytes 2359300 | tf_op jit(solution)/shard_map/cond
  94.3 29.6 %copy-start.5 = (bf16[512,768]{1,0:T(8,128)(2,1)S(1)}, bf16[512,768]{1,0:T(8,128)(2,1)}, u32[]{:S(2)}) copy-start(bf16[512,768]{1,0:T(8,128)(2,1)} %copy-done.4) | copy-start | bytes 2359300 | tf_op jit(solution)/shard_map/cond
  94.3 29.6 %all-to-all-start.1 = ((bf16[16,128,384]{2,1,0:T(8,128)(2,1)}), bf16[16,128,384]{2,1,0:T(8,128)(2,1)}, u32[]{:S(2)}, u32[]{:S(2)}) async-start(bf16[16,128,384]{2,1,0:T(8,128)(2,1)} %broadcast_in_dim.0), calls=%async_computation.1 | async-start | bytes 3145728 | tf_op jit(solution)/shard_map/cond/branch_1_fun/all_to_all | solution.py:191
  124.0 1.6 copy-start
  127.2 5.3 %collective-permute-start.4 = (bf16[512,384]{1,0:T(8,128)(2,1)}, bf16[512,384]{1,0:T(8,128)(2,1)}, u32[]{:S(2)}, u32[]{:S(2)}) collective-permute-start(bf16[512,384]{1,0:T(8,128)(2,1)} %fusion.6), channel_id=1, source_target_pairs={{0,1},{1,0},{2,3},{3,2},{4,5},{5,4},{6,7},{7,6},{8,9},{9,8},{10,11... | collective-permute-start | bytes 1179656 | tf_op jit(solution)/shard_map/ppermute | solution.py:142
  132.5 2.3 copy-start.10
  134.9 23.7 %all-to-all-start.2 = ((bf16[16,32,384]{2,1,0:T(8,128)(2,1)}), bf16[16,32,384]{2,1,0:T(8,128)(2,1)}, u32[]{:S(2)}, u32[]{:S(2)}) async-start(bf16[16,32,384]{2,1,0:T(8,128)(2,1)} %bitcast.19), calls=%async_computation.2 | async-start | bytes 786432 | tf_op jit(solution)/shard_map/cond/branch_1_fun/all_to_all | solution.py:229
  142.6 1.7 copy-start.6
  144.3 1.0 copy-start.8
  144.4 1.5 copy-start.7
  191.1 14.0 %collective-permute-start.3 = (bf16[512,384]{1,0:T(8,128)(2,1)}, bf16[512,384]{1,0:T(8,128)(2,1)}, u32[]{:S(2)}, u32[]{:S(2)}) collective-permute-start(bf16[512,384]{1,0:T(8,128)(2,1)} %all_gather.15), channel_id=1, source_target_pairs={{0,1},{1,0},{2,3},{3,2},{4,5},{5,4},{6,7},{7,6},{8,9},{9,8},{10,11... | collective-permute-start | bytes 1179656 | tf_op jit(solution)/shard_map/cond/branch_1_fun/ppermute | solution.py:142
  208.2 19.9 %all-to-all-start.3 = ((bf16[16,2,64,128]{3,2,1,0:T(8,128)(2,1)}), bf16[16,2,64,128]{3,2,1,0:T(8,128)(2,1)S(1)}, u32[]{:S(2)}, u32[]{:S(2)}) async-start(bf16[16,2,64,128]{3,2,1,0:T(8,128)(2,1)} %bitcast.49), calls=%async_computation.3 | async-start | bytes 1048576 | tf_op jit(solution)/shard_map/all_to_all | solution.py:259
  217.0 11.1 %collective-permute-start = (f32[96,384]{1,0:T(8,128)S(1)}, f32[96,384]{1,0:T(8,128)S(1)}, u32[]{:S(2)}, u32[]{:S(2)}) collective-permute-start(f32[96,384]{1,0:T(8,128)S(1)} %slice.71), channel_id=1, source_target_pairs={{0,32},{32,0},{1,33},{33,1},{2,34},{34,2},{3,35},{35,3},{4,36},{36... | collective-permute-start | bytes 442376 | tf_op jit(solution)/shard_map/cond/branch_1_fun/ppermute | solution.py:142
  228.2 0.9 copy-start.9
Sparse Core Ops, SparseCore 0:
  15.7 77.4 all-gather.5
  134.9 38.4 all-gather.7

commit v7 on v5

--- a/solution.py
+++ b/solution.py
@@ -199,12 +199,20 @@
     pre_own = by_z(grad_pre_all[:, 0])
     pre_other = by_z(grad_pre_all[:, 1])
 
-    came = swap(dot_nt(pre_other, up_weight).astype(jnp.bfloat16), "c")
-    part = (dot_nt(pre_own, up_weight) + came.astype(jnp.float32)).reshape(n_z, 2, per, features)
-    keep = lax.dynamic_index_in_dim(part, half, 1, keepdims=False)
-    send = lax.dynamic_index_in_dim(part, 1 - half, 1, keepdims=False).astype(jnp.bfloat16)
+    rows_own = grad_pre_all[:, 0].reshape(2, -1, hidden_width)
+    came = swap(
+        dot_nt(grad_pre_all[:, 1].reshape(-1, hidden_width), up_weight).astype(jnp.bfloat16), "c"
+    ).reshape(2, -1, features)
+
+    def stream_part(which):
+        rows = lax.dynamic_index_in_dim(rows_own, which, 0, keepdims=False)
+        other = lax.dynamic_index_in_dim(came, which, 0, keepdims=False)
+        return dot_nt(rows, up_weight) + other.astype(jnp.float32)
+
+    received = swap(stream_part(1 - half).astype(jnp.bfloat16), "yh")
     by_core = stream_all.reshape(n_z, 2, 2 * per, features)
-    part = (keep + swap(send, "yh").astype(jnp.float32)).astype(jnp.bfloat16)
+    part = (stream_part(half) + received.astype(jnp.float32)).astype(jnp.bfloat16)
+    part = part.reshape(n_z, per, features)
     part, saved, by_core = lax.optimization_barrier((part, saved, by_core))
     saved_all = lax.all_gather(saved, ROWS, axis=0)
     padded_out = jnp.pad(out_weight, ((0, -ctx_width % 128), (0, 0)))
@@ -216,6 +224,7 @@
         stream_own = stream_own.reshape(-1, features)
         stream_other = stream_other.reshape(-1, features)
         grad_up = dot_tn(stream_own, pre_own) + dot_tn(stream_other, pre_other)
+        came, grad_up = lax.optimization_barrier((came, grad_up))
         summed = jnp.sum(came.astype(jnp.float32), axis=0)
         grad_stream = (grad_out.astype(jnp.float32) + summed).astype(jnp.bfloat16)
         gs_own = gather_z(lax.all_gather(grad_stream, "yh", axis=0))

time: 222 us -> 223 us (level)
  waiting for transfers between devices: 39.6 us -> 35.8 us
  local copies, waits for them, and re-layouts: 8.39 us -> 11.1 us
    all_to_all x1, waiting for transfers between devices: 15.1 us -> 11.7 us  [second_half(): came = lax.all_to_all(part, 'z', 0, 0, tiled=True)]
    dot_general x6 -> x7, matrix products: 7.54 us -> 9.27 us  [dot_nt(): lax.dot_general(left, right, (((1,), (1,)), ((), ())), preferred_element_...]
  transfers between devices with their start and end apart: 9 -> 9, of which waited for: 6 -> 7; matrix products, arithmetic and copies ran while one was open for 8% -> 9% of each run, Pallas kernels for 2% -> 2%
where the time goes in v7:
time: 223 us; the launch traced here: 222 us
  blocking collectives  95 us (43%)
  starting transfers between devices  46.5 us (21%)
  waiting for transfers between devices  35.8 us (16%)
  between operations  14.2 us (6%)
  matrix products  11.5 us (5%)
  local copies, waits for them, and re-layouts  11.1 us (5%)
  Pallas kernels  5.1 us (2%)
  other arithmetic  2.4 us (1%)
    all_gather x2, blocking collectives, gather_z(): return lax.all_gather(pair.reshape(-1, features), 'z', axis=0, tiled=True)  68.3 us
    ppermute x4, starting transfers between devices, swap(): return lax.ppermute(block, axis, SWAP)  30.6 us
    all_to_all x1, blocking collectives, gather_rows(): every = lax.all_to_all(copies, ROWS, 0, 0, tiled=True)  14.2 us
    all_to_all x2, waiting for transfers between devices, scatter_rows(): came = lax.all_to_all(sent, ROWS, 0, 0, tiled=True)  12.8 us
    all_to_all x1, waiting for transfers between devices, second_half(): came = lax.all_to_all(part, 'z', 0, 0, tiled=True)  11.7 us
    ppermute x4, waiting for transfers between devices, swap(): return lax.ppermute(block, axis, SWAP)  11.1 us
    all_to_all x2, starting transfers between devices, scatter_rows(): came = lax.all_to_all(sent, ROWS, 0, 0, tiled=True)  9.3 us
    dot_general x7, matrix products, dot_nt(): lax.dot_general(left, right, (((1,), (1,)), ((), ())), preferred_element_...  9.27 us
  transfers between devices with their start and end apart: 9, of which 7 were waited for; matrix products, arithmetic and copies ran while one was open for 9% of the time, Pallas kernels for 2%

profile of v7, /device:TPU:1, one launch (start us, length us, event | category | flops | bytes accessed | tf_op | source)
XLA Modules:
  0.0 221.8 jit_solution(5385217702041203084)
XLA Ops:
  7.2 1.6 shard_map.133
  8.8 6.1 %all-gather.1 = bf16[4,16,768]{2,1,0:T(8,128)(2,1)S(1)} all-gather(bf16[2,16,768]{2,1,0:T(8,128)(2,1)} %shard_map.133), channel_id=3, replica_groups=mesh['x'=4,'yl'=2,'yh'=2,'z'=16,'c'=2] {'yh'}, dimensions={0}, use_global_device_ids=true | all-gather | bytes 147456 | tf_op jit(solution)/shard_map/all_gather | solution.py:171
  15.7 82.3 %conditional.2 = (bf16[512,768]{1,0:T(8,128)(2,1)S(1)}, bf16[512,768]{1,0:T(8,128)(2,1)S(1)}, bf16[128,384]{1,0:T(8,128)(2,1)S(1)}, bf16[8,2,64,384]{3,2,0,1:T(8...) conditional(s32[]{:T(128)} %convert_element_type.88, () %tuple.28, ...), branch_computations={%region_0.0_spmd, %region_1.3_spmd} | conditional | flops 606093312 | bytes 38713668 | solution.py:195
  15.7 35.5 %all_gather.18 = bf16[512,768]{1,0:T(8,128)(2,1)S(1)} all-gather(bf16[32,768]{1,0:T(8,128)(2,1)S(1)} %bitcast.135), channel_id=1, replica_groups=mesh['x'=4,'yl'=2,'yh'=2,'z'=16,'c'=2] {'z'}, dimensions={0}, use_global_device_ids=true | all-gather | bytes 835584 | tf_op jit(solution)/shard_map/cond/branch_1_fun/all_gather | solution.py:162
  51.2 9.7 %collective-permute-start.1 = (bf16[512,768]{1,0:T(8,128)(2,1)S(1)}, bf16[512,768]{1,0:T(8,128)(2,1)S(1)}, u32[]{:S(2)}, u32[]{:S(2)}) collective-permute-start(bf16[512,768]{1,0:T(8,128)(2,1)S(1)} %all_gather.18), channel_id=1, source_target_pairs={{0,1},{1,0},{2,3},{3,2},{4,5},{5,4},{6,7},{7,6},{8,9},{9,8},{10,11... | collective-permute-start | bytes 2359304 | tf_op jit(solution)/shard_map/cond/branch_1_fun/ppermute | solution.py:142
  60.8 1.7 convolution_convert_fusion.1
  63.7 1.0 copy.66
  64.7 5.2 %all-to-all-start.1 = ((bf16[8,2,64,384]{3,2,1,0:T(8,128)(2,1)}), bf16[8,2,64,384]{3,2,1,0:T(8,128)(2,1)S(1)}, u32[]{:S(2)}, u32[]{:S(2)}) async-start(bf16[8,2,64,384]{3,2,1,0:T(8,128)(2,1)} %copy.66), calls=%async_computation.1 | async-start | bytes 1572864 | tf_op jit(solution)/shard_map/cond/branch_1_fun/all_to_all | solution.py:148
  70.3 11.6 %all-to-all-done.1 = bf16[8,2,64,384]{3,2,1,0:T(8,128)(2,1)S(1)} async-done(((bf16[8,2,64,384]{3,2,1,0:T(8,128)(2,1)}), bf16[8,2,64,384]{3,2,1,0:T(8,128)(2,1)S(1)}, u32[]{:S(2)}, u32[]{:S(2)}) %all-to-all-start.1) | async-done | bytes 786464 | tf_op jit(solution)/shard_map/cond/branch_1_fun/all_to_all | solution.py:148
  82.1 14.2 %all_to_all.17 = bf16[8,128,384]{2,1,0:T(8,128)(2,1)S(1)} all-to-all(bf16[8,128,384]{2,1,0:T(8,128)(2,1)S(1)} %broadcast_in_dim.0), channel_id=1, replica_groups=mesh['x'=4,'yl'=2,'yh'=2,'z'=16,'c'=2] {'x','yl'}, dimensions={0} | all-to-all | bytes 1572864 | tf_op jit(solution)/shard_map/cond/branch_1_fun/all_to_all | solution.py:168
  96.4 1.0 copy.83
  98.0 1.5 convolution_convert_fusion.4
  99.5 4.4 %collective-permute-start.2 = (bf16[512,768]{1,0:T(8,128)(2,1)}, bf16[512,768]{1,0:T(8,128)(2,1)}, u32[]{:S(2)}, u32[]{:S(2)}) collective-permute-start(bf16[512,768]{1,0:T(8,128)(2,1)} %convolution_convert_fusion.4), channel_id=1, source_target_pairs={{0,1},{1,0},{2,3},{3,2},{4,5},{5,4},{6,7},{7,6},{8,9},{9,8},{10,11... | collective-permute-start | bytes 2359304 | tf_op jit(solution)/shard_map/ppermute | solution.py:142
  104.2 1.9 collective-permute-done.2
  106.1 2.1 fusion.7
  108.3 4.6 %collective-permute-start.3 = (bf16[256,768]{1,0:T(8,128)(2,1)}, bf16[256,768]{1,0:T(8,128)(2,1)}, u32[]{:S(2)}, u32[]{:S(2)}) collective-permute-start(bf16[256,768]{1,0:T(8,128)(2,1)} %fusion.7), channel_id=1, source_target_pairs={{0,32},{32,0},{1,33},{33,1},{2,34},{34,2},{3,35},{35,3},{4,36},{36... | collective-permute-start | bytes 1179656 | tf_op jit(solution)/shard_map/ppermute | solution.py:142
  114.0 8.3 %collective-permute-done.3 = bf16[256,768]{1,0:T(8,128)(2,1)} collective-permute-done((bf16[256,768]{1,0:T(8,128)(2,1)}, bf16[256,768]{1,0:T(8,128)(2,1)}, u32[]{:S(2)}, u32[]{:S(2)}) %collective-permute-start.3) | collective-permute-done | bytes 393248 | tf_op jit(solution)/shard_map/ppermute | solution.py:142
  122.3 1.2 fusion.9
  123.6 79.8 %conditional.3 = (bf16[512,768]{1,0:T(8,128)(2,1)}, bf16[512,768]{1,0:T(8,128)(2,1)}, bf16[8,2,64,128]{3,2,1,0:T(8,128)(2,1)S(1)}, f32[768,384]{1,0:T(8,128)}) conditional(s32[]{:T(128)} %convert_element_type.88, () %tuple.27, (bf16[16,768]{1,0:T(8,128)(2,1)S(1)}, bf16[16,16,768]{2,1,0:T(8,128)(2,1)S(1)}, s32[]{:T(128)}, ...), branch_computations={%region_3.4_spmd, %region_4.6_spmd} | conditional | flops 806281216 | bytes 24289556 | solution.py:247
  124.4 6.4 %all-to-all-start = ((bf16[16,16,768]{2,1,0:T(8,128)(2,1)}), bf16[16,16,768]{2,1,0:T(8,128)(2,1)S(1)}, u32[]{:S(2)}, u32[]{:S(2)}) async-start(bf16[16,16,768]{2,1,0:T(8,128)(2,1)} %copy-done.8), calls=%async_computation | async-start | bytes 786432 | tf_op jit(solution)/shard_map/cond/branch_1_fun/all_to_all | solution.py:221
  132.4 1.5 constant_dynamic-slice_fusion
  135.0 1.6 convolution_add_fusion
  136.6 11.7 %all-to-all-done = bf16[16,16,768]{2,1,0:T(8,128)(2,1)S(1)} async-done(((bf16[16,16,768]{2,1,0:T(8,128)(2,1)}), bf16[16,16,768]{2,1,0:T(8,128)(2,1)S(1)}, u32[]{:S(2)}, u32[]{:S(2)}) %all-to-all-start) | async-done | bytes 393248 | tf_op jit(solution)/shard_map/cond/branch_1_fun/all_to_all | solution.py:221
  148.4 6.4 %all-gather = bf16[32,768]{1,0:T(8,128)(2,1)S(1)} all-gather(bf16[16,768]{1,0:T(8,128)(2,1)S(1)} %add_convert_fusion), channel_id=2, replica_groups=mesh['x'=4,'yl'=2,'yh'=2,'z'=16,'c'=2] {'yh'}, dimensions={0}, use_global_device_ids=true | all-gather | bytes 73728 | tf_op jit(solution)/shard_map/cond/branch_1_fun/all_gather | solution.py:230
  154.8 32.8 %all_gather.21 = bf16[512,768]{1,0:T(8,128)(2,1)} all-gather(bf16[32,768]{1,0:T(8,128)(2,1)S(1)} %all-gather), channel_id=1, replica_groups=mesh['x'=4,'yl'=2,'yh'=2,'z'=16,'c'=2] {'z'}, dimensions={0}, use_global_device_ids=true | all-gather | bytes 835584 | tf_op jit(solution)/shard_map/cond/branch_1_fun/all_gather | solution.py:162
  187.6 12.0 %collective-permute-start = (bf16[512,768]{1,0:T(8,128)(2,1)}, bf16[512,768]{1,0:T(8,128)(2,1)}, u32[]{:S(2)}, u32[]{:S(2)}) collective-permute-start(bf16[512,768]{1,0:T(8,128)(2,1)} %all_gather.21), channel_id=1, source_target_pairs={{0,1},{1,0},{2,3},{3,2},{4,5},{5,4},{6,7},{7,6},{8,9},{9,8},{10,11... | collective-permute-start | bytes 2359304 | tf_op jit(solution)/shard_map/cond/branch_1_fun/ppermute | solution.py:142
  199.6 1.5 convolution_convert_fusion.3
  201.8 1.5 convolution_convert_fusion.2
  204.1 4.1 %all-to-all-start.3 = ((bf16[8,2,64,128]{3,2,1,0:T(8,128)(2,1)}), bf16[8,2,64,128]{3,2,1,0:T(8,128)(2,1)S(1)}, u32[]{:S(2)}, u32[]{:S(2)}) async-start(bf16[8,2,64,128]{3,2,1,0:T(8,128)(2,1)} %copy-done.9), calls=%async_computation.3 | async-start | bytes 524288 | tf_op jit(solution)/shard_map/all_to_all | solution.py:148
  208.2 1.2 copy-done.1
  209.4 3.5 %shard_map.134 = (f32[384,768]{1,0:T(8,128)}, f32[96,768]{1,0:T(8,128)}) custom-call(bf16[8,2,64,512]{3,2,1,0:T(8,128)(2,1)S(1)} %bitcast.108, bf16[512,768]{1,0:T(8,128)(2,1)S(1)} %get-tuple-element.69.grad_own_ref, bf16[512,768]{1,0:T(8,128)(2,1)S(1)} %get-tuple-element.70.grad_other_ref, bf16[512,768]{1,0:T(8,128)(2,1)} %get-tuple-element.71.gs_own_ref, ...), custom_call_target="tpu_custom_call" | custom-call | flops 805306368 | bytes 4194304 | tf_op jit(solution)/shard_map/pallas_call | solution.py:86
  212.9 1.2 all-to-all-done.3
  (79 shorter events, 10.1 us)
Async XLA Ops:
  7.2 90.9 %copy-start = (bf16[768,384]{1,0:T(8,128)(2,1)S(1)}, bf16[768,384]{1,0:T(8,128)(2,1)}, u32[]{:S(2)}) copy-start(bf16[768,384]{1,0:T(8,128)(2,1)} %param.22) | copy-start | bytes 1769476
  7.2 116.4 %all-gather.7.cloned.1.call-start = ((), (), s32[]{:S(2)}) async-start(), calls=%async_computation.4 | async-start | bytes 1622016 | tf_op jit(solution)/shard_map/all_gather | solution.py:172
  15.6 187.8 %all-gather.9.cloned.1.call-start = ((), (), s32[]{:S(2)}) async-start(), calls=%async_computation.5 | async-start | bytes 1179648 | tf_op jit(solution)/shard_map/all_gather | solution.py:217
  51.2 11.4 %copy-start.2 = (bf16[512,768]{1,0:T(8,128)(2,1)}, bf16[512,768]{1,0:T(8,128)(2,1)S(1)}, u32[]{:S(2)}) copy-start(bf16[512,768]{1,0:T(8,128)(2,1)S(1)} %all_gather.18) | copy-start | bytes 2359300 | tf_op jit(solution)/shard_map/cond
  51.2 11.6 %collective-permute-start.1 = (bf16[512,768]{1,0:T(8,128)(2,1)S(1)}, bf16[512,768]{1,0:T(8,128)(2,1)S(1)}, u32[]{:S(2)}, u32[]{:S(2)}) collective-permute-start(bf16[512,768]{1,0:T(8,128)(2,1)S(1)} %all_gather.18), channel_id=1, source_target_pairs={{0,1},{1,0},{2,3},{3,2},{4,5},{5,4},{6,7},{7,6},{8,9},{9,8},{10,11... | collective-permute-start | bytes 2359304 | tf_op jit(solution)/shard_map/cond/branch_1_fun/ppermute | solution.py:142
  60.8 1.9 copy-start.16
  62.7 0.9 copy-start.4
  64.7 5.2 %copy-start.11 = (bf16[128,384]{1,0:T(8,128)(2,1)S(1)}, bf16[128,384]{1,0:T(8,128)(2,1)}, u32[]{:S(2)}) copy-start(bf16[128,384]{1,0:T(8,128)(2,1)} %get-tuple-element.124) | copy-start | bytes 294916 | tf_op jit(solution)/shard_map/cond
  64.7 5.3 %copy-start.14 = (f32[128,12]{0,1:T(8,128)S(1)}, f32[128,12]{0,1:T(8,128)}, u32[]{:S(2)}) copy-start(f32[128,12]{0,1:T(8,128)} %get-tuple-element.81) | copy-start | bytes 18436 | tf_op jit(solution)/shard_map/cond
  64.7 17.2 %all-to-all-start.1 = ((bf16[8,2,64,384]{3,2,1,0:T(8,128)(2,1)}), bf16[8,2,64,384]{3,2,1,0:T(8,128)(2,1)S(1)}, u32[]{:S(2)}, u32[]{:S(2)}) async-start(bf16[8,2,64,384]{3,2,1,0:T(8,128)(2,1)} %copy.66), calls=%async_computation.1 | async-start | bytes 1572864 | tf_op jit(solution)/shard_map/cond/branch_1_fun/all_to_all | solution.py:148
  96.4 1.4 copy-start.3
  96.4 1.6 copy-start.5
  98.0 5.9 %copy-start.13 = (bf16[128,96]{0,1:T(8,128)(2,1)S(1)}, bf16[128,96]{0,1:T(8,128)(2,1)}, u32[]{:S(2)}) copy-start(bf16[128,96]{0,1:T(8,128)(2,1)} %param.15) | copy-start | bytes 73732
  98.0 5.9 %copy-start.15 = (f32[128,3]{0,1:T(4,128)S(1)}, f32[128,3]{0,1:T(4,128)}, u32[]{:S(2)}) copy-start(f32[128,3]{0,1:T(4,128)} %param.16) | copy-start | bytes 4612
  99.5 6.6 %collective-permute-start.2 = (bf16[512,768]{1,0:T(8,128)(2,1)}, bf16[512,768]{1,0:T(8,128)(2,1)}, u32[]{:S(2)}, u32[]{:S(2)}) collective-permute-start(bf16[512,768]{1,0:T(8,128)(2,1)} %convolution_convert_fusion.4), channel_id=1, source_target_pairs={{0,1},{1,0},{2,3},{3,2},{4,5},{5,4},{6,7},{7,6},{8,9},{9,8},{10,11... | collective-permute-start | bytes 2359304 | tf_op jit(solution)/shard_map/ppermute | solution.py:142
  108.3 14.0 %collective-permute-start.3 = (bf16[256,768]{1,0:T(8,128)(2,1)}, bf16[256,768]{1,0:T(8,128)(2,1)}, u32[]{:S(2)}, u32[]{:S(2)}) collective-permute-start(bf16[256,768]{1,0:T(8,128)(2,1)} %fusion.7), channel_id=1, source_target_pairs={{0,32},{32,0},{1,33},{33,1},{2,34},{34,2},{3,35},{35,3},{4,36},{36... | collective-permute-start | bytes 1179656 | tf_op jit(solution)/shard_map/ppermute | solution.py:142
  113.9 9.7 %copy-start.10 = (bf16[96,768]{1,0:T(8,128)(2,1)S(1)}, bf16[96,768]{1,0:T(8,128)(2,1)}, u32[]{:S(2)}) copy-start(bf16[96,768]{1,0:T(8,128)(2,1)} %param.21) | copy-start | bytes 442372
  114.0 9.7 %copy-start.12 = (bf16[16,768]{1,0:T(8,128)(2,1)S(1)}, bf16[16,768]{1,0:T(8,128)(2,1)}, u32[]{:S(2)}) copy-start(bf16[16,768]{1,0:T(8,128)(2,1)} %grad_ref.1) | copy-start | bytes 73732
  123.6 0.7 copy-start.8
  124.4 23.9 %all-to-all-start = ((bf16[16,16,768]{2,1,0:T(8,128)(2,1)}), bf16[16,16,768]{2,1,0:T(8,128)(2,1)S(1)}, u32[]{:S(2)}, u32[]{:S(2)}) async-start(bf16[16,16,768]{2,1,0:T(8,128)(2,1)} %copy-done.8), calls=%async_computation | async-start | bytes 786432 | tf_op jit(solution)/shard_map/cond/branch_1_fun/all_to_all | solution.py:221
  132.4 1.5 copy-start.7
  133.9 1.0 copy-start.6
  187.6 14.2 %collective-permute-start = (bf16[512,768]{1,0:T(8,128)(2,1)}, bf16[512,768]{1,0:T(8,128)(2,1)}, u32[]{:S(2)}, u32[]{:S(2)}) collective-permute-start(bf16[512,768]{1,0:T(8,128)(2,1)} %all_gather.21), channel_id=1, source_target_pairs={{0,1},{1,0},{2,3},{3,2},{4,5},{5,4},{6,7},{7,6},{8,9},{9,8},{10,11... | collective-permute-start | bytes 2359304 | tf_op jit(solution)/shard_map/cond/branch_1_fun/ppermute | solution.py:142
  203.4 0.7 copy-start.9
  204.1 10.0 %all-to-all-start.3 = ((bf16[8,2,64,128]{3,2,1,0:T(8,128)(2,1)}), bf16[8,2,64,128]{3,2,1,0:T(8,128)(2,1)S(1)}, u32[]{:S(2)}, u32[]{:S(2)}) async-start(bf16[8,2,64,128]{3,2,1,0:T(8,128)(2,1)} %copy-done.9), calls=%async_computation.3 | async-start | bytes 524288 | tf_op jit(solution)/shard_map/all_to_all | solution.py:148
  208.2 1.2 copy-start.1
Sparse Core Ops, SparseCore 0:
  15.8 77.4 all-gather.6
  123.7 36.7 all-gather.8

commit v8 on v5

--- a/solution.py
+++ b/solution.py
@@ -54,6 +54,31 @@
         in_specs=[pl.BlockSpec(memory_space=pltpu.VMEM)] * 3,
         out_specs=pl.BlockSpec(memory_space=pltpu.VMEM),
     )(grad_out, code, scale)
+
+
+def row_blocks_kernel(own_ref, other_ref, weight_ref, out_ref):
+    n_rows, _, block, _ = out_ref.shape
+    runs = block // PER
+    for side, ref in ((0, own_ref), (1, other_ref)):
+        product = dot_nt(ref[...], weight_ref[...]).astype(jnp.bfloat16)
+        for piece in range(n_rows * runs):
+            layer, half = piece // 2, piece % 2
+            row, run = half * (n_rows // 2) + layer // runs, layer % runs
+            out_ref[row, side, pl.ds(run * PER, PER), :] = product[piece * PER : piece * PER + PER]
+
+
+def row_blocks(own, other, weight, n_rows):
+    width = weight.shape[0]
+    return pl.pallas_call(
+        row_blocks_kernel,
+        out_shape=jax.ShapeDtypeStruct((n_rows, 2, own.shape[0] // n_rows, width), jnp.bfloat16),
+        in_specs=[pl.BlockSpec(memory_space=pltpu.VMEM)] * 3,
+        out_specs=pl.BlockSpec(memory_space=pltpu.VMEM),
+        compiler_params=pltpu.CompilerParams(vmem_limit_bytes=32 * 2**20),
+        cost_estimate=pl.CostEstimate(
+            flops=4 * own.size * width, bytes_accessed=4 * own.size, transcendentals=0
+        ),
+    )(own, other, weight)
 
 
 def last_kernel(
@@ -141,17 +166,9 @@
     def swap(block, axis):
         return lax.ppermute(block, axis, SWAP)
 
-    def blocks_of(own, other):
-        return jnp.stack([by_row(own), by_row(other)], axis=1)
-
     def scatter_rows(sent):
         came = lax.all_to_all(sent, ROWS, 0, 0, tiled=True)
         return jnp.sum(came.astype(jnp.float32), axis=0).reshape(-1, sent.shape[-1])
-
-    def by_row(block):
-        width = block.shape[1]
-        parts = block.reshape(n_rows // 2, runs, 2, per, width)
-        return parts.transpose(2, 0, 1, 3, 4).reshape(n_rows, runs * per, width)
 
     def by_z(block):
         width = block.shape[-1]
@@ -174,10 +191,7 @@
     def first_half(both):
         grad_own = gather_z(both[:, 0])
         grad_other = swap(grad_own, "c")
-        sent = blocks_of(
-            dot_nt(grad_own, down_weight).astype(jnp.bfloat16),
-            dot_nt(grad_other, down_weight).astype(jnp.bfloat16),
-        )
+        sent = row_blocks(grad_own, grad_other, down_weight, n_rows)
         grad_act = scatter_rows(sent)
         positive = jnp.maximum(
             own_first(restore(hidden_code, hidden_scale)).astype(jnp.float32), 0.0
@@ -203,30 +217,29 @@
     part = (dot_nt(pre_own, up_weight) + came.astype(jnp.float32)).reshape(n_z, 2, per, features)
     keep = lax.dynamic_index_in_dim(part, half, 1, keepdims=False)
     send = lax.dynamic_index_in_dim(part, 1 - half, 1, keepdims=False).astype(jnp.bfloat16)
+    received = swap(send, "yh")
     by_core = stream_all.reshape(n_z, 2, 2 * per, features)
-    part = (keep + swap(send, "yh").astype(jnp.float32)).astype(jnp.bfloat16)
-    part, saved, by_core = lax.optimization_barrier((part, saved, by_core))
+    received, saved, by_core = lax.optimization_barrier((received, saved, by_core))
     saved_all = lax.all_gather(saved, ROWS, axis=0)
     padded_out = jnp.pad(out_weight, ((0, -ctx_width % 128), (0, 0)))
 
-    def second_half(part, by_core):
+    def second_half(keep, received, by_core):
+        part = (keep + received.astype(jnp.float32)).astype(jnp.bfloat16)
         came = lax.all_to_all(part, "z", 0, 0, tiled=True)
         stream_own = lax.dynamic_index_in_dim(by_core, core, 1, keepdims=False)
         stream_other = lax.dynamic_index_in_dim(by_core, 1 - core, 1, keepdims=False)
         stream_own = stream_own.reshape(-1, features)
         stream_other = stream_other.reshape(-1, features)
         grad_up = dot_tn(stream_own, pre_own) + dot_tn(stream_other, pre_other)
+        came, grad_up = lax.optimization_barrier((came, grad_up))
         summed = jnp.sum(came.astype(jnp.float32), axis=0)
         grad_stream = (grad_out.astype(jnp.float32) + summed).astype(jnp.bfloat16)
         gs_own = gather_z(lax.all_gather(grad_stream, "yh", axis=0))
         gs_other = swap(gs_own, "c")
-        sent = blocks_of(
-            dot_nt(gs_own, padded_out).astype(jnp.bfloat16),
-            dot_nt(gs_other, padded_out).astype(jnp.bfloat16),
-        )
+        sent = row_blocks(gs_own, gs_other, padded_out, n_rows)
         return gs_own, gs_other, sent, grad_up
 
-    def skip_second(part, by_core):
+    def skip_second(keep, received, by_core):
         wide = jnp.zeros((n_z * 2 * per, features), jnp.bfloat16)
         return (
             wide,
@@ -235,7 +248,9 @@
             jnp.zeros((features, hidden_width), jnp.float32),
         )
 
-    gs_own, gs_other, sent, grad_up = lax.cond(always, second_half, skip_second, part, by_core)
+    gs_own, gs_other, sent, grad_up = lax.cond(
+        always, second_half, skip_second, keep, received, by_core
+    )
     sent, saved_all = lax.optimization_barrier((sent, saved_all))
     grad_ctx = natural(scatter_rows(sent)[:, :ctx_width].astype(jnp.bfloat16))
     grad_down, grad_outw = last_products(

time: 222 us -> 224 us (level)
  Pallas kernels: 5.34 us -> 11 us
  matrix products: 9.76 us -> 5.43 us
  waiting for transfers between devices: 39.6 us -> 41.9 us
    pallas_call x0 -> x2, Pallas kernels: none -> 5.89 us  [row_blocks(): pl.pallas_call(row_blocks_kernel, out_shape=jax.ShapeDtypeStruct((n_rows,...]
    dot_general x6 -> x2, matrix products: 7.54 us -> 3.21 us  [dot_nt(): lax.dot_general(left, right, (((1,), (1,)), ((), ())), preferred_element_...]
    ppermute x4, waiting for transfers between devices: 11 us -> 14.7 us  [swap(): return lax.ppermute(block, axis, SWAP)]
  transfers between devices with their start and end apart: 9 -> 9, of which waited for: 6 -> 7; matrix products, arithmetic and copies ran while one was open for 8% -> 5% of each run, Pallas kernels for 2% -> 4%
where the time goes in v8:
time: 224 us
  blocking collectives  94.5 us (42%)
  starting transfers between devices  46.6 us (21%)
  waiting for transfers between devices  41.9 us (19%)
  between operations  14.2 us (6%)
  Pallas kernels  11 us (5%)
  local copies, waits for them, and re-layouts  6.71 us (3%)
  matrix products  5.43 us (2%)
  other arithmetic  3.03 us (1%)
    all_gather x2, blocking collectives, gather_z(): return lax.all_gather(pair.reshape(-1, features), 'z', axis=0, tiled=True)  68.5 us
    ppermute x4, starting transfers between devices, swap(): return lax.ppermute(block, axis, SWAP)  31.5 us
    ppermute x4, waiting for transfers between devices, swap(): return lax.ppermute(block, axis, SWAP)  14.7 us
    all_to_all x1, blocking collectives, gather_rows(): every = lax.all_to_all(copies, ROWS, 0, 0, tiled=True)  14.3 us
    all_to_all x1, waiting for transfers between devices, second_half(): came = lax.all_to_all(part, 'z', 0, 0, tiled=True)  13.8 us
    all_to_all x2, waiting for transfers between devices, scatter_rows(): came = lax.all_to_all(sent, ROWS, 0, 0, tiled=True)  13.3 us
    all_to_all x2, starting transfers between devices, scatter_rows(): came = lax.all_to_all(sent, ROWS, 0, 0, tiled=True)  8.61 us
    all_to_all x1, starting transfers between devices, second_half(): came = lax.all_to_all(part, 'z', 0, 0, tiled=True)  6.38 us
  transfers between devices with their start and end apart: 9, of which 7 were waited for; matrix products, arithmetic and copies ran while one was open for 5% of the time, Pallas kernels for 4%

profile of v8, /device:TPU:1, one launch (start us, length us, event | category | flops | bytes accessed | tf_op | source)
XLA Modules:
  0.0 223.6 jit_solution(9896711078723011906)
XLA Ops:
  7.2 1.6 shard_map.133
  8.8 6.1 %all-gather.1 = bf16[4,16,768]{2,1,0:T(8,128)(2,1)S(1)} all-gather(bf16[2,16,768]{2,1,0:T(8,128)(2,1)} %shard_map.133), channel_id=3, replica_groups=mesh['x'=4,'yl'=2,'yh'=2,'z'=16,'c'=2] {'yh'}, dimensions={0}, use_global_device_ids=true | all-gather | bytes 147456 | tf_op jit(solution)/shard_map/all_gather | solution.py:188
  15.7 82.1 %conditional.2 = (bf16[512,768]{1,0:T(8,128)(2,1)S(1)}, bf16[512,768]{1,0:T(8,128)(2,1)S(1)}, bf16[8,2,64,384]{3,2,1,0:T(8,128)(2,1)S(1)}, bf16[128,384]{1,0:T(8,128)(2,1)S(1)}) conditional(s32[]{:T(128)} %convert_element_type.70, () %tuple.29, (bf16[2,2,16,768]{3,2,1,0:T(8,128)(2,1)S(1)}, bf16[384,768]{1,0:T(8,128)(2,1)}, s32[]{:T(128)}, ...), branch_computations={%region_0.0_spmd, %region_1.3_spmd} | conditional | flops 605306880 | bytes 26720536 | solution.py:209
  15.7 35.5 %all_gather.18.own_ref = bf16[512,768]{1,0:T(8,128)(2,1)S(1)} all-gather(bf16[32,768]{1,0:T(8,128)(2,1)S(1)} %bitcast.97), channel_id=1, replica_groups=mesh['x'=4,'yl'=2,'yh'=2,'z'=16,'c'=2] {'z'}, dimensions={0}, use_global_device_ids=true | all-gather | bytes 835584 | tf_op jit(solution)/shard_map/cond/branch_1_fun/all_gather | solution.py:179
  51.2 9.7 %collective-permute-start = (bf16[512,768]{1,0:T(8,128)(2,1)S(1)}, bf16[512,768]{1,0:T(8,128)(2,1)S(1)}, u32[]{:S(2)}, u32[]{:S(2)}) collective-permute-start(bf16[512,768]{1,0:T(8,128)(2,1)S(1)} %all_gather.18.own_ref), channel_id=1, source_target_pairs={{0,1},{1,0},{2,3},{3,2},{4,5},{5,4},{6,7},{7,6},{8,9},{9,8},{10,11... | collective-permute-start | bytes 2359304 | tf_op jit(solution)/shard_map/cond/branch_1_fun/ppermute | solution.py:167
  60.9 1.9 collective-permute-done.other_ref
  62.8 3.2 %branch_1_fun.2 = bf16[8,2,64,384]{3,2,1,0:T(8,128)(2,1)} custom-call(bf16[512,768]{1,0:T(8,128)(2,1)S(1)} %all_gather.18.own_ref, bf16[512,768]{1,0:T(8,128)(2,1)S(1)} %collective-permute-done.other_ref, bf16[384,768]{1,0:T(8,128)(2,1)} %get-tuple-element.93.weight_ref), custom_call_target="tpu_custom_call" | custom-call | flops 603979776 | bytes 1572864 | tf_op jit(solution)/shard_map/cond/branch_1_fun/pallas_call | solution.py:72
  66.1 5.2 %all-to-all-start = ((bf16[8,2,64,384]{3,2,1,0:T(8,128)(2,1)}), bf16[8,2,64,384]{3,2,1,0:T(8,128)(2,1)S(1)}, u32[]{:S(2)}, u32[]{:S(2)}) async-start(bf16[8,2,64,384]{3,2,1,0:T(8,128)(2,1)} %branch_1_fun.2), calls=%async_computation | async-start | bytes 1572864 | tf_op jit(solution)/shard_map/cond/branch_1_fun/all_to_all | solution.py:170
  71.6 11.6 %all-to-all-done = bf16[8,2,64,384]{3,2,1,0:T(8,128)(2,1)S(1)} async-done(((bf16[8,2,64,384]{3,2,1,0:T(8,128)(2,1)}), bf16[8,2,64,384]{3,2,1,0:T(8,128)(2,1)S(1)}, u32[]{:S(2)}, u32[]{:S(2)}) %all-to-all-start) | async-done | bytes 786464 | tf_op jit(solution)/shard_map/cond/branch_1_fun/all_to_all | solution.py:170
  83.5 14.3 %all_to_all.17 = bf16[8,128,384]{2,1,0:T(8,128)(2,1)S(1)} all-to-all(bf16[8,128,384]{2,1,0:T(8,128)(2,1)S(1)} %broadcast_in_dim.0), channel_id=1, replica_groups=mesh['x'=4,'yl'=2,'yh'=2,'z'=16,'c'=2] {'x','yl'}, dimensions={0} | all-to-all | bytes 1572864 | tf_op jit(solution)/shard_map/cond/branch_1_fun/all_to_all | solution.py:185
  98.0 1.5 convolution_convert_fusion
  99.4 4.4 %collective-permute-start.2 = (bf16[512,768]{1,0:T(8,128)(2,1)}, bf16[512,768]{1,0:T(8,128)(2,1)}, u32[]{:S(2)}, u32[]{:S(2)}) collective-permute-start(bf16[512,768]{1,0:T(8,128)(2,1)} %convolution_convert_fusion), channel_id=1, source_target_pairs={{0,1},{1,0},{2,3},{3,2},{4,5},{5,4},{6,7},{7,6},{8,9},{9,8},{10,11... | collective-permute-start | bytes 2359304 | tf_op jit(solution)/shard_map/ppermute | solution.py:167
  104.1 2.0 collective-permute-done.2
  106.1 1.7 convert_add_fusion
  107.8 1.1 copy-done.6
  109.8 4.5 %collective-permute-start.3 = (bf16[16,16,768]{2,1,0:T(8,128)(2,1)}, bf16[16,16,768]{2,1,0:T(8,128)(2,1)S(1)}, u32[]{:S(2)}, u32[]{:S(2)}) collective-permute-start(bf16[16,16,768]{2,1,0:T(8,128)(2,1)} %fusion.4), channel_id=1, source_target_pairs={{0,32},{32,0},{1,33},{33,1},{2,34},{34,2},{3,35},{35,3},{4,36},{36... | collective-permute-start | bytes 1179656 | tf_op jit(solution)/shard_map/ppermute | solution.py:167
  115.1 8.6 %collective-permute-done.3 = bf16[16,16,768]{2,1,0:T(8,128)(2,1)S(1)} collective-permute-done((bf16[16,16,768]{2,1,0:T(8,128)(2,1)}, bf16[16,16,768]{2,1,0:T(8,128)(2,1)S(1)}, u32[]{:S(2)}, u32[]{:S(2)}) %collective-permute-start.3) | collective-permute-done | bytes 393248 | tf_op jit(solution)/shard_map/ppermute | solution.py:167
  123.7 82.4 %conditional.3 = (bf16[512,768]{1,0:T(8,128)(2,1)}, bf16[512,768]{1,0:T(8,128)(2,1)}, bf16[8,2,64,128]{3,2,1,0:T(8,128)(2,1)}, f32[768,384]{1,0:T(8,128)}) conditional(s32[]{:T(128)} %convert_element_type.70, () %tuple.28, (bf16[16,768]{1,0:T(8,128)(2,1)S(1)}, s32[]{:T(128)}, f32[16,2,16,768]{3,2,1,0:T(8,128)}, bf16[16,16,768]{2,1,0:T(8,128)(2,1)S(1)}, ...), branch_computations={%region_3.4_spmd, %region_4.6_spmd} | conditional | flops 806608896 | bytes 18899204 | solution.py:251
  123.7 2.0 fusion.3
  125.7 6.4 %all-to-all-start.2 = ((bf16[16,16,768]{2,1,0:T(8,128)(2,1)}), bf16[16,16,768]{2,1,0:T(8,128)(2,1)S(1)}, u32[]{:S(2)}, u32[]{:S(2)}) async-start(bf16[16,16,768]{2,1,0:T(8,128)(2,1)} %fusion.3), calls=%async_computation.2 | async-start | bytes 786432 | tf_op jit(solution)/shard_map/cond/branch_1_fun/all_to_all | solution.py:228
  132.1 1.5 constant_dynamic-slice_fusion
  134.2 1.6 convolution_add_fusion
  135.8 13.8 %all-to-all-done.2 = bf16[16,16,768]{2,1,0:T(8,128)(2,1)S(1)} async-done(((bf16[16,16,768]{2,1,0:T(8,128)(2,1)}), bf16[16,16,768]{2,1,0:T(8,128)(2,1)S(1)}, u32[]{:S(2)}, u32[]{:S(2)}) %all-to-all-start.2) | async-done | bytes 393248 | tf_op jit(solution)/shard_map/cond/branch_1_fun/all_to_all | solution.py:228
  149.7 5.6 %all-gather = bf16[32,768]{1,0:T(8,128)(2,1)S(1)} all-gather(bf16[16,768]{1,0:T(8,128)(2,1)S(1)} %add_convert_fusion), channel_id=2, replica_groups=mesh['x'=4,'yl'=2,'yh'=2,'z'=16,'c'=2] {'yh'}, dimensions={0}, use_global_device_ids=true | all-gather | bytes 73728 | tf_op jit(solution)/shard_map/cond/branch_1_fun/all_gather | solution.py:237
  155.3 33.0 %all_gather.21.own_ref = bf16[512,768]{1,0:T(8,128)(2,1)} all-gather(bf16[32,768]{1,0:T(8,128)(2,1)S(1)} %all-gather), channel_id=1, replica_groups=mesh['x'=4,'yl'=2,'yh'=2,'z'=16,'c'=2] {'z'}, dimensions={0}, use_global_device_ids=true | all-gather | bytes 835584 | tf_op jit(solution)/shard_map/cond/branch_1_fun/all_gather | solution.py:179
  188.3 12.9 %collective-permute-start.1 = (bf16[512,768]{1,0:T(8,128)(2,1)}, bf16[512,768]{1,0:T(8,128)(2,1)}, u32[]{:S(2)}, u32[]{:S(2)}) collective-permute-start(bf16[512,768]{1,0:T(8,128)(2,1)} %all_gather.21.own_ref), channel_id=1, source_target_pairs={{0,1},{1,0},{2,3},{3,2},{4,5},{5,4},{6,7},{7,6},{8,9},{9,8},{10,11... | collective-permute-start | bytes 2359304 | tf_op jit(solution)/shard_map/cond/branch_1_fun/ppermute | solution.py:167
  201.3 2.2 collective-permute-done.1.other_ref
  203.5 2.6 %branch_1_fun.3 = bf16[8,2,64,128]{3,2,1,0:T(8,128)(2,1)} custom-call(bf16[512,768]{1,0:T(8,128)(2,1)} %all_gather.21.own_ref, bf16[512,768]{1,0:T(8,128)(2,1)} %collective-permute-done.1.other_ref, bf16[128,768]{1,0:T(8,128)(2,1)S(1)} %pad.4.weight_ref), custom_call_target="tpu_custom_call" | custom-call | flops 201326592 | bytes 1572864 | tf_op jit(solution)/shard_map/cond/branch_1_fun/pallas_call | solution.py:72
  206.1 3.4 %all-to-all-start.3 = ((bf16[8,2,64,128]{3,2,1,0:T(8,128)(2,1)}), bf16[8,2,64,128]{3,2,1,0:T(8,128)(2,1)S(1)}, u32[]{:S(2)}, u32[]{:S(2)}) async-start(bf16[8,2,64,128]{3,2,1,0:T(8,128)(2,1)} %get-tuple-element.81), calls=%async_computation.3 | async-start | bytes 524288 | tf_op jit(solution)/shard_map/all_to_all | solution.py:170
  209.5 1.2 copy-done.1
  210.8 3.5 %shard_map.134 = (f32[384,768]{1,0:T(8,128)}, f32[96,768]{1,0:T(8,128)}) custom-call(bf16[8,2,64,512]{3,2,1,0:T(8,128)(2,1)S(1)} %bitcast.79, bf16[512,768]{1,0:T(8,128)(2,1)S(1)} %get-tuple-element.83.grad_own_ref, bf16[512,768]{1,0:T(8,128)(2,1)S(1)} %get-tuple-element.84.grad_other_ref, bf16[512,768]{1,0:T(8,128)(2,1)} %get-tuple-element.85.gs_own_ref, ...), custom_call_target="tpu_custom_call" | custom-call | flops 805306368 | bytes 4194304 | tf_op jit(solution)/shard_map/pallas_call | solution.py:111
  214.2 1.7 all-to-all-done.3
  (63 shorter events, 4.7 us)
Async XLA Ops:
  7.2 90.8 %copy-start = (bf16[768,384]{1,0:T(8,128)(2,1)S(1)}, bf16[768,384]{1,0:T(8,128)(2,1)}, u32[]{:S(2)}) copy-start(bf16[768,384]{1,0:T(8,128)(2,1)} %param.22) | copy-start | bytes 1769476
  7.2 116.5 %all-gather.7.cloned.1.call-start = ((), (), s32[]{:S(2)}) async-start(), calls=%async_computation.4 | async-start | bytes 1622016 | tf_op jit(solution)/shard_map/all_gather | solution.py:189
  15.6 190.5 %all-gather.9.cloned.1.call-start = ((), (), s32[]{:S(2)}) async-start(), calls=%async_computation.5 | async-start | bytes 1179648 | tf_op jit(solution)/shard_map/all_gather | solution.py:223
  51.2 14.9 %copy-start.4 = (bf16[512,768]{1,0:T(8,128)(2,1)}, bf16[512,768]{1,0:T(8,128)(2,1)S(1)}, u32[]{:S(2)}) copy-start(bf16[512,768]{1,0:T(8,128)(2,1)S(1)} %all_gather.18.own_ref) | copy-start | bytes 2359300 | tf_op jit(solution)/shard_map/cond
  51.2 11.6 %collective-permute-start = (bf16[512,768]{1,0:T(8,128)(2,1)S(1)}, bf16[512,768]{1,0:T(8,128)(2,1)S(1)}, u32[]{:S(2)}, u32[]{:S(2)}) collective-permute-start(bf16[512,768]{1,0:T(8,128)(2,1)S(1)} %all_gather.18.own_ref), channel_id=1, source_target_pairs={{0,1},{1,0},{2,3},{3,2},{4,5},{5,4},{6,7},{7,6},{8,9},{9,8},{10,11... | collective-permute-start | bytes 2359304 | tf_op jit(solution)/shard_map/cond/branch_1_fun/ppermute | solution.py:167
  62.8 3.3 %copy-start.2 = (bf16[512,768]{1,0:T(8,128)(2,1)}, bf16[512,768]{1,0:T(8,128)(2,1)S(1)}, u32[]{:S(2)}) copy-start(bf16[512,768]{1,0:T(8,128)(2,1)S(1)} %collective-permute-done.other_ref) | copy-start | bytes 2359300 | tf_op jit(solution)/shard_map/cond
  62.8 8.5 %copy-start.8 = (bf16[128,384]{1,0:T(8,128)(2,1)S(1)}, bf16[128,384]{1,0:T(8,128)(2,1)}, u32[]{:S(2)}) copy-start(bf16[128,384]{1,0:T(8,128)(2,1)} %get-tuple-element.124) | copy-start | bytes 294916 | tf_op jit(solution)/shard_map/cond
  66.1 5.3 %copy-start.11 = (f32[128,12]{0,1:T(8,128)S(1)}, f32[128,12]{0,1:T(8,128)}, u32[]{:S(2)}) copy-start(f32[128,12]{0,1:T(8,128)} %get-tuple-element.95) | copy-start | bytes 18436 | tf_op jit(solution)/shard_map/cond
  66.1 17.1 %all-to-all-start = ((bf16[8,2,64,384]{3,2,1,0:T(8,128)(2,1)}), bf16[8,2,64,384]{3,2,1,0:T(8,128)(2,1)S(1)}, u32[]{:S(2)}, u32[]{:S(2)}) async-start(bf16[8,2,64,384]{3,2,1,0:T(8,128)(2,1)} %branch_1_fun.2), calls=%async_computation | async-start | bytes 1572864 | tf_op jit(solution)/shard_map/cond/branch_1_fun/all_to_all | solution.py:170
  83.4 14.4 %copy-start.3 = (bf16[512,768]{1,0:T(8,128)(2,1)S(1)}, bf16[512,768]{1,0:T(8,128)(2,1)}, u32[]{:S(2)}) copy-start(bf16[512,768]{1,0:T(8,128)(2,1)} %copy-done.2) | copy-start | bytes 2359300 | tf_op jit(solution)/shard_map/cond
  83.4 14.4 %copy-start.5 = (bf16[512,768]{1,0:T(8,128)(2,1)S(1)}, bf16[512,768]{1,0:T(8,128)(2,1)}, u32[]{:S(2)}) copy-start(bf16[512,768]{1,0:T(8,128)(2,1)} %copy-done.4) | copy-start | bytes 2359300 | tf_op jit(solution)/shard_map/cond
  97.9 6.0 %copy-start.10 = (bf16[128,96]{0,1:T(8,128)(2,1)S(1)}, bf16[128,96]{0,1:T(8,128)(2,1)}, u32[]{:S(2)}) copy-start(bf16[128,96]{0,1:T(8,128)(2,1)} %param.15) | copy-start | bytes 73732
  97.9 6.0 %copy-start.12 = (f32[128,3]{0,1:T(4,128)S(1)}, f32[128,3]{0,1:T(4,128)}, u32[]{:S(2)}) copy-start(f32[128,3]{0,1:T(4,128)} %param.16) | copy-start | bytes 4612
  99.4 6.6 %collective-permute-start.2 = (bf16[512,768]{1,0:T(8,128)(2,1)}, bf16[512,768]{1,0:T(8,128)(2,1)}, u32[]{:S(2)}, u32[]{:S(2)}) collective-permute-start(bf16[512,768]{1,0:T(8,128)(2,1)} %convolution_convert_fusion), channel_id=1, source_target_pairs={{0,1},{1,0},{2,3},{3,2},{4,5},{5,4},{6,7},{7,6},{8,9},{9,8},{10,11... | collective-permute-start | bytes 2359304 | tf_op jit(solution)/shard_map/ppermute | solution.py:167
  106.1 17.6 %copy-start.9 = (bf16[16,768]{1,0:T(8,128)(2,1)S(1)}, bf16[16,768]{1,0:T(8,128)(2,1)}, u32[]{:S(2)}) copy-start(bf16[16,768]{1,0:T(8,128)(2,1)} %grad_ref.1) | copy-start | bytes 73732
  107.8 1.1 copy-start.6
  109.8 13.9 %collective-permute-start.3 = (bf16[16,16,768]{2,1,0:T(8,128)(2,1)}, bf16[16,16,768]{2,1,0:T(8,128)(2,1)S(1)}, u32[]{:S(2)}, u32[]{:S(2)}) collective-permute-start(bf16[16,16,768]{2,1,0:T(8,128)(2,1)} %fusion.4), channel_id=1, source_target_pairs={{0,32},{32,0},{1,33},{33,1},{2,34},{34,2},{3,35},{35,3},{4,36},{36... | collective-permute-start | bytes 1179656 | tf_op jit(solution)/shard_map/ppermute | solution.py:167
  125.7 23.9 %all-to-all-start.2 = ((bf16[16,16,768]{2,1,0:T(8,128)(2,1)}), bf16[16,16,768]{2,1,0:T(8,128)(2,1)S(1)}, u32[]{:S(2)}, u32[]{:S(2)}) async-start(bf16[16,16,768]{2,1,0:T(8,128)(2,1)} %fusion.3), calls=%async_computation.2 | async-start | bytes 786432 | tf_op jit(solution)/shard_map/cond/branch_1_fun/all_to_all | solution.py:228
  134.2 67.0 %copy-start.7 = (bf16[96,768]{1,0:T(8,128)(2,1)S(1)}, bf16[96,768]{1,0:T(8,128)(2,1)}, u32[]{:S(2)}) copy-start(bf16[96,768]{1,0:T(8,128)(2,1)} %get-tuple-element.97) | copy-start | bytes 442372 | tf_op jit(solution)/shard_map/cond
  188.3 15.1 %collective-permute-start.1 = (bf16[512,768]{1,0:T(8,128)(2,1)}, bf16[512,768]{1,0:T(8,128)(2,1)}, u32[]{:S(2)}, u32[]{:S(2)}) collective-permute-start(bf16[512,768]{1,0:T(8,128)(2,1)} %all_gather.21.own_ref), channel_id=1, source_target_pairs={{0,1},{1,0},{2,3},{3,2},{4,5},{5,4},{6,7},{7,6},{8,9},{9,8},{10,11... | collective-permute-start | bytes 2359304 | tf_op jit(solution)/shard_map/cond/branch_1_fun/ppermute | solution.py:167
  206.1 9.8 %all-to-all-start.3 = ((bf16[8,2,64,128]{3,2,1,0:T(8,128)(2,1)}), bf16[8,2,64,128]{3,2,1,0:T(8,128)(2,1)S(1)}, u32[]{:S(2)}, u32[]{:S(2)}) async-start(bf16[8,2,64,128]{3,2,1,0:T(8,128)(2,1)} %get-tuple-element.81), calls=%async_computation.3 | async-start | bytes 524288 | tf_op jit(solution)/shard_map/all_to_all | solution.py:170
  209.5 1.2 copy-start.1
Sparse Core Ops, SparseCore 0:
  15.7 77.4 all-gather.6
  123.8 36.3 all-gather.8

commit v9 on v5

--- a/solution.py
+++ b/solution.py
@@ -204,18 +204,19 @@
     keep = lax.dynamic_index_in_dim(part, half, 1, keepdims=False)
     send = lax.dynamic_index_in_dim(part, 1 - half, 1, keepdims=False).astype(jnp.bfloat16)
     by_core = stream_all.reshape(n_z, 2, 2 * per, features)
-    part = (keep + swap(send, "yh").astype(jnp.float32)).astype(jnp.bfloat16)
-    part, saved, by_core = lax.optimization_barrier((part, saved, by_core))
+    send, saved, by_core = lax.optimization_barrier((send, saved, by_core))
     saved_all = lax.all_gather(saved, ROWS, axis=0)
     padded_out = jnp.pad(out_weight, ((0, -ctx_width % 128), (0, 0)))
 
-    def second_half(part, by_core):
+    def second_half(keep, send, by_core):
+        part = (keep + swap(send, "yh").astype(jnp.float32)).astype(jnp.bfloat16)
         came = lax.all_to_all(part, "z", 0, 0, tiled=True)
         stream_own = lax.dynamic_index_in_dim(by_core, core, 1, keepdims=False)
         stream_other = lax.dynamic_index_in_dim(by_core, 1 - core, 1, keepdims=False)
         stream_own = stream_own.reshape(-1, features)
         stream_other = stream_other.reshape(-1, features)
         grad_up = dot_tn(stream_own, pre_own) + dot_tn(stream_other, pre_other)
+        came, grad_up = lax.optimization_barrier((came, grad_up))
         summed = jnp.sum(came.astype(jnp.float32), axis=0)
         grad_stream = (grad_out.astype(jnp.float32) + summed).astype(jnp.bfloat16)
         gs_own = gather_z(lax.all_gather(grad_stream, "yh", axis=0))
@@ -226,7 +227,7 @@
         )
         return gs_own, gs_other, sent, grad_up
 
-    def skip_second(part, by_core):
+    def skip_second(keep, send, by_core):
         wide = jnp.zeros((n_z * 2 * per, features), jnp.bfloat16)
         return (
             wide,
@@ -235,7 +236,9 @@
             jnp.zeros((features, hidden_width), jnp.float32),
         )
 
-    gs_own, gs_other, sent, grad_up = lax.cond(always, second_half, skip_second, part, by_core)
+    gs_own, gs_other, sent, grad_up = lax.cond(
+        always, second_half, skip_second, keep, send, by_core
+    )
     sent, saved_all = lax.optimization_barrier((sent, saved_all))
     grad_ctx = natural(scatter_rows(sent)[:, :ctx_width].astype(jnp.bfloat16))
     grad_down, grad_outw = last_products(

time: 222 us -> 220 us (level)
  transfers between devices with their start and end apart: 9 -> 9, of which waited for: 6 -> 7; matrix products, arithmetic and copies ran while one was open for 8% -> 8% of each run, Pallas kernels for 2% -> 2%
where the time goes in v9:
time: 220 us
  blocking collectives  94.4 us (43%)
  starting transfers between devices  45.4 us (21%)
  waiting for transfers between devices  39.4 us (18%)
  between operations  14.3 us (6%)
  matrix products  9.8 us (4%)
  local copies, waits for them, and re-layouts  6.95 us (3%)
  Pallas kernels  5.58 us (3%)
  other arithmetic  3.69 us (2%)
    all_gather x2, blocking collectives, gather_z(): return lax.all_gather(pair.reshape(-1, features), 'z', axis=0, tiled=True)  68.9 us
    ppermute x4, starting transfers between devices, swap(): return lax.ppermute(block, axis, SWAP)  32 us
    all_to_all x1, blocking collectives, gather_rows(): every = lax.all_to_all(copies, ROWS, 0, 0, tiled=True)  14.2 us
    all_to_all x1, waiting for transfers between devices, second_half(): came = lax.all_to_all(part, 'z', 0, 0, tiled=True)  13.8 us
    all_to_all x2, waiting for transfers between devices, scatter_rows(): came = lax.all_to_all(sent, ROWS, 0, 0, tiled=True)  12.9 us
    ppermute x4, waiting for transfers between devices, swap(): return lax.ppermute(block, axis, SWAP)  12.7 us
    all_to_all x2, starting transfers between devices, scatter_rows(): came = lax.all_to_all(sent, ROWS, 0, 0, tiled=True)  8.51 us
    dot_general x6, matrix products, dot_nt(): lax.dot_general(left, right, (((1,), (1,)), ((), ())), preferred_element_...  7.58 us
  transfers between devices with their start and end apart: 9, of which 7 were waited for; matrix products, arithmetic and copies ran while one was open for 8% of the time, Pallas kernels for 2%

profile of v9, /device:TPU:1, one launch (start us, length us, event | category | flops | bytes accessed | tf_op | source)
XLA Modules:
  0.0 219.6 jit_solution(6234443835039250593)
XLA Ops:
  7.2 1.6 shard_map.133
  8.8 6.1 %all-gather.1 = bf16[4,16,768]{2,1,0:T(8,128)(2,1)S(1)} all-gather(bf16[2,16,768]{2,1,0:T(8,128)(2,1)} %shard_map.133), channel_id=3, replica_groups=mesh['x'=4,'yl'=2,'yh'=2,'z'=16,'c'=2] {'yh'}, dimensions={0}, use_global_device_ids=true | all-gather | bytes 147456 | tf_op jit(solution)/shard_map/all_gather | solution.py:171
  15.7 80.7 %conditional.2 = (bf16[512,768]{1,0:T(8,128)(2,1)}, bf16[512,768]{1,0:T(8,128)(2,1)}, bf16[8,2,64,384]{3,2,1,0:T(8,128)(2,1)S(1)}, bf16[128,384]{1,0:T(8,128)(2,1)S(1)}) conditional(s32[]{:T(128)} %convert_element_type.82, () %tuple.29, (bf16[2,2,16,768]{3,2,1,0:T(8,128)(2,1)S(1)}, bf16[384,768]{1,0:T(8,128)(2,1)}, s32[]{:T(128)}, ...), branch_computations={%region_0.0_spmd, %region_1.3_spmd} | conditional | flops 606093312 | bytes 29276414 | solution.py:195
  15.7 35.5 %all_gather.18 = bf16[512,768]{1,0:T(8,128)(2,1)S(1)} all-gather(bf16[32,768]{1,0:T(8,128)(2,1)S(1)} %bitcast.127), channel_id=1, replica_groups=mesh['x'=4,'yl'=2,'yh'=2,'z'=16,'c'=2] {'z'}, dimensions={0}, use_global_device_ids=true | all-gather | bytes 835584 | tf_op jit(solution)/shard_map/cond/branch_1_fun/all_gather | solution.py:162
  51.2 9.9 %collective-permute-start = (bf16[512,768]{1,0:T(8,128)(2,1)S(1)}, bf16[512,768]{1,0:T(8,128)(2,1)S(1)}, u32[]{:S(2)}, u32[]{:S(2)}) collective-permute-start(bf16[512,768]{1,0:T(8,128)(2,1)S(1)} %all_gather.18), channel_id=1, source_target_pairs={{0,1},{1,0},{2,3},{3,2},{4,5},{5,4},{6,7},{7,6},{8,9},{9,8},{10,11... | collective-permute-start | bytes 2359304 | tf_op jit(solution)/shard_map/cond/branch_1_fun/ppermute | solution.py:142
  61.2 1.7 convolution_convert_fusion.1
  64.0 1.0 copy.67
  65.0 5.1 %all-to-all-start = ((bf16[8,2,64,384]{3,2,1,0:T(8,128)(2,1)}), bf16[8,2,64,384]{3,2,1,0:T(8,128)(2,1)S(1)}, u32[]{:S(2)}, u32[]{:S(2)}) async-start(bf16[8,2,64,384]{3,2,1,0:T(8,128)(2,1)} %copy.67), calls=%async_computation | async-start | bytes 1572864 | tf_op jit(solution)/shard_map/cond/branch_1_fun/all_to_all | solution.py:148
  70.4 11.6 %all-to-all-done = bf16[8,2,64,384]{3,2,1,0:T(8,128)(2,1)S(1)} async-done(((bf16[8,2,64,384]{3,2,1,0:T(8,128)(2,1)}), bf16[8,2,64,384]{3,2,1,0:T(8,128)(2,1)S(1)}, u32[]{:S(2)}, u32[]{:S(2)}) %all-to-all-start) | async-done | bytes 786464 | tf_op jit(solution)/shard_map/cond/branch_1_fun/all_to_all | solution.py:148
  82.2 14.2 %all_to_all.17 = bf16[8,128,384]{2,1,0:T(8,128)(2,1)S(1)} all-to-all(bf16[8,128,384]{2,1,0:T(8,128)(2,1)S(1)} %broadcast_in_dim.0), channel_id=1, replica_groups=mesh['x'=4,'yl'=2,'yh'=2,'z'=16,'c'=2] {'x','yl'}, dimensions={0} | all-to-all | bytes 1572864 | tf_op jit(solution)/shard_map/cond/branch_1_fun/all_to_all | solution.py:168
  97.2 4.4 %collective-permute-start.3 = (bf16[512,768]{1,0:T(8,128)(2,1)S(1)}, bf16[512,768]{1,0:T(8,128)(2,1)S(1)}, u32[]{:S(2)}, u32[]{:S(2)}) collective-permute-start(bf16[512,768]{1,0:T(8,128)(2,1)S(1)} %convolution_convert_fusion.4), channel_id=1, source_target_pairs={{0,1},{1,0},{2,3},{3,2},{4,5},{5,4},{6,7},{7,6},{8,9},{9,8},{10,11... | collective-permute-start | bytes 2359304 | tf_op jit(solution)/shard_map/ppermute | solution.py:142
  102.6 0.9 collective-permute-done.3
  103.5 0.9 copy-done.4
  104.4 1.8 convert_add_fusion
  106.3 95.8 %conditional.3 = (bf16[512,768]{1,0:T(8,128)(2,1)}, bf16[512,768]{1,0:T(8,128)(2,1)}, bf16[8,2,64,128]{3,2,1,0:T(8,128)(2,1)}, f32[768,384]{1,0:T(8,128)}) conditional(s32[]{:T(128)} %convert_element_type.82, () %tuple.28, (bf16[16,768]{1,0:T(8,128)(2,1)S(1)}, s32[]{:T(128)}, f32[16,2,16,768]{3,2,1,0:T(8,128)S(1)}, ...), branch_computations={%region_3.4_spmd, %region_4.6_spmd} | conditional | flops 806871040 | bytes 21143822 | solution.py:239
  106.3 4.2 %collective-permute-start.1 = (bf16[16,16,768]{2,1,0:T(8,128)(2,1)S(1)}, bf16[16,16,768]{2,1,0:T(8,128)(2,1)}, u32[]{:S(2)}, u32[]{:S(2)}) collective-permute-start(bf16[16,16,768]{2,1,0:T(8,128)(2,1)S(1)} %get-tuple-element.48), channel_id=1, source_target_pairs={{0,32},{32,0},{1,33},{33,1},{2,34},{34,2},{3,35},{35,3},{4,36},{36... | collective-permute-start | bytes 1179656 | tf_op jit(solution)/shard_map/cond/branch_1_fun/ppermute | solution.py:142
  110.5 10.9 %collective-permute-done.1 = bf16[16,16,768]{2,1,0:T(8,128)(2,1)} collective-permute-done((bf16[16,16,768]{2,1,0:T(8,128)(2,1)S(1)}, bf16[16,16,768]{2,1,0:T(8,128)(2,1)}, u32[]{:S(2)}, u32[]{:S(2)}) %collective-permute-start.1) | collective-permute-done | bytes 393248 | tf_op jit(solution)/shard_map/cond/branch_1_fun/ppermute | solution.py:142
  121.4 1.8 fusion.3
  123.3 4.8 %all-to-all-start.2 = ((bf16[16,16,768]{2,1,0:T(8,128)(2,1)}), bf16[16,16,768]{2,1,0:T(8,128)(2,1)S(1)}, u32[]{:S(2)}, u32[]{:S(2)}) async-start(bf16[16,16,768]{2,1,0:T(8,128)(2,1)} %fusion.3), calls=%async_computation.2 | async-start | bytes 786432 | tf_op jit(solution)/shard_map/cond/branch_1_fun/all_to_all | solution.py:213
  128.0 1.5 constant_dynamic-slice_fusion
  130.1 1.6 convolution_add_fusion
  131.8 13.8 %all-to-all-done.2 = bf16[16,16,768]{2,1,0:T(8,128)(2,1)S(1)} async-done(((bf16[16,16,768]{2,1,0:T(8,128)(2,1)}), bf16[16,16,768]{2,1,0:T(8,128)(2,1)S(1)}, u32[]{:S(2)}, u32[]{:S(2)}) %all-to-all-start.2) | async-done | bytes 393248 | tf_op jit(solution)/shard_map/cond/branch_1_fun/all_to_all | solution.py:213
  145.6 5.2 %all-gather = bf16[32,768]{1,0:T(8,128)(2,1)S(1)} all-gather(bf16[16,768]{1,0:T(8,128)(2,1)S(1)} %add_convert_fusion), channel_id=2, replica_groups=mesh['x'=4,'yl'=2,'yh'=2,'z'=16,'c'=2] {'yh'}, dimensions={0}, use_global_device_ids=true | all-gather | bytes 73728 | tf_op jit(solution)/shard_map/cond/branch_1_fun/all_gather | solution.py:222
  150.8 33.4 %all_gather.21 = bf16[512,768]{1,0:T(8,128)(2,1)} all-gather(bf16[32,768]{1,0:T(8,128)(2,1)S(1)} %all-gather), channel_id=1, replica_groups=mesh['x'=4,'yl'=2,'yh'=2,'z'=16,'c'=2] {'z'}, dimensions={0}, use_global_device_ids=true | all-gather | bytes 835584 | tf_op jit(solution)/shard_map/cond/branch_1_fun/all_gather | solution.py:162
  184.2 13.4 %collective-permute-start.2 = (bf16[512,768]{1,0:T(8,128)(2,1)}, bf16[512,768]{1,0:T(8,128)(2,1)}, u32[]{:S(2)}, u32[]{:S(2)}) collective-permute-start(bf16[512,768]{1,0:T(8,128)(2,1)} %all_gather.21), channel_id=1, source_target_pairs={{0,1},{1,0},{2,3},{3,2},{4,5},{5,4},{6,7},{7,6},{8,9},{9,8},{10,11... | collective-permute-start | bytes 2359304 | tf_op jit(solution)/shard_map/cond/branch_1_fun/ppermute | solution.py:142
  197.6 1.5 convolution_convert_fusion.3
  199.9 1.5 convolution_convert_fusion.2
  201.4 0.7 pad_maximum_fusion.1
  202.1 3.4 %all-to-all-start.3 = ((bf16[8,2,64,128]{3,2,1,0:T(8,128)(2,1)}), bf16[8,2,64,128]{3,2,1,0:T(8,128)(2,1)S(1)}, u32[]{:S(2)}, u32[]{:S(2)}) async-start(bf16[8,2,64,128]{3,2,1,0:T(8,128)(2,1)} %get-tuple-element.81), calls=%async_computation.3 | async-start | bytes 524288 | tf_op jit(solution)/shard_map/all_to_all | solution.py:148
  205.5 1.2 copy-done.1
  206.7 4.0 %shard_map.134 = (f32[384,768]{1,0:T(8,128)}, f32[96,768]{1,0:T(8,128)}) custom-call(bf16[8,2,64,512]{3,2,1,0:T(8,128)(2,1)S(1)} %bitcast.101, bf16[512,768]{1,0:T(8,128)(2,1)} %get-tuple-element.83.grad_own_ref, bf16[512,768]{1,0:T(8,128)(2,1)} %get-tuple-element.84.grad_other_ref, bf16[512,768]{1,0:T(8,128)(2,1)} %get-tuple-element.85.gs_own_ref, ...), custom_call_target="tpu_custom_call" | custom-call | flops 805306368 | bytes 4194304 | tf_op jit(solution)/shard_map/pallas_call | solution.py:86
  210.7 1.3 all-to-all-done.3
  (68 shorter events, 6.4 us)
Async XLA Ops:
  7.2 89.4 %copy-start = (bf16[768,384]{1,0:T(8,128)(2,1)S(1)}, bf16[768,384]{1,0:T(8,128)(2,1)}, u32[]{:S(2)}) copy-start(bf16[768,384]{1,0:T(8,128)(2,1)} %param.22) | copy-start | bytes 1769476
  7.2 99.0 %all-gather.7.cloned.1.call-start = ((), (), s32[]{:S(2)}) async-start(), calls=%async_computation.4 | async-start | bytes 1622016 | tf_op jit(solution)/shard_map/all_gather | solution.py:172
  15.6 186.5 %all-gather.9.cloned.1.call-start = ((), (), s32[]{:S(2)}) async-start(), calls=%async_computation.5 | async-start | bytes 1179648 | tf_op jit(solution)/shard_map/all_gather | solution.py:208
  15.7 47.3 %copy-start.11 = (bf16[384,768]{1,0:T(8,128)(2,1)S(1)}, bf16[384,768]{1,0:T(8,128)(2,1)}, u32[]{:S(2)}) copy-start(bf16[384,768]{1,0:T(8,128)(2,1)} %get-tuple-element.93) | copy-start | bytes 1769476 | tf_op jit(solution)/shard_map/cond
  51.2 12.5 %copy-start.3 = (bf16[512,768]{1,0:T(8,128)(2,1)}, bf16[512,768]{1,0:T(8,128)(2,1)S(1)}, u32[]{:S(2)}) copy-start(bf16[512,768]{1,0:T(8,128)(2,1)S(1)} %all_gather.18) | copy-start | bytes 2359300 | tf_op jit(solution)/shard_map/cond
  51.2 11.8 %collective-permute-start = (bf16[512,768]{1,0:T(8,128)(2,1)S(1)}, bf16[512,768]{1,0:T(8,128)(2,1)S(1)}, u32[]{:S(2)}, u32[]{:S(2)}) collective-permute-start(bf16[512,768]{1,0:T(8,128)(2,1)S(1)} %all_gather.18), channel_id=1, source_target_pairs={{0,1},{1,0},{2,3},{3,2},{4,5},{5,4},{6,7},{7,6},{8,9},{9,8},{10,11... | collective-permute-start | bytes 2359304 | tf_op jit(solution)/shard_map/cond/branch_1_fun/ppermute | solution.py:142
  63.0 0.9 copy-start.2
  64.0 6.1 %copy-start.6 = (bf16[128,384]{1,0:T(8,128)(2,1)S(1)}, bf16[128,384]{1,0:T(8,128)(2,1)}, u32[]{:S(2)}) copy-start(bf16[128,384]{1,0:T(8,128)(2,1)} %get-tuple-element.124) | copy-start | bytes 294916 | tf_op jit(solution)/shard_map/cond
  64.0 6.2 %copy-start.9 = (f32[128,12]{0,1:T(8,128)S(1)}, f32[128,12]{0,1:T(8,128)}, u32[]{:S(2)}) copy-start(f32[128,12]{0,1:T(8,128)} %get-tuple-element.95) | copy-start | bytes 18436 | tf_op jit(solution)/shard_map/cond
  65.0 17.0 %all-to-all-start = ((bf16[8,2,64,384]{3,2,1,0:T(8,128)(2,1)}), bf16[8,2,64,384]{3,2,1,0:T(8,128)(2,1)S(1)}, u32[]{:S(2)}, u32[]{:S(2)}) async-start(bf16[8,2,64,384]{3,2,1,0:T(8,128)(2,1)} %copy.67), calls=%async_computation | async-start | bytes 1572864 | tf_op jit(solution)/shard_map/cond/branch_1_fun/all_to_all | solution.py:148
  96.5 5.1 %copy-start.8 = (bf16[128,96]{0,1:T(8,128)(2,1)S(1)}, bf16[128,96]{0,1:T(8,128)(2,1)}, u32[]{:S(2)}) copy-start(bf16[128,96]{0,1:T(8,128)(2,1)} %param.15) | copy-start | bytes 73732
  96.5 5.1 %copy-start.10 = (f32[128,3]{0,1:T(4,128)S(1)}, f32[128,3]{0,1:T(4,128)}, u32[]{:S(2)}) copy-start(f32[128,3]{0,1:T(4,128)} %param.16) | copy-start | bytes 4612
  97.2 6.3 %collective-permute-start.3 = (bf16[512,768]{1,0:T(8,128)(2,1)S(1)}, bf16[512,768]{1,0:T(8,128)(2,1)S(1)}, u32[]{:S(2)}, u32[]{:S(2)}) collective-permute-start(bf16[512,768]{1,0:T(8,128)(2,1)S(1)} %convolution_convert_fusion.4), channel_id=1, source_target_pairs={{0,1},{1,0},{2,3},{3,2},{4,5},{5,4},{6,7},{7,6},{8,9},{9,8},{10,11... | collective-permute-start | bytes 2359304 | tf_op jit(solution)/shard_map/ppermute | solution.py:142
  103.5 0.9 copy-start.4
  104.4 1.9 copy-start.5
  104.4 1.9 copy-start.7
  106.3 15.2 %collective-permute-start.1 = (bf16[16,16,768]{2,1,0:T(8,128)(2,1)S(1)}, bf16[16,16,768]{2,1,0:T(8,128)(2,1)}, u32[]{:S(2)}, u32[]{:S(2)}) collective-permute-start(bf16[16,16,768]{2,1,0:T(8,128)(2,1)S(1)} %get-tuple-element.48), channel_id=1, source_target_pairs={{0,32},{32,0},{1,33},{33,1},{2,34},{34,2},{3,35},{35,3},{4,36},{36... | collective-permute-start | bytes 1179656 | tf_op jit(solution)/shard_map/cond/branch_1_fun/ppermute | solution.py:142
  123.3 22.3 %all-to-all-start.2 = ((bf16[16,16,768]{2,1,0:T(8,128)(2,1)}), bf16[16,16,768]{2,1,0:T(8,128)(2,1)S(1)}, u32[]{:S(2)}, u32[]{:S(2)}) async-start(bf16[16,16,768]{2,1,0:T(8,128)(2,1)} %fusion.3), calls=%async_computation.2 | async-start | bytes 786432 | tf_op jit(solution)/shard_map/cond/branch_1_fun/all_to_all | solution.py:213
  184.2 15.7 %collective-permute-start.2 = (bf16[512,768]{1,0:T(8,128)(2,1)}, bf16[512,768]{1,0:T(8,128)(2,1)}, u32[]{:S(2)}, u32[]{:S(2)}) collective-permute-start(bf16[512,768]{1,0:T(8,128)(2,1)} %all_gather.21), channel_id=1, source_target_pairs={{0,1},{1,0},{2,3},{3,2},{4,5},{5,4},{6,7},{7,6},{8,9},{9,8},{10,11... | collective-permute-start | bytes 2359304 | tf_op jit(solution)/shard_map/cond/branch_1_fun/ppermute | solution.py:142
  202.1 9.9 %all-to-all-start.3 = ((bf16[8,2,64,128]{3,2,1,0:T(8,128)(2,1)}), bf16[8,2,64,128]{3,2,1,0:T(8,128)(2,1)S(1)}, u32[]{:S(2)}, u32[]{:S(2)}) async-start(bf16[8,2,64,128]{3,2,1,0:T(8,128)(2,1)} %get-tuple-element.81), calls=%async_computation.3 | async-start | bytes 524288 | tf_op jit(solution)/shard_map/all_to_all | solution.py:148
  205.5 1.2 copy-start.1
Sparse Core Ops, SparseCore 0:
  15.8 77.4 all-gather.6
  106.4 36.4 all-gather.8

commit v10 on v9

--- a/solution.py
+++ b/solution.py
@@ -206,17 +206,18 @@
     by_core = stream_all.reshape(n_z, 2, 2 * per, features)
     send, saved, by_core = lax.optimization_barrier((send, saved, by_core))
     saved_all = lax.all_gather(saved, ROWS, axis=0)
-    padded_out = jnp.pad(out_weight, ((0, -ctx_width % 128), (0, 0)))
+    padded_width = ctx_width + -ctx_width % 128
 
     def second_half(keep, send, by_core):
         part = (keep + swap(send, "yh").astype(jnp.float32)).astype(jnp.bfloat16)
         came = lax.all_to_all(part, "z", 0, 0, tiled=True)
+        padded_out = jnp.pad(out_weight, ((0, padded_width - ctx_width), (0, 0)))
         stream_own = lax.dynamic_index_in_dim(by_core, core, 1, keepdims=False)
         stream_other = lax.dynamic_index_in_dim(by_core, 1 - core, 1, keepdims=False)
         stream_own = stream_own.reshape(-1, features)
         stream_other = stream_other.reshape(-1, features)
         grad_up = dot_tn(stream_own, pre_own) + dot_tn(stream_other, pre_other)
-        came, grad_up = lax.optimization_barrier((came, grad_up))
+        came, grad_up, padded_out = lax.optimization_barrier((came, grad_up, padded_out))
         summed = jnp.sum(came.astype(jnp.float32), axis=0)
         grad_stream = (grad_out.astype(jnp.float32) + summed).astype(jnp.bfloat16)
         gs_own = gather_z(lax.all_gather(grad_stream, "yh", axis=0))
@@ -232,7 +233,7 @@
         return (
             wide,
             wide,
-            jnp.zeros((n_rows, 2, runs * per, padded_out.shape[0]), jnp.bfloat16),
+            jnp.zeros((n_rows, 2, runs * per, padded_width), jnp.bfloat16),
             jnp.zeros((features, hidden_width), jnp.float32),
         )
 

time: 220 us -> 220 us (level)
  no operation moved by 1% of the time
where the time goes in v10:
time: 220 us
  blocking collectives  94.4 us (43%)
  starting transfers between devices  45.4 us (21%)
  waiting for transfers between devices  39.3 us (18%)
  between operations  14.3 us (6%)
  matrix products  9.82 us (4%)
  local copies, waits for them, and re-layouts  6.97 us (3%)
  Pallas kernels  5.58 us (3%)
  other arithmetic  3.7 us (2%)
    all_gather x2, blocking collectives, gather_z(): return lax.all_gather(pair.reshape(-1, features), 'z', axis=0, tiled=True)  68.9 us
    ppermute x4, starting transfers between devices, swap(): return lax.ppermute(block, axis, SWAP)  32 us
    all_to_all x1, blocking collectives, gather_rows(): every = lax.all_to_all(copies, ROWS, 0, 0, tiled=True)  14.2 us
    all_to_all x1, waiting for transfers between devices, second_half(): came = lax.all_to_all(part, 'z', 0, 0, tiled=True)  13.8 us
    all_to_all x2, waiting for transfers between devices, scatter_rows(): came = lax.all_to_all(sent, ROWS, 0, 0, tiled=True)  12.9 us
    ppermute x4, waiting for transfers between devices, swap(): return lax.ppermute(block, axis, SWAP)  12.7 us
    all_to_all x2, starting transfers between devices, scatter_rows(): came = lax.all_to_all(sent, ROWS, 0, 0, tiled=True)  8.51 us
    dot_general x6, matrix products, dot_nt(): lax.dot_general(left, right, (((1,), (1,)), ((), ())), preferred_element_...  7.59 us
  transfers between devices with their start and end apart: 9, of which 7 were waited for; matrix products, arithmetic and copies ran while one was open for 8% of the time, Pallas kernels for 2%

profile of v10, /device:TPU:1, one launch (start us, length us, event | category | flops | bytes accessed | tf_op | source)
XLA Modules:
  0.0 219.6 jit_solution(1784721189403031370)
XLA Ops:
  7.2 1.6 shard_map.133
  8.8 6.1 %all-gather.1 = bf16[4,16,768]{2,1,0:T(8,128)(2,1)S(1)} all-gather(bf16[2,16,768]{2,1,0:T(8,128)(2,1)} %shard_map.133), channel_id=3, replica_groups=mesh['x'=4,'yl'=2,'yh'=2,'z'=16,'c'=2] {'yh'}, dimensions={0}, use_global_device_ids=true | all-gather | bytes 147456 | tf_op jit(solution)/shard_map/all_gather | solution.py:171
  15.7 80.7 %conditional.2 = (bf16[512,768]{1,0:T(8,128)(2,1)}, bf16[512,768]{1,0:T(8,128)(2,1)}, bf16[8,2,64,384]{3,2,1,0:T(8,128)(2,1)S(1)}, bf16[128,384]{1,0:T(8,128)(2,1)S(1)}) conditional(s32[]{:T(128)} %convert_element_type.82, () %tuple.29, (bf16[2,2,16,768]{3,2,1,0:T(8,128)(2,1)S(1)}, bf16[384,768]{1,0:T(8,128)(2,1)}, s32[]{:T(128)}, ...), branch_computations={%region_0.0_spmd, %region_1.3_spmd} | conditional | flops 606093312 | bytes 29276414 | solution.py:195
  15.7 35.5 %all_gather.18 = bf16[512,768]{1,0:T(8,128)(2,1)S(1)} all-gather(bf16[32,768]{1,0:T(8,128)(2,1)S(1)} %bitcast.129), channel_id=1, replica_groups=mesh['x'=4,'yl'=2,'yh'=2,'z'=16,'c'=2] {'z'}, dimensions={0}, use_global_device_ids=true | all-gather | bytes 835584 | tf_op jit(solution)/shard_map/cond/branch_1_fun/all_gather | solution.py:162
  51.2 9.9 %collective-permute-start = (bf16[512,768]{1,0:T(8,128)(2,1)S(1)}, bf16[512,768]{1,0:T(8,128)(2,1)S(1)}, u32[]{:S(2)}, u32[]{:S(2)}) collective-permute-start(bf16[512,768]{1,0:T(8,128)(2,1)S(1)} %all_gather.18), channel_id=1, source_target_pairs={{0,1},{1,0},{2,3},{3,2},{4,5},{5,4},{6,7},{7,6},{8,9},{9,8},{10,11... | collective-permute-start | bytes 2359304 | tf_op jit(solution)/shard_map/cond/branch_1_fun/ppermute | solution.py:142
  61.2 1.7 convolution_convert_fusion.1
  64.0 1.0 copy.67
  65.0 5.1 %all-to-all-start = ((bf16[8,2,64,384]{3,2,1,0:T(8,128)(2,1)}), bf16[8,2,64,384]{3,2,1,0:T(8,128)(2,1)S(1)}, u32[]{:S(2)}, u32[]{:S(2)}) async-start(bf16[8,2,64,384]{3,2,1,0:T(8,128)(2,1)} %copy.67), calls=%async_computation | async-start | bytes 1572864 | tf_op jit(solution)/shard_map/cond/branch_1_fun/all_to_all | solution.py:148
  70.4 11.6 %all-to-all-done = bf16[8,2,64,384]{3,2,1,0:T(8,128)(2,1)S(1)} async-done(((bf16[8,2,64,384]{3,2,1,0:T(8,128)(2,1)}), bf16[8,2,64,384]{3,2,1,0:T(8,128)(2,1)S(1)}, u32[]{:S(2)}, u32[]{:S(2)}) %all-to-all-start) | async-done | bytes 786464 | tf_op jit(solution)/shard_map/cond/branch_1_fun/all_to_all | solution.py:148
  82.2 14.2 %all_to_all.17 = bf16[8,128,384]{2,1,0:T(8,128)(2,1)S(1)} all-to-all(bf16[8,128,384]{2,1,0:T(8,128)(2,1)S(1)} %broadcast_in_dim.0), channel_id=1, replica_groups=mesh['x'=4,'yl'=2,'yh'=2,'z'=16,'c'=2] {'x','yl'}, dimensions={0} | all-to-all | bytes 1572864 | tf_op jit(solution)/shard_map/cond/branch_1_fun/all_to_all | solution.py:168
  97.2 4.4 %collective-permute-start.3 = (bf16[512,768]{1,0:T(8,128)(2,1)S(1)}, bf16[512,768]{1,0:T(8,128)(2,1)S(1)}, u32[]{:S(2)}, u32[]{:S(2)}) collective-permute-start(bf16[512,768]{1,0:T(8,128)(2,1)S(1)} %convolution_convert_fusion.4), channel_id=1, source_target_pairs={{0,1},{1,0},{2,3},{3,2},{4,5},{5,4},{6,7},{7,6},{8,9},{9,8},{10,11... | collective-permute-start | bytes 2359304 | tf_op jit(solution)/shard_map/ppermute | solution.py:142
  102.6 0.9 collective-permute-done.3
  103.5 0.9 copy-done.4
  104.4 1.8 convert_add_fusion
  106.3 95.8 %conditional.3 = (bf16[512,768]{1,0:T(8,128)(2,1)}, bf16[512,768]{1,0:T(8,128)(2,1)}, bf16[8,2,64,128]{3,2,1,0:T(8,128)(2,1)}, f32[768,384]{1,0:T(8,128)}) conditional(s32[]{:T(128)} %convert_element_type.82, () %tuple.28, (bf16[16,768]{1,0:T(8,128)(2,1)S(1)}, s32[]{:T(128)}, f32[16,2,16,768]{3,2,1,0:T(8,128)S(1)}, ...), branch_computations={%region_3.4_spmd, %region_4.6_spmd} | conditional | flops 806871040 | bytes 21586192 | solution.py:240
  106.3 4.2 %collective-permute-start.1 = (bf16[16,16,768]{2,1,0:T(8,128)(2,1)S(1)}, bf16[16,16,768]{2,1,0:T(8,128)(2,1)}, u32[]{:S(2)}, u32[]{:S(2)}) collective-permute-start(bf16[16,16,768]{2,1,0:T(8,128)(2,1)S(1)} %get-tuple-element.46), channel_id=1, source_target_pairs={{0,32},{32,0},{1,33},{33,1},{2,34},{34,2},{3,35},{35,3},{4,36},{36... | collective-permute-start | bytes 1179656 | tf_op jit(solution)/shard_map/cond/branch_1_fun/ppermute | solution.py:142
  110.5 10.9 %collective-permute-done.1 = bf16[16,16,768]{2,1,0:T(8,128)(2,1)} collective-permute-done((bf16[16,16,768]{2,1,0:T(8,128)(2,1)S(1)}, bf16[16,16,768]{2,1,0:T(8,128)(2,1)}, u32[]{:S(2)}, u32[]{:S(2)}) %collective-permute-start.1) | collective-permute-done | bytes 393248 | tf_op jit(solution)/shard_map/cond/branch_1_fun/ppermute | solution.py:142
  121.4 1.8 fusion.3
  123.3 4.8 %all-to-all-start.2 = ((bf16[16,16,768]{2,1,0:T(8,128)(2,1)}), bf16[16,16,768]{2,1,0:T(8,128)(2,1)S(1)}, u32[]{:S(2)}, u32[]{:S(2)}) async-start(bf16[16,16,768]{2,1,0:T(8,128)(2,1)} %fusion.3), calls=%async_computation.2 | async-start | bytes 786432 | tf_op jit(solution)/shard_map/cond/branch_1_fun/all_to_all | solution.py:213
  128.0 1.5 constant_dynamic-slice_fusion
  130.2 1.6 convolution_add_fusion
  131.8 13.8 %all-to-all-done.2 = bf16[16,16,768]{2,1,0:T(8,128)(2,1)S(1)} async-done(((bf16[16,16,768]{2,1,0:T(8,128)(2,1)}), bf16[16,16,768]{2,1,0:T(8,128)(2,1)S(1)}, u32[]{:S(2)}, u32[]{:S(2)}) %all-to-all-start.2) | async-done | bytes 393248 | tf_op jit(solution)/shard_map/cond/branch_1_fun/all_to_all | solution.py:213
  145.6 5.2 %all-gather = bf16[32,768]{1,0:T(8,128)(2,1)S(1)} all-gather(bf16[16,768]{1,0:T(8,128)(2,1)S(1)} %add_convert_fusion), channel_id=2, replica_groups=mesh['x'=4,'yl'=2,'yh'=2,'z'=16,'c'=2] {'yh'}, dimensions={0}, use_global_device_ids=true | all-gather | bytes 73728 | tf_op jit(solution)/shard_map/cond/branch_1_fun/all_gather | solution.py:223
  150.8 33.4 %all_gather.21 = bf16[512,768]{1,0:T(8,128)(2,1)} all-gather(bf16[32,768]{1,0:T(8,128)(2,1)S(1)} %all-gather), channel_id=1, replica_groups=mesh['x'=4,'yl'=2,'yh'=2,'z'=16,'c'=2] {'z'}, dimensions={0}, use_global_device_ids=true | all-gather | bytes 835584 | tf_op jit(solution)/shard_map/cond/branch_1_fun/all_gather | solution.py:162
  184.2 13.4 %collective-permute-start.2 = (bf16[512,768]{1,0:T(8,128)(2,1)}, bf16[512,768]{1,0:T(8,128)(2,1)}, u32[]{:S(2)}, u32[]{:S(2)}) collective-permute-start(bf16[512,768]{1,0:T(8,128)(2,1)} %all_gather.21), channel_id=1, source_target_pairs={{0,1},{1,0},{2,3},{3,2},{4,5},{5,4},{6,7},{7,6},{8,9},{9,8},{10,11... | collective-permute-start | bytes 2359304 | tf_op jit(solution)/shard_map/cond/branch_1_fun/ppermute | solution.py:142
  197.6 1.5 convolution_convert_fusion.3
  199.9 1.5 convolution_convert_fusion.2
  201.4 0.7 pad_maximum_fusion.1
  202.1 3.4 %all-to-all-start.3 = ((bf16[8,2,64,128]{3,2,1,0:T(8,128)(2,1)}), bf16[8,2,64,128]{3,2,1,0:T(8,128)(2,1)S(1)}, u32[]{:S(2)}, u32[]{:S(2)}) async-start(bf16[8,2,64,128]{3,2,1,0:T(8,128)(2,1)} %get-tuple-element.80), calls=%async_computation.3 | async-start | bytes 524288 | tf_op jit(solution)/shard_map/all_to_all | solution.py:148
  205.5 1.2 copy-done.1
  206.7 4.0 %shard_map.134 = (f32[384,768]{1,0:T(8,128)}, f32[96,768]{1,0:T(8,128)}) custom-call(bf16[8,2,64,512]{3,2,1,0:T(8,128)(2,1)S(1)} %bitcast.103, bf16[512,768]{1,0:T(8,128)(2,1)} %get-tuple-element.82.grad_own_ref, bf16[512,768]{1,0:T(8,128)(2,1)} %get-tuple-element.83.grad_other_ref, bf16[512,768]{1,0:T(8,128)(2,1)} %get-tuple-element.84.gs_own_ref, ...), custom_call_target="tpu_custom_call" | custom-call | flops 805306368 | bytes 4194304 | tf_op jit(solution)/shard_map/pallas_call | solution.py:86
  210.7 1.3 all-to-all-done.3
  (69 shorter events, 6.4 us)
Async XLA Ops:
  7.2 89.4 %copy-start = (bf16[768,384]{1,0:T(8,128)(2,1)S(1)}, bf16[768,384]{1,0:T(8,128)(2,1)}, u32[]{:S(2)}) copy-start(bf16[768,384]{1,0:T(8,128)(2,1)} %param.22) | copy-start | bytes 1769476
  7.2 99.0 %all-gather.7.cloned.1.call-start = ((), (), s32[]{:S(2)}) async-start(), calls=%async_computation.4 | async-start | bytes 1622016 | tf_op jit(solution)/shard_map/all_gather | solution.py:172
  15.6 186.5 %all-gather.9.cloned.1.call-start = ((), (), s32[]{:S(2)}) async-start(), calls=%async_computation.5 | async-start | bytes 1179648 | tf_op jit(solution)/shard_map/all_gather | solution.py:208
  15.7 47.3 %copy-start.11 = (bf16[384,768]{1,0:T(8,128)(2,1)S(1)}, bf16[384,768]{1,0:T(8,128)(2,1)}, u32[]{:S(2)}) copy-start(bf16[384,768]{1,0:T(8,128)(2,1)} %get-tuple-element.92) | copy-start | bytes 1769476 | tf_op jit(solution)/shard_map/cond
  51.2 12.5 %copy-start.3 = (bf16[512,768]{1,0:T(8,128)(2,1)}, bf16[512,768]{1,0:T(8,128)(2,1)S(1)}, u32[]{:S(2)}) copy-start(bf16[512,768]{1,0:T(8,128)(2,1)S(1)} %all_gather.18) | copy-start | bytes 2359300 | tf_op jit(solution)/shard_map/cond
  51.2 11.8 %collective-permute-start = (bf16[512,768]{1,0:T(8,128)(2,1)S(1)}, bf16[512,768]{1,0:T(8,128)(2,1)S(1)}, u32[]{:S(2)}, u32[]{:S(2)}) collective-permute-start(bf16[512,768]{1,0:T(8,128)(2,1)S(1)} %all_gather.18), channel_id=1, source_target_pairs={{0,1},{1,0},{2,3},{3,2},{4,5},{5,4},{6,7},{7,6},{8,9},{9,8},{10,11... | collective-permute-start | bytes 2359304 | tf_op jit(solution)/shard_map/cond/branch_1_fun/ppermute | solution.py:142
  63.0 0.9 copy-start.2
  64.0 6.1 %copy-start.6 = (bf16[128,384]{1,0:T(8,128)(2,1)S(1)}, bf16[128,384]{1,0:T(8,128)(2,1)}, u32[]{:S(2)}) copy-start(bf16[128,384]{1,0:T(8,128)(2,1)} %get-tuple-element.123) | copy-start | bytes 294916 | tf_op jit(solution)/shard_map/cond
  64.0 6.2 %copy-start.9 = (f32[128,12]{0,1:T(8,128)S(1)}, f32[128,12]{0,1:T(8,128)}, u32[]{:S(2)}) copy-start(f32[128,12]{0,1:T(8,128)} %get-tuple-element.94) | copy-start | bytes 18436 | tf_op jit(solution)/shard_map/cond
  65.0 17.0 %all-to-all-start = ((bf16[8,2,64,384]{3,2,1,0:T(8,128)(2,1)}), bf16[8,2,64,384]{3,2,1,0:T(8,128)(2,1)S(1)}, u32[]{:S(2)}, u32[]{:S(2)}) async-start(bf16[8,2,64,384]{3,2,1,0:T(8,128)(2,1)} %copy.67), calls=%async_computation | async-start | bytes 1572864 | tf_op jit(solution)/shard_map/cond/branch_1_fun/all_to_all | solution.py:148
  96.5 5.1 %copy-start.8 = (bf16[128,96]{0,1:T(8,128)(2,1)S(1)}, bf16[128,96]{0,1:T(8,128)(2,1)}, u32[]{:S(2)}) copy-start(bf16[128,96]{0,1:T(8,128)(2,1)} %param.15) | copy-start | bytes 73732
  96.5 5.1 %copy-start.10 = (f32[128,3]{0,1:T(4,128)S(1)}, f32[128,3]{0,1:T(4,128)}, u32[]{:S(2)}) copy-start(f32[128,3]{0,1:T(4,128)} %param.16) | copy-start | bytes 4612
  97.2 6.3 %collective-permute-start.3 = (bf16[512,768]{1,0:T(8,128)(2,1)S(1)}, bf16[512,768]{1,0:T(8,128)(2,1)S(1)}, u32[]{:S(2)}, u32[]{:S(2)}) collective-permute-start(bf16[512,768]{1,0:T(8,128)(2,1)S(1)} %convolution_convert_fusion.4), channel_id=1, source_target_pairs={{0,1},{1,0},{2,3},{3,2},{4,5},{5,4},{6,7},{7,6},{8,9},{9,8},{10,11... | collective-permute-start | bytes 2359304 | tf_op jit(solution)/shard_map/ppermute | solution.py:142
  103.5 0.9 copy-start.4
  104.4 1.9 copy-start.5
  104.4 1.9 copy-start.7
  106.3 15.2 %collective-permute-start.1 = (bf16[16,16,768]{2,1,0:T(8,128)(2,1)S(1)}, bf16[16,16,768]{2,1,0:T(8,128)(2,1)}, u32[]{:S(2)}, u32[]{:S(2)}) collective-permute-start(bf16[16,16,768]{2,1,0:T(8,128)(2,1)S(1)} %get-tuple-element.46), channel_id=1, source_target_pairs={{0,32},{32,0},{1,33},{33,1},{2,34},{34,2},{3,35},{35,3},{4,36},{36... | collective-permute-start | bytes 1179656 | tf_op jit(solution)/shard_map/cond/branch_1_fun/ppermute | solution.py:142
  123.3 22.3 %all-to-all-start.2 = ((bf16[16,16,768]{2,1,0:T(8,128)(2,1)}), bf16[16,16,768]{2,1,0:T(8,128)(2,1)S(1)}, u32[]{:S(2)}, u32[]{:S(2)}) async-start(bf16[16,16,768]{2,1,0:T(8,128)(2,1)} %fusion.3), calls=%async_computation.2 | async-start | bytes 786432 | tf_op jit(solution)/shard_map/cond/branch_1_fun/all_to_all | solution.py:213
  184.2 15.7 %collective-permute-start.2 = (bf16[512,768]{1,0:T(8,128)(2,1)}, bf16[512,768]{1,0:T(8,128)(2,1)}, u32[]{:S(2)}, u32[]{:S(2)}) collective-permute-start(bf16[512,768]{1,0:T(8,128)(2,1)} %all_gather.21), channel_id=1, source_target_pairs={{0,1},{1,0},{2,3},{3,2},{4,5},{5,4},{6,7},{7,6},{8,9},{9,8},{10,11... | collective-permute-start | bytes 2359304 | tf_op jit(solution)/shard_map/cond/branch_1_fun/ppermute | solution.py:142
  202.1 9.9 %all-to-all-start.3 = ((bf16[8,2,64,128]{3,2,1,0:T(8,128)(2,1)}), bf16[8,2,64,128]{3,2,1,0:T(8,128)(2,1)S(1)}, u32[]{:S(2)}, u32[]{:S(2)}) async-start(bf16[8,2,64,128]{3,2,1,0:T(8,128)(2,1)} %get-tuple-element.80), calls=%async_computation.3 | async-start | bytes 524288 | tf_op jit(solution)/shard_map/all_to_all | solution.py:148
  205.5 1.2 copy-start.1
Sparse Core Ops, SparseCore 0:
  15.8 77.4 all-gather.6
  106.4 36.4 all-gather.8
